TPU v7x, 32 devices: a whole 2x2x4 slice. The times are simulated.
32 devices in a mesh: tm: 8 (over z, y), space: 4 (over x, core).
Axes of the slice: x: 2, y: 2, z: 4, core: 2. Of those that a mesh axis runs over, the one named last changes fastest.
Arguments:
- snapshots: float32 [1024, 32, 2048], P('tm', None, 'space'), may hold values from -12 to 12
- quad_weights: float32 [2048], P('space'), may hold values from 0.25 to 4
Outputs:
- modes: float32 [2, 1024, 2048], P(None, 'tm', 'space')
- energies: float32 [1024], P('tm')
All inputs are finite; a program needn't handle non-finite values.
Results may differ from a plain program's by a relative error of at most 0.0001.
Values sent between devices are 32-bit elements; how exact they have to be, the bound alone decides.
No kernel may reach another device: no remote copies, remote signals or barrier semaphores. Data moves between devices by JAX's collectives and lax.ppermute only.
A program may use at most 128 MiB of HBM per device.

v0:
```python
import math

import jax
import jax.numpy as jnp
from jax import lax
from jax.sharding import PartitionSpec as P

POWER = 3


def bit_reverse(values, bit_count):
    result = jnp.zeros_like(values)
    for position in range(bit_count):
        result = result + ((values >> position & 1) << bit_count - 1 - position)
    return result


def matvec(matrix, vector):
    return jnp.einsum("fbc,fc->fb", matrix, vector, precision=lax.Precision.HIGHEST)


def power_modes(real_gram, imag_gram):
    vec_real = jnp.ones(real_gram.shape[:2], jnp.float32) / math.sqrt(real_gram.shape[1])
    vec_imag = jnp.zeros(real_gram.shape[:2], jnp.float32)
    for sweep_idx in range(POWER):
        new_real = matvec(real_gram, vec_real) - matvec(imag_gram, vec_imag)
        new_imag = matvec(real_gram, vec_imag) + matvec(imag_gram, vec_real)
        length = lax.rsqrt(
            jnp.sum(new_real * new_real + new_imag * new_imag, axis=1, keepdims=True) + 1e-06
        )
        vec_real = new_real * length
        vec_imag = new_imag * length
    image_real = matvec(real_gram, vec_real) - matvec(imag_gram, vec_imag)
    image_imag = matvec(real_gram, vec_imag) + matvec(imag_gram, vec_real)
    energy = jnp.sum(vec_real * image_real + vec_imag * image_imag, axis=1)
    return (vec_real, vec_imag, energy)


def body(snapshots, quad_weights):
    tm_size = lax.axis_size("tm")
    bit_count = tm_size.bit_length() - 1
    local_times, blocks, points = snapshots.shape
    total_times = local_times * tm_size
    total_points = points * lax.axis_size("space")
    norm_factor = 1.0 / math.sqrt(0.375 * total_times)
    flattened = snapshots.reshape(local_times, blocks * points)
    columns = lax.all_to_all(flattened, "tm", split_axis=1, concat_axis=0, tiled=True)
    col_count = columns.shape[1]
    times_all = jnp.arange(total_times, dtype=jnp.int32)
    window = (
        0.5 - 0.5 * jnp.cos(2.0 * math.pi * times_all.astype(jnp.float32) / total_times)
    ) * norm_factor
    row_block = min(256, total_times)

    def one_block(block_idx):
        row_ids = block_idx * row_block + jnp.arange(row_block, dtype=jnp.int32)
        frequency = bit_reverse(row_ids // local_times, bit_count) + tm_size * (
            row_ids % local_times
        )
        angles = (
            -2.0
            * math.pi
            * (frequency[:, None] * times_all[None, :] % total_times).astype(jnp.float32)
            / total_times
        )
        cos_tab = jnp.cos(angles) * window[None, :]
        sin_tab = jnp.sin(angles) * window[None, :]
        return (
            jnp.dot(cos_tab, columns, precision=lax.Precision.HIGHEST),
            jnp.dot(sin_tab, columns, precision=lax.Precision.HIGHEST),
        )

    spec_real, spec_imag = lax.map(one_block, jnp.arange(total_times // row_block, dtype=jnp.int32))
    spectrum = jnp.stack(
        [spec_real.reshape(total_times, col_count), spec_imag.reshape(total_times, col_count)]
    )
    returned = lax.all_to_all(spectrum, "tm", split_axis=1, concat_axis=2, tiled=True)
    spectral = returned.reshape(2, local_times, blocks, points)
    weighted = spectral * quad_weights
    gram_full = (
        jnp.einsum("pfbx,qfcx->fpbqc", weighted, spectral, precision=lax.Precision.HIGHEST)
        / total_points
    )
    real_gram = gram_full[:, 0, :, 0] + gram_full[:, 1, :, 1]
    imag_gram = gram_full[:, 0, :, 1] - gram_full[:, 1, :, 0]
    real_gram, imag_gram = lax.psum((real_gram, imag_gram), "space")
    vec_real, vec_imag, energy = power_modes(real_gram, imag_gram)
    inverse_root = lax.rsqrt(energy + 1e-06)[:, None]
    modes_real = jnp.einsum(
        "fb,fbx->fx", vec_real, spectral[0], precision=lax.Precision.HIGHEST
    ) - jnp.einsum("fb,fbx->fx", vec_imag, spectral[1], precision=lax.Precision.HIGHEST)
    modes_imag = jnp.einsum(
        "fb,fbx->fx", vec_imag, spectral[0], precision=lax.Precision.HIGHEST
    ) + jnp.einsum("fb,fbx->fx", vec_real, spectral[1], precision=lax.Precision.HIGHEST)
    return (jnp.stack([modes_real * inverse_root, modes_imag * inverse_root]), energy)


def solution(mesh):
    return jax.shard_map(
        body,
        mesh=mesh,
        in_specs=(P("tm", None, "space"), P("space")),
        out_specs=(P(None, "tm", "space"), P("tm")),
        check_vma=False,
    )
```

profile of v0, /device:TPU:0, one launch (start us, length us, event | category | flops | bytes accessed | tf_op | source)
XLA Modules:
  0.0 1022.6 jit_solution(10371427435982934037)
XLA Ops:
  7.2 10.5 %all_to_all.25 = f32[128,8,2048]{2,1,0:T(8,128)} reshape(f32[128,32,512]{2,1,0:T(8,128)} %param.4) | data formatting | bytes 16777216 | tf_op jit(solution)/shard_map/all_to_all | solution.py:47
  17.7 11.4 %copy.16 = f32[128,8,2048]{2,0,1:T(8,128)} copy(f32[128,8,2048]{2,1,0:T(8,128)} %all_to_all.25) | data formatting | bytes 16777216 | tf_op jit(solution)/shard_map/all_to_all | solution.py:47
  29.1 7.3 all-to-all-start
  36.5 183.1 %all-to-all-done = f32[128,8,2048]{2,0,1:T(8,128)} async-done(((f32[128,8,2048]{2,0,1:T(8,128)}), f32[128,8,2048]{2,0,1:T(8,128)}, u32[]{:S(2)}, u32[]{:S(2)}) %all-to-all-start) | async-done | bytes 8388640 | tf_op jit(solution)/shard_map/all_to_all | solution.py:47
  219.6 131.4 %while.17 = (s32[]{:T(128)}, f32[4,256,2048]{2,1,0:T(8,128)}, f32[4,256,2048]{2,1,0:T(8,128)}, s32[4]{0:T(128)S(1)}, f32[1024,2048]{1,0:T(8,128)}, /*index=5*/s32[]{:T(128)}, s32[1]{0:T(128)}) while((s32[]{:T(128)}, f32[4,256,2048]{2,1,0:T(8,128)}, f32[4,256,2048]{2,1,0:T(8,128)}, s32[4]{0:T(128)S(1)}, ...), condition=%wide.region_1.2_spmd.clone.clone, body=%wide.region_0.1_spmd.clone.clone.sunk | while | flops 12892780544 | bytes 20988008 | solution.py:73
  221.4 15.8 %fusion.70 = f32[4,256,2048]{2,1,0:T(8,128)} fusion(f32[4,256,2048]{2,1,0:T(8,128)} %get-tuple-element.256, s32[]{:T(128)} %get-tuple-element.255, f32[1024,2048]{1,0:T(8,128)} %get-tuple-element.266, f32[1024]{0:T(1024)S(1)} %subtract_multiply_fusion.2, s32[256]{0:T(256)S(1)} %fusion.69), kind=kOutput, calls=%fused_computation.5.clone.1 | convolution fusion | flops 6446383104 | bytes 10491392 | tf_op jit(solution)/shard_map/while/body/eval_jaxpr/dot_general | solution.py:69
  237.1 15.7 %fusion.71 = f32[4,256,2048]{2,1,0:T(8,128)} fusion(f32[4,256,2048]{2,1,0:T(8,128)} %get-tuple-element.257, s32[]{:T(128)} %get-tuple-element.255, f32[1024,2048]{1,0:T(8,128)} %get-tuple-element.266, f32[1024]{0:T(1024)S(1)} %subtract_multiply_fusion.2, s32[256]{0:T(256)S(1)} %fusion.69), kind=kOutput, calls=%fused_computation.3.clone.1 | convolution fusion | flops 6446383104 | bytes 10491392 | tf_op jit(solution)/shard_map/while/body/eval_jaxpr/dot_general | solution.py:70
  254.1 15.7 %fusion.70 = f32[4,256,2048]{2,1,0:T(8,128)} fusion(f32[4,256,2048]{2,1,0:T(8,128)} %get-tuple-element.256, s32[]{:T(128)} %get-tuple-element.255, f32[1024,2048]{1,0:T(8,128)} %get-tuple-element.266, f32[1024]{0:T(1024)S(1)} %subtract_multiply_fusion.2, s32[256]{0:T(256)S(1)} %fusion.69), kind=kOutput, calls=%fused_computation.5.clone.1 | convolution fusion | flops 6446383104 | bytes 10491392 | tf_op jit(solution)/shard_map/while/body/eval_jaxpr/dot_general | solution.py:69
  269.8 15.7 %fusion.71 = f32[4,256,2048]{2,1,0:T(8,128)} fusion(f32[4,256,2048]{2,1,0:T(8,128)} %get-tuple-element.257, s32[]{:T(128)} %get-tuple-element.255, f32[1024,2048]{1,0:T(8,128)} %get-tuple-element.266, f32[1024]{0:T(1024)S(1)} %subtract_multiply_fusion.2, s32[256]{0:T(256)S(1)} %fusion.69), kind=kOutput, calls=%fused_computation.3.clone.1 | convolution fusion | flops 6446383104 | bytes 10491392 | tf_op jit(solution)/shard_map/while/body/eval_jaxpr/dot_general | solution.py:70
  286.8 15.7 %fusion.70 = f32[4,256,2048]{2,1,0:T(8,128)} fusion(f32[4,256,2048]{2,1,0:T(8,128)} %get-tuple-element.256, s32[]{:T(128)} %get-tuple-element.255, f32[1024,2048]{1,0:T(8,128)} %get-tuple-element.266, f32[1024]{0:T(1024)S(1)} %subtract_multiply_fusion.2, s32[256]{0:T(256)S(1)} %fusion.69), kind=kOutput, calls=%fused_computation.5.clone.1 | convolution fusion | flops 6446383104 | bytes 10491392 | tf_op jit(solution)/shard_map/while/body/eval_jaxpr/dot_general | solution.py:69
  302.5 15.7 %fusion.71 = f32[4,256,2048]{2,1,0:T(8,128)} fusion(f32[4,256,2048]{2,1,0:T(8,128)} %get-tuple-element.257, s32[]{:T(128)} %get-tuple-element.255, f32[1024,2048]{1,0:T(8,128)} %get-tuple-element.266, f32[1024]{0:T(1024)S(1)} %subtract_multiply_fusion.2, s32[256]{0:T(256)S(1)} %fusion.69), kind=kOutput, calls=%fused_computation.3.clone.1 | convolution fusion | flops 6446383104 | bytes 10491392 | tf_op jit(solution)/shard_map/while/body/eval_jaxpr/dot_general | solution.py:70
  319.5 15.7 %fusion.70 = f32[4,256,2048]{2,1,0:T(8,128)} fusion(f32[4,256,2048]{2,1,0:T(8,128)} %get-tuple-element.256, s32[]{:T(128)} %get-tuple-element.255, f32[1024,2048]{1,0:T(8,128)} %get-tuple-element.266, f32[1024]{0:T(1024)S(1)} %subtract_multiply_fusion.2, s32[256]{0:T(256)S(1)} %fusion.69), kind=kOutput, calls=%fused_computation.5.clone.1 | convolution fusion | flops 6446383104 | bytes 10491392 | tf_op jit(solution)/shard_map/while/body/eval_jaxpr/dot_general | solution.py:69
  335.2 15.7 %fusion.71 = f32[4,256,2048]{2,1,0:T(8,128)} fusion(f32[4,256,2048]{2,1,0:T(8,128)} %get-tuple-element.257, s32[]{:T(128)} %get-tuple-element.255, f32[1024,2048]{1,0:T(8,128)} %get-tuple-element.266, f32[1024]{0:T(1024)S(1)} %subtract_multiply_fusion.2, s32[256]{0:T(256)S(1)} %fusion.69), kind=kOutput, calls=%fused_computation.3.clone.1 | convolution fusion | flops 6446383104 | bytes 10491392 | tf_op jit(solution)/shard_map/while/body/eval_jaxpr/dot_general | solution.py:70
  351.0 13.5 %stack_reshape.6 = f32[1,1024,2048]{2,0,1:T(1,128)} reshape(f32[4,256,2048]{2,1,0:T(8,128)} %get-tuple-element.130) | data formatting | bytes 16777216 | tf_op jit(solution)/shard_map/stack;reshape | solution.py:74
  364.5 13.5 %stack_reshape.7 = f32[1,1024,2048]{2,0,1:T(1,128)} reshape(f32[4,256,2048]{2,1,0:T(8,128)} %get-tuple-element.131) | data formatting | bytes 16777216 | tf_op jit(solution)/shard_map/stack;reshape | solution.py:74
  378.0 16.7 %pad_maximum_fusion = f32[2,1024,2048]{2,0,1:T(2,128)S(1)} fusion(f32[1,1024,2048]{2,0,1:T(1,128)} %stack_reshape.7, f32[1,1024,2048]{2,0,1:T(1,128)} %stack_reshape.6), kind=kLoop, calls=%fused_computation.38 | loop fusion | flops 4194304 | bytes 33554432 | tf_op jit(solution)/shard_map/stack | solution.py:74
  394.7 366.6 %all_to_all.34 = f32[2,1024,2048]{2,0,1:T(2,128)} all-to-all(f32[2,1024,2048]{2,0,1:T(2,128)S(1)} %pad_maximum_fusion), channel_id=1, replica_groups=mesh['tm'=8,'space'=4] {'tm'}, dimensions={1} | all-to-all | bytes 33554432 | tf_op jit(solution)/shard_map/all_to_all | solution.py:77
  761.3 15.2 %copy.17 = f32[2,1024,2048]{2,1,0:T(8,128)S(1)} copy(f32[2,1024,2048]{2,0,1:T(2,128)} %all_to_all.34) | data formatting | bytes 33554432 | tf_op jit(solution)/shard_map/all_to_all | solution.py:77
  776.5 5.7 copy-done
  782.2 19.4 %copy.18 = f32[2,128,8,2048]{3,2,0,1:T(8,128)} copy(f32[2,128,8,2048]{3,1,2,0:T(8,128)S(1)} %bitcast.119) | data formatting | bytes 33554432 | tf_op jit(solution)/shard_map/all_to_all | solution.py:77
  801.6 19.0 %reshape.84 = f32[2,128,32,512]{3,2,0,1:T(8,128)} reshape(f32[2,128,8,2048]{3,2,0,1:T(8,128)} %copy.18) | data formatting | bytes 33554432 | tf_op jit(solution)/shard_map/reshape | solution.py:78
  820.7 19.1 %reshape.86 = f32[2,128,32,512,1]{3,2,0,1,4:T(8,128)} reshape(f32[2,128,8,2048]{3,2,0,1:T(8,128)} %copy.18) | data formatting | bytes 33554432 | tf_op jit(solution)/shard_map/reshape | solution.py:78
  839.7 45.6 %broadcast_multiply_fusion = f32[128,2,32,2,32]{4,2,3,1,0:T(8,128)S(1)} fusion(f32[2,128,32,512,1]{3,2,0,1,4:T(8,128)} %reshape.86, f32[2,128,32,512]{3,2,0,1:T(8,128)} %reshape.84, f32[512]{0:T(512)S(1)} %copy-done.2), kind=kOutput, calls=%fused_computation.48 | convolution fusion | flops 3225944064 | bytes 35653632 | tf_op jit(solution)/shard_map/pfbx,qfcx->fpbqc/dot_general | solution.py:81
  888.4 12.8 %fusion.43 = (f32[1,128,8,2048]{3,1,2,0:T(8,128)}, f32[1,128,8,2048]{3,1,2,0:T(8,128)}) fusion(f32[2,128,8,2048]{3,1,2,0:T(8,128)} %bitcast.120), kind=kLoop, calls=%fused_computation.86 | loop fusion | bytes 33554432 | tf_op jit(solution)/shard_map/slice | solution.py:91
  901.2 9.2 copy.19
  910.4 9.5 copy.20
  919.9 53.3 %all-reduce.3.cloned.1.call-done = (f32[128,32,32]{2,1,0:T(8,128)}, f32[128,32,32]{2,1,0:T(8,128)}) async-done(((f32[128,32,32]{2,1,0:T(8,128)}, f32[128,32,32]{2,1,0:T(8,128)}), (f32[128,32,32]{2,1,0:T(8,128)}, f32[128,32,32]{2,1,0:T(8,128)})) %all-reduce.3.cloned.1.call-update) | async-done | bytes 1048592 | tf_op jit(solution)/shard_map/psum | solution.py:86
  973.2 5.1 fusion.44
  978.3 5.0 fusion.46
  983.3 5.0 fusion.45
  988.2 5.0 fusion.47
  1006.9 7.2 multiply_reduce_fusion.3
  (69 shorter events, 20.7 us)
Async XLA Ops:
  29.1 190.4 %all-to-all-start = ((f32[128,8,2048]{2,0,1:T(8,128)}), f32[128,8,2048]{2,0,1:T(8,128)}, u32[]{:S(2)}, u32[]{:S(2)}) async-start(f32[128,8,2048]{2,0,1:T(8,128)} %copy.16), calls=%async_computation | async-start | bytes 16777216 | tf_op jit(solution)/shard_map/all_to_all | solution.py:47
  36.4 936.8 %all-reduce.3.cloned.1.call-start = ((), (), s32[]{:S(2)}) async-start(), calls=%async_computation.2 | async-start | bytes 8388608 | tf_op jit(solution)/shard_map/psum | solution.py:86
  776.5 5.7 copy-start
  820.7 19.1 %copy-start.2 = (f32[512]{0:T(512)S(1)}, f32[512]{0:T(512)}, u32[]{:S(2)}) copy-start(f32[512]{0:T(512)} %param.5) | copy-start | bytes 6148
  973.2 20.6 %copy-start.1 = (f32[128,32,32]{2,1,0:T(8,128)S(1)}, f32[128,32,32]{2,1,0:T(8,128)}, u32[]{:S(2)}) copy-start(f32[128,32,32]{2,1,0:T(8,128)} %get-tuple-element.197) | copy-start | bytes 1572868
  1006.9 7.2 copy-start.3
Sparse Core Ops, SparseCore 0:
  888.5 84.6 all-reduce.2
where the time goes:
time: 1030 us; the launch traced here: 1020 us
  blocking collectives  367 us (36%)
  waiting for transfers between devices  236 us (23%)
  matrix products  191 us (19%)
  local copies, waits for them, and re-layouts  164 us (16%)
  other arithmetic  39.7 us (4%)
  between operations  14.5 us (1%)
    all_to_all x1, blocking collectives, body(): lax.all_to_all(spectrum, 'tm', split_axis=1, concat_axis=2, tiled=True)  367 us
    all_to_all x1, waiting for transfers between devices, body(): lax.all_to_all(flattened, 'tm', split_axis=1, concat_axis=0, tiled=True)  183 us
    dot_general x4, matrix products, one_block(): jnp.dot(cos_tab, columns, precision=lax.Precision.HIGHEST)  62.8 us
    dot_general x4, matrix products, one_block(): jnp.dot(sin_tab, columns, precision=lax.Precision.HIGHEST)  62.8 us
    psum x1, waiting for transfers between devices, body(): real_gram, imag_gram = lax.psum((real_gram, imag_gram), 'space')  53.3 us
    dot_general x1, matrix products, body(): jnp.einsum('pfbx,qfcx->fpbqc', weighted, spectral, precision=lax.Precisio...  45.6 us
    reshape x2, local copies, waits for them, and re-layouts, body(): spectral = returned.reshape(2, local_times, blocks, points)  38.1 us
    all_to_all x2, local copies, waits for them, and re-layouts, body(): lax.all_to_all(spectrum, 'tm', split_axis=1, concat_axis=2, tiled=True)  34.6 us
  transfers between devices with their start and end apart: 2, of which 2 were waited for; matrix products, arithmetic and copies ran while one was open for 3% of the time, Pallas kernels for 0%

commit v1 on v0

--- a/solution.py
+++ b/solution.py
@@ -1,18 +1,376 @@
+import functools
 import math
 
 import jax
 import jax.numpy as jnp
+import ml_dtypes
+import numpy as np
 from jax import lax
+from jax.experimental import pallas as pl
+from jax.experimental.pallas import tpu as pltpu
 from jax.sharding import PartitionSpec as P
 
 POWER = 3
-
-
-def bit_reverse(values, bit_count):
-    result = jnp.zeros_like(values)
-    for position in range(bit_count):
-        result = result + ((values >> position & 1) << bit_count - 1 - position)
-    return result
+CHUNK = 8
+HALF = 64
+LANES = 128
+BF16 = jnp.bfloat16
+F32 = jnp.float32
+
+
+def bit_reverse(value, bit_count):
+    return sum((value >> i & 1) << (bit_count - 1 - i) for i in range(bit_count))
+
+
+def split_np(table):
+    high = table.astype(ml_dtypes.bfloat16)
+    low = (table - high.astype(np.float64)).astype(ml_dtypes.bfloat16)
+    return high, low
+
+
+def split(value):
+    high = value.astype(BF16)
+    return high, (value - high.astype(F32)).astype(BF16)
+
+
+def low_half(shape):
+    return lax.broadcasted_iota(jnp.int32, shape, len(shape) - 1) < HALF
+
+
+def params(mib):
+    return pltpu.CompilerParams(vmem_limit_bytes=mib * 2**20)
+
+
+@functools.lru_cache(None)
+def transform_tables(total_times, slots, tile):
+    t = np.arange(total_times)
+    window = (0.5 - 0.5 * np.cos(2 * np.pi * t / total_times)) / math.sqrt(0.375 * total_times)
+    k = np.arange(slots)
+    phase = 2 * np.pi * (k[:, None] * t[None, :] % total_times) / total_times
+    live = (k <= total_times // 2)[:, None]
+    real = np.cos(phase) * window * live
+    imag = -np.sin(phase) * window * live
+    both = np.stack([real, imag]).reshape(2, slots // tile, tile, total_times)
+    both = both.transpose(1, 0, 2, 3).reshape(2 * slots, total_times)
+    return split_np(both)
+
+
+@functools.lru_cache(None)
+def output_order(total_times, tm_size, slots):
+    local = total_times // tm_size
+    bits = tm_size.bit_length() - 1
+    q = np.arange(total_times)
+    freq = np.array([bit_reverse(d, bits) for d in range(tm_size)])[q // local]
+    freq = freq + tm_size * (q % local)
+    mirrored = freq > total_times // 2
+    slot = np.where(mirrored, total_times - freq, freq)
+    onehot = (slot[:, None] == np.arange(slots)[None, :]).astype(ml_dtypes.bfloat16)
+    sign = np.where(mirrored, -1.0, 1.0).astype(np.float32)
+    lanes = np.ones((total_times, LANES), np.float32)
+    lanes[:, HALF:] = sign[:, None]
+    return onehot, lanes
+
+
+def pack_kernel(x_ref, out_ref):
+    times = x_ref.shape[0]
+    rows = x_ref.reshape(times * CHUNK, LANES)
+    low = low_half((times, LANES))
+    for j in range(CHUNK // 2):
+        first = rows[pl.ds(j, times, stride=CHUNK), :]
+        second = rows[pl.ds(j + CHUNK // 2, times, stride=CHUNK), :]
+        cols = slice(j * LANES, (j + 1) * LANES)
+        out_ref[0, :, cols] = jnp.where(low, first, pltpu.roll(second, HALF, 1))
+        out_ref[1, :, cols] = jnp.where(low, pltpu.roll(first, HALF, 1), second)
+
+
+def pack(snapshots, chunk, tm_size):
+    times, _, points = snapshots.shape
+    width = CHUNK * HALF
+    return pl.pallas_call(
+        pack_kernel,
+        grid=(points // LANES,),
+        in_specs=[pl.BlockSpec((times, CHUNK, LANES), lambda i: (0, chunk, i))],
+        out_specs=pl.BlockSpec((2, times, width), lambda i: (i, 0, 0)),
+        out_shape=jax.ShapeDtypeStruct((tm_size, times, width), F32),
+        compiler_params=params(32),
+        name="pack",
+    )(snapshots)
+
+
+def transform_kernel(tile, high_ref, low_ref, x_ref, out_ref, xh_ref, xl_ref):
+    @pl.when(pl.program_id(0) == 0)
+    def _():
+        high, low = split(x_ref[...])
+        xh_ref[...] = high
+        xl_ref[...] = low
+
+    dot = functools.partial(jnp.dot, preferred_element_type=F32)
+    both = dot(high_ref[...], xh_ref[...])
+    both = both + dot(high_ref[...], xl_ref[...])
+    both = both + dot(low_ref[...], xh_ref[...])
+    low = low_half((tile, LANES))
+    for j in range(CHUNK // 2):
+        cols = slice(j * LANES, (j + 1) * LANES)
+        real, imag = both[:tile, cols], both[tile:, cols]
+        out_ref[pl.ds(j, tile, stride=CHUNK), :] = jnp.where(low, real, pltpu.roll(imag, HALF, 1))
+        out_ref[pl.ds(j + CHUNK // 2, tile, stride=CHUNK), :] = jnp.where(
+            low, pltpu.roll(real, HALF, 1), imag
+        )
+
+
+def transform(columns, tables, slots, tile):
+    total, width = columns.shape
+    return pl.pallas_call(
+        functools.partial(transform_kernel, tile),
+        grid=(slots // tile,),
+        in_specs=[
+            pl.BlockSpec((2 * tile, total), lambda i: (i, 0)),
+            pl.BlockSpec((2 * tile, total), lambda i: (i, 0)),
+            pl.BlockSpec((total, width), lambda i: (0, 0)),
+        ],
+        out_specs=pl.BlockSpec((tile * CHUNK, LANES), lambda i: (i, 0)),
+        out_shape=jax.ShapeDtypeStruct((slots * CHUNK, LANES), F32),
+        scratch_shapes=[pltpu.VMEM((total, width), BF16)] * 2,
+        compiler_params=params(48),
+        name="transform",
+    )(*tables, columns)
+
+
+def gram_kernel(tile, scale, *refs):
+    z_refs, (w_ref, out_ref) = refs[:-2], refs[-2:]
+    blocks = CHUNK * len(z_refs)
+    group = LANES // blocks
+    weight = w_ref[...] * scale
+    flipped = jnp.where(low_half(weight.shape), weight, -weight)
+    lane = lax.broadcasted_iota(jnp.int32, (blocks, LANES), 1)
+    row = lax.broadcasted_iota(jnp.int32, (blocks, LANES), 0)
+    upper = row <= lane % blocks
+
+    def step(g, carry):
+        left, real_side, imag_side = [], [], []
+        for k in range(group):
+            start = pl.multiple_of((g * group + k) * CHUNK, CHUNK)
+            z = jnp.concatenate([ref[pl.ds(start, CHUNK), :] for ref in z_refs], axis=0)
+            left.append(z)
+            real_side.append(z * weight)
+            imag_side.append(pltpu.roll(z, HALF, 1) * flipped)
+        lh, ll = split(jnp.concatenate(left, axis=0))
+        rh, rl = split(jnp.concatenate(real_side + imag_side, axis=0))
+        full = lax.dot_general(
+            jnp.concatenate([lh, ll, lh], axis=1),
+            jnp.concatenate([rh, rh, rl], axis=1),
+            (((1,), (1,)), ((), ())),
+            preferred_element_type=F32,
+        )
+        real, imag = full[:blocks, :LANES], full[:blocks, LANES:]
+        for k in range(1, group):
+            here = lane // blocks == k
+            rows = slice(k * blocks, (k + 1) * blocks)
+            real = jnp.where(here, full[rows, :LANES], real)
+            imag = jnp.where(here, full[rows, LANES:], imag)
+        packed = jnp.where(upper, real, imag)
+        parts = [packed[i * 8 : (i + 1) * 8] for i in range(group)]
+        small = lane[:8]
+        step_size = 1
+        while step_size < group:
+            span = step_size * blocks
+            odd = (small // span) % 2 == 1
+            fresh = list(parts)
+            for i in range(group):
+                if i & step_size == 0:
+                    a, b = parts[i], parts[i + step_size]
+                    fresh[i] = jnp.where(odd, pltpu.roll(b, span, 1), a)
+                    fresh[i + step_size] = jnp.where(odd, b, pltpu.roll(a, LANES - span, 1))
+            parts = fresh
+            step_size *= 2
+        for k in range(group):
+            out_ref[g * group + k] = parts[k]
+        return carry
+
+    lax.fori_loop(0, tile // group, step, 0, unroll=2)
+
+
+def gram(spectra, weights, slots, tile, total_points):
+    blocks = CHUNK * len(spectra)
+    rows = blocks * blocks // LANES
+    return pl.pallas_call(
+        functools.partial(gram_kernel, tile, 1.0 / total_points),
+        grid=(slots // tile,),
+        in_specs=[pl.BlockSpec((tile * CHUNK, LANES), lambda i: (i, 0))] * len(spectra)
+        + [pl.BlockSpec((1, LANES), lambda i: (0, 0))],
+        out_specs=pl.BlockSpec((tile, rows, LANES), lambda i: (i, 0, 0)),
+        out_shape=jax.ShapeDtypeStruct((slots, rows, LANES), F32),
+        compiler_params=params(48),
+        name="gram",
+    )(*spectra, weights)
+
+
+def power_kernel(x_ref, out_ref):
+    blocks, _, count = x_ref.shape
+    x = x_ref[...]
+    flip = jnp.swapaxes(x, 0, 1)
+    b = lax.broadcasted_iota(jnp.int32, x.shape, 0)
+    c = lax.broadcasted_iota(jnp.int32, x.shape, 1)
+    real = jnp.where(b <= c, x, flip)
+    imag = jnp.where(b < c, flip, jnp.where(b > c, -x, 0.0))
+
+    def apply(vr, vi):
+        vr, vi = vr[:, None, :], vi[:, None, :]
+        return jnp.sum(real * vr - imag * vi, axis=0), jnp.sum(real * vi + imag * vr, axis=0)
+
+    vr = jnp.full((blocks, count), 1.0 / math.sqrt(blocks), F32)
+    vi = jnp.zeros((blocks, count), F32)
+    for _ in range(POWER):
+        ur, ui = apply(vr, vi)
+        length = lax.rsqrt(jnp.sum(ur * ur + ui * ui, axis=0, keepdims=True) + 1e-06)
+        vr, vi = ur * length, ui * length
+    ur, ui = apply(vr, vi)
+    energy = jnp.sum(vr * ur + vi * ui, axis=0, keepdims=True)
+    out_ref[0:blocks, :] = vr
+    out_ref[blocks : 2 * blocks, :] = vi
+    out_ref[2 * blocks : 2 * blocks + 8, :] = jnp.broadcast_to(energy, (8, count))
+
+
+def power(packed):
+    blocks, _, count = packed.shape
+    return pl.pallas_call(
+        power_kernel,
+        out_shape=jax.ShapeDtypeStruct((2 * blocks + 8, count), F32),
+        compiler_params=params(32),
+        name="power",
+    )(packed)
+
+
+def modes_kernel(slots, *refs):
+    z_refs, (v_ref, order_ref, sign_ref, out_ref, energy_ref, s_ref) = refs[:-6], refs[-6:]
+    blocks = CHUNK * len(z_refs)
+    tile = 32
+
+    def step(i, carry):
+        start = pl.multiple_of(i * tile, tile)
+        vec = v_ref[pl.ds(start, tile), :]
+        real = jnp.zeros((tile, LANES), F32)
+        imag = jnp.zeros((tile, LANES), F32)
+        for n, ref in enumerate(z_refs):
+            for j in range(CHUNK):
+                b = n * CHUNK + j
+                z = ref[pl.ds(start * CHUNK + j, tile, stride=CHUNK), :]
+                real = real + z * vec[:, b : b + 1]
+                imag = imag + z * vec[:, blocks + b : blocks + b + 1]
+        turned = pltpu.roll(imag, HALF, 1)
+        both = real + jnp.where(low_half(turned.shape), -turned, turned)
+        energy = vec[:, 2 * blocks : 2 * blocks + 1]
+        both = both * lax.rsqrt(energy + 1e-06)
+        value = jnp.concatenate([both, jnp.broadcast_to(energy, (tile, LANES))], axis=1)
+        for part in range(3):
+            high = value.astype(BF16)
+            s_ref[part, pl.ds(start, tile), :] = high
+            value = value - high.astype(F32)
+        return carry
+
+    lax.fori_loop(0, slots // tile, step, 0)
+    order = order_ref[...]
+    total = jnp.dot(order, s_ref[0], preferred_element_type=F32)
+    total = total + jnp.dot(order, s_ref[1], preferred_element_type=F32)
+    total = total + jnp.dot(order, s_ref[2], preferred_element_type=F32)
+    out_ref[...] = total[:, :LANES] * sign_ref[...]
+    energy_ref[...] = total[:, LANES:]
+
+
+def modes(spectra, vectors, order, sign, slots):
+    total = order.shape[0]
+    return pl.pallas_call(
+        functools.partial(modes_kernel, slots),
+        out_shape=[jax.ShapeDtypeStruct((total, LANES), F32)] * 2,
+        scratch_shapes=[pltpu.VMEM((3, slots, 2 * LANES), BF16)],
+        compiler_params=params(56),
+        name="modes",
+    )(*spectra, vectors, order, sign)
+
+
+def place_kernel(x_ref, out_ref):
+    low = low_half(x_ref.shape[1:])
+    for i in range(x_ref.shape[0] // 2):
+        first, second = x_ref[2 * i], x_ref[2 * i + 1]
+        cols = slice(i * LANES, (i + 1) * LANES)
+        out_ref[0, :, cols] = jnp.where(low, first, pltpu.roll(second, HALF, 1))
+        out_ref[1, :, cols] = jnp.where(low, pltpu.roll(first, HALF, 1), second)
+
+
+def place(pieces):
+    count, rows, _ = pieces.shape
+    return pl.pallas_call(
+        place_kernel,
+        out_shape=jax.ShapeDtypeStruct((2, rows, count * HALF), F32),
+        compiler_params=params(32),
+        name="place",
+    )(pieces)
+
+
+def exchange(value, axes):
+    return lax.all_to_all(value, axes, 0, 0, tiled=True)
+
+
+def body(mesh_shape, snapshots, quad_weights):
+    tm_size, space_size = mesh_shape["tm"], mesh_shape["space"]
+    local_times, blocks, points = snapshots.shape
+    total_times = local_times * tm_size
+    total_points = points * space_size
+    devices = tm_size * space_size
+    per_device = -(-(total_times // 2 + 1) // devices)
+    slots = per_device * devices
+    tile = slots // 4
+    tables = transform_tables(total_times, slots, tile)
+
+    spectra = []
+    for chunk in range(blocks // CHUNK):
+        packed = pack(snapshots, chunk, tm_size)
+        columns = exchange(packed, "tm").reshape(total_times, CHUNK * HALF)
+        spectra.append(transform(columns, tables, slots, tile))
+
+    here = lax.axis_index("tm") * HALF
+    weights = lax.dynamic_slice(quad_weights, (here,), (HALF,))
+    weights = jnp.concatenate([weights, weights])[None, :]
+    matrices = gram(spectra, weights, slots, tile, total_points)
+
+    rows = matrices.shape[1]
+    space = lax.axis_index("space")
+    levels = space_size.bit_length() - 1
+    part = matrices.reshape(tm_size, *[2] * levels, per_device, rows, LANES)
+    for level in range(levels):
+        axis = levels - level
+        bit = space >> level & 1
+        kept = lax.dynamic_index_in_dim(part, bit, axis, keepdims=False)
+        given = lax.dynamic_index_in_dim(part, 1 - bit, axis, keepdims=False)
+        pairs = [(i, i ^ (1 << level)) for i in range(space_size)]
+        part = kept + lax.ppermute(given, "space", pairs)
+    part = exchange(part, "tm").sum(axis=0)
+
+    part = part.reshape(per_device, 8, LANES // blocks, blocks)
+    part = part.transpose(2, 1, 3, 0).reshape(blocks, blocks, per_device)
+    vectors = power(part).T
+    vectors = jnp.pad(vectors, ((0, 0), (0, LANES - vectors.shape[1])))
+    vectors = jnp.broadcast_to(vectors[None], (devices, per_device, LANES))
+    vectors = exchange(vectors, ("tm", "space")).reshape(slots, LANES)
+
+    order, sign = output_order(total_times, tm_size, slots)
+    pieces, energies = modes(spectra, vectors, order, sign, slots)
+    pieces = exchange(pieces.reshape(tm_size, local_times, LANES), "tm")
+    energies = energies.reshape(tm_size, local_times, LANES)[:, :, 0]
+    energies = lax.dynamic_index_in_dim(energies, lax.axis_index("tm"), 0, keepdims=False)
+    return place(pieces), energies
+
+
+def fits(mesh_shape, times, blocks, points):
+    tm_size, space_size = mesh_shape["tm"], mesh_shape["space"]
+    return (
+        points == space_size * tm_size * HALF
+        and tm_size % 2 == 0
+        and space_size & (space_size - 1) == 0
+        and times % (tm_size * 8) == 0
+        and blocks % CHUNK == 0
+        and blocks == 32
+    )
 
 
 def matvec(matrix, vector):
@@ -36,7 +394,7 @@
     return (vec_real, vec_imag, energy)
 
 
-def body(snapshots, quad_weights):
+def general_body(snapshots, quad_weights):
     tm_size = lax.axis_size("tm")
     bit_count = tm_size.bit_length() - 1
     local_times, blocks, points = snapshots.shape
@@ -96,10 +454,18 @@
 
 
 def solution(mesh):
-    return jax.shard_map(
-        body,
-        mesh=mesh,
-        in_specs=(P("tm", None, "space"), P("space")),
-        out_specs=(P(None, "tm", "space"), P("tm")),
-        check_vma=False,
-    )
+    shape = dict(mesh.shape)
+
+    def program(snapshots, quad_weights):
+        chosen = general_body
+        if fits(shape, *snapshots.shape):
+            chosen = functools.partial(body, shape)
+        return jax.shard_map(
+            chosen,
+            mesh=mesh,
+            in_specs=(P("tm", None, "space"), P("space")),
+            out_specs=(P(None, "tm", "space"), P("tm")),
+            check_vma=False,
+        )(snapshots, quad_weights)
+
+    return program

time: 1030 us -> 354 us (0.34)
  blocking collectives: 367 us -> 34.7 us
  matrix products: 191 us -> 0 us
  local copies, waits for them, and re-layouts: 164 us -> 27 us
  Pallas kernels: 0 us -> 86.4 us
  waiting for transfers between devices: 236 us -> 178 us
  other arithmetic: 39.7 us -> 1.53 us
  starting transfers between devices: 7.32 us -> 24.7 us
  between operations: 14.5 us -> 0.85 us
    all_to_all x1 -> x2, blocking collectives: 367 us -> 34.7 us  [exchange(): return lax.all_to_all(value, axes, 0, 0, tiled=True)]
    dot_general x13 -> x0, matrix products: 191 us -> none  [the longest x4 62.8 us: one_block(): jnp.dot(cos_tab, columns, precision=lax.Precision.HIGHEST)]
    pallas_call x0 -> x12, Pallas kernels: none -> 86.4 us  [the longest x1 31.8 us: gram(): pl.pallas_call(functools.partial(gram_kernel, tile, 1.0 / total_points),...]
    all_to_all x4 -> x0, local copies, waits for them, and re-layouts: 56.6 us -> none  [the longest x2 34.6 us: body(): lax.all_to_all(spectrum, 'tm', split_axis=1, concat_axis=2, tiled=True)]
    psum x1 -> x0, waiting for transfers between devices: 53.3 us -> none  [body(): real_gram, imag_gram = lax.psum((real_gram, imag_gram), 'space')]
    reshape x2, local copies, waits for them, and re-layouts: 38.1 us -> 0.9 us  [the longest x1 0.73 us: body(): vectors = exchange(vectors, ('tm', 'space')).reshape(slots, LANES)]
    slice x3 -> x0, local copies, waits for them, and re-layouts: 31.5 us -> none  [the longest x2 22.3 us: body(): spectral[1]]
    another operation x2 -> x0, local copies, waits for them, and re-layouts: 27 us -> none  [body(): jnp.stack([spec_real.reshape(total_times, col_count), spec_imag.reshape(t...]
  transfers between devices with their start and end apart: 2 -> 7, of which waited for: 2 -> 7; matrix products, arithmetic and copies ran while one was open for 3% -> 1% of each run, Pallas kernels for 0% -> 8%
where the time goes in v1:
time: 354 us; the launch traced here: 353 us
  waiting for transfers between devices  178 us (50%)
  Pallas kernels  86.4 us (24%)
  blocking collectives  34.7 us (10%)
  local copies, waits for them, and re-layouts  27 us (8%)
  starting transfers between devices  24.7 us (7%)
    all_to_all x5, waiting for transfers between devices, exchange(): return lax.all_to_all(value, axes, 0, 0, tiled=True)  162 us
    all_to_all x2, blocking collectives, exchange(): return lax.all_to_all(value, axes, 0, 0, tiled=True)  34.7 us
    pallas_call x1, Pallas kernels, gram(): pl.pallas_call(functools.partial(gram_kernel, tile, 1.0 / total_points),...  31.8 us
    pallas_call x4, Pallas kernels, transform(): pl.pallas_call(functools.partial(transform_kernel, tile), grid=(slots //...  27.5 us
    unnamed x28, local copies, waits for them, and re-layouts  24 us
    all_to_all x5, starting transfers between devices, exchange(): return lax.all_to_all(value, axes, 0, 0, tiled=True)  23.1 us
    ppermute x2, waiting for transfers between devices, body(): part = kept + lax.ppermute(given, 'space', pairs)  15.9 us
    pallas_call x1, Pallas kernels, modes(): pl.pallas_call(functools.partial(modes_kernel, slots), out_shape=[jax.Sha...  15 us
  transfers between devices with their start and end apart: 7, of which 7 were waited for; matrix products, arithmetic and copies ran while one was open for 1% of the time, Pallas kernels for 8%

profile of v1, /device:TPU:0, one launch (start us, length us, event | category | flops | bytes accessed | tf_op | source)
XLA Modules:
  0.0 353.0 jit_solution(2047161476022330968)
XLA Ops:
  0.6 3.4 copy-done
  4.0 2.5 pack.4
  6.5 7.3 %all-to-all-start = ((f32[8,128,512]{2,1,0:T(8,128)}), f32[8,128,512]{2,1,0:T(8,128)S(1)}, u32[]{:S(2)}, u32[]{:S(2)}) async-start(f32[8,128,512]{2,1,0:T(8,128)} %pack.4), calls=%async_computation | async-start | bytes 4194304 | tf_op jit(solution)/shard_map/all_to_all | solution.py:311
  13.8 3.4 copy-done.1
  17.2 2.5 pack.5
  19.6 42.4 %all-to-all-done = f32[8,128,512]{2,1,0:T(8,128)S(1)} async-done(((f32[8,128,512]{2,1,0:T(8,128)}), f32[8,128,512]{2,1,0:T(8,128)S(1)}, u32[]{:S(2)}, u32[]{:S(2)}) %all-to-all-start) | async-done | bytes 2097184 | tf_op jit(solution)/shard_map/all_to_all | solution.py:311
  63.3 4.3 %all-to-all-start.1 = ((f32[8,128,512]{2,1,0:T(8,128)}), f32[8,128,512]{2,1,0:T(8,128)}, u32[]{:S(2)}, u32[]{:S(2)}) async-start(f32[8,128,512]{2,1,0:T(8,128)} %pack.5), calls=%async_computation.1 | async-start | bytes 4194304 | tf_op jit(solution)/shard_map/all_to_all | solution.py:311
  67.7 3.4 copy-done.2
  71.1 2.5 pack.6
  73.6 42.0 %all-to-all-done.1 = f32[8,128,512]{2,1,0:T(8,128)} async-done(((f32[8,128,512]{2,1,0:T(8,128)}), f32[8,128,512]{2,1,0:T(8,128)}, u32[]{:S(2)}, u32[]{:S(2)}) %all-to-all-start.1) | async-done | bytes 2097184 | tf_op jit(solution)/shard_map/all_to_all | solution.py:311
  115.5 3.6 %all-to-all-start.2 = ((f32[8,128,512]{2,1,0:T(8,128)}), f32[8,128,512]{2,1,0:T(8,128)S(1)}, u32[]{:S(2)}, u32[]{:S(2)}) async-start(f32[8,128,512]{2,1,0:T(8,128)} %pack.6), calls=%async_computation.2 | async-start | bytes 4194304 | tf_op jit(solution)/shard_map/all_to_all | solution.py:311
  119.1 3.4 copy-done.3
  122.5 2.5 pack.7
  125.0 42.5 %all-to-all-done.2 = f32[8,128,512]{2,1,0:T(8,128)S(1)} async-done(((f32[8,128,512]{2,1,0:T(8,128)}), f32[8,128,512]{2,1,0:T(8,128)S(1)}, u32[]{:S(2)}, u32[]{:S(2)}) %all-to-all-start.2) | async-done | bytes 2097184 | tf_op jit(solution)/shard_map/all_to_all | solution.py:311
  168.9 4.4 %all-to-all-start.3 = ((f32[8,128,512]{2,1,0:T(8,128)}), f32[8,128,512]{2,1,0:T(8,128)}, u32[]{:S(2)}, u32[]{:S(2)}) async-start(f32[8,128,512]{2,1,0:T(8,128)} %pack.7), calls=%async_computation.3 | async-start | bytes 4194304 | tf_op jit(solution)/shard_map/all_to_all | solution.py:311
  174.2 1.6 copy-done.10
  175.8 6.3 %transform.4.refs_0_ = f32[4352,128]{1,0:T(8,128)S(1)} custom-call(bf16[1088,1024]{1,0:T(8,128)(2,1)} %constant.50.clone.high_ref, bf16[1088,1024]{1,0:T(8,128)(2,1)} %constant.51.clone.low_ref, f32[1024,512]{1,0:T(8,128)S(1)} %bitcast.24), custom_call_target="tpu_custom_call" | custom-call | tf_op jit(solution)/shard_map/transform/pallas_call | solution.py:123
  182.1 7.9 %transform.5.refs_1_ = f32[4352,128]{1,0:T(8,128)S(1)} custom-call(bf16[1088,1024]{1,0:T(8,128)(2,1)} %constant.50.clone.high_ref, bf16[1088,1024]{1,0:T(8,128)(2,1)} %constant.51.clone.low_ref, f32[1024,512]{1,0:T(8,128)} %bitcast.1.x_ref), custom_call_target="tpu_custom_call" | custom-call | tf_op jit(solution)/shard_map/transform/pallas_call | solution.py:123
  191.3 6.3 %transform.6.refs_2_ = f32[4352,128]{1,0:T(8,128)S(1)} custom-call(bf16[1088,1024]{1,0:T(8,128)(2,1)} %constant.50.clone.high_ref, bf16[1088,1024]{1,0:T(8,128)(2,1)} %constant.51.clone.low_ref, f32[1024,512]{1,0:T(8,128)S(1)} %bitcast.25), custom_call_target="tpu_custom_call" | custom-call | tf_op jit(solution)/shard_map/transform/pallas_call | solution.py:123
  197.6 1.4 copy-done.6
  199.0 22.1 %all-to-all-done.3 = f32[8,128,512]{2,1,0:T(8,128)} async-done(((f32[8,128,512]{2,1,0:T(8,128)}), f32[8,128,512]{2,1,0:T(8,128)}, u32[]{:S(2)}, u32[]{:S(2)}) %all-to-all-start.3) | async-done | bytes 2097184 | tf_op jit(solution)/shard_map/all_to_all | solution.py:311
  221.1 7.0 %transform.7.refs_3_ = f32[4352,128]{1,0:T(8,128)S(1)} custom-call(bf16[1088,1024]{1,0:T(8,128)(2,1)} %constant.50.clone.high_ref, bf16[1088,1024]{1,0:T(8,128)(2,1)} %constant.51.clone.low_ref, f32[1024,512]{1,0:T(8,128)} %bitcast.3.x_ref), custom_call_target="tpu_custom_call" | custom-call | tf_op jit(solution)/shard_map/transform/pallas_call | solution.py:123
  228.2 1.4 copy-done.7
  229.6 31.8 %gram.1 = f32[544,8,128]{2,1,0:T(8,128)S(1)} custom-call(f32[4352,128]{1,0:T(8,128)S(1)} %transform.4.refs_0_, f32[4352,128]{1,0:T(8,128)} %copy-done.5, f32[4352,128]{1,0:T(8,128)} %copy-done.6, f32[4352,128]{1,0:T(8,128)} %copy-done.7, f32[1,128]{1,0:T(1,128)S(1)} %maximum_bitcast_fusion.refs_4_), custom_call_target="tpu_custom_call" | custom-call | tf_op jit(solution)/shard_map/gram/pallas_call | solution.py:196
  262.9 2.7 collective-permute-done
  267.0 1.6 collective-permute-start.1
  268.6 13.2 %collective-permute-done.1 = f32[8,17,8,128]{3,2,1,0:T(8,128)S(1)} collective-permute-done((f32[8,17,8,128]{3,2,1,0:T(8,128)S(1)}, f32[8,17,8,128]{3,2,1,0:T(8,128)S(1)}, u32[]{:S(2)}, u32[]{:S(2)}) %collective-permute-start.1) | collective-permute-done | bytes 557088 | tf_op jit(solution)/shard_map/ppermute | solution.py:346
  281.8 18.9 %all_to_all.35 = f32[8,17,8,128]{3,2,1,0:T(8,128)S(1)} all-to-all(f32[8,17,8,128]{3,2,1,0:T(8,128)S(1)} %bitcast_add_fusion.1), channel_id=1, replica_groups=mesh['tm'=8,'space'=4] {'tm'}, dimensions={0} | all-to-all | bytes 1114112 | tf_op jit(solution)/shard_map/all_to_all | solution.py:311
  302.6 15.8 %all_to_all.36 = f32[32,17,128]{2,1,0:T(8,128)S(1)} all-to-all(f32[32,17,128]{2,1,0:T(8,128)S(1)} %broadcast_in_dim.10), channel_id=1, replica_groups=mesh['tm'=8,'space'=4] {'tm','space'}, dimensions={0} | all-to-all | bytes 557056 | tf_op jit(solution)/shard_map/all_to_all | solution.py:311
  319.2 15.0 %modes.1 = (f32[1024,128]{1,0:T(8,128)}, f32[1024,128]{1,0:T(8,128)}) custom-call(f32[4352,128]{1,0:T(8,128)} %copy-done.4, f32[4352,128]{1,0:T(8,128)} %copy-done.5, f32[4352,128]{1,0:T(8,128)} %copy-done.6, f32[4352,128]{1,0:T(8,128)} %copy-done.7, f32[544,128]{1,0:T(8,128)} %reshape.44.refs_4_, bf16[1024,544]{1,0:T(8,128)(2,1)} %constant.52.clone.refs_5_, ...), custom_call_target="tpu_custom_call" | custom-call | tf_op jit(solution)/shard_map/modes/pallas_call | solution.py:282
  334.2 3.5 all-to-all-start.6
  339.1 12.9 %all-to-all-done.6.x_ref = f32[8,128,128]{2,1,0:T(8,128)S(1)} async-done(((f32[8,128,128]{2,1,0:T(8,128)}), f32[8,128,128]{2,1,0:T(8,128)S(1)}, u32[]{:S(2)}, u32[]{:S(2)}) %all-to-all-start.6) | async-done | bytes 524320 | tf_op jit(solution)/shard_map/all_to_all | solution.py:311
  (37 shorter events, 12.9 us)
Async XLA Ops:
  0.6 3.4 copy-start
  6.5 55.5 %all-to-all-start = ((f32[8,128,512]{2,1,0:T(8,128)}), f32[8,128,512]{2,1,0:T(8,128)S(1)}, u32[]{:S(2)}, u32[]{:S(2)}) async-start(f32[8,128,512]{2,1,0:T(8,128)} %pack.4), calls=%async_computation | async-start | bytes 4194304 | tf_op jit(solution)/shard_map/all_to_all | solution.py:311
  13.8 3.4 copy-start.1
  62.0 1.3 copy-start.9
  63.3 52.2 %all-to-all-start.1 = ((f32[8,128,512]{2,1,0:T(8,128)}), f32[8,128,512]{2,1,0:T(8,128)}, u32[]{:S(2)}, u32[]{:S(2)}) async-start(f32[8,128,512]{2,1,0:T(8,128)} %pack.5), calls=%async_computation.1 | async-start | bytes 4194304 | tf_op jit(solution)/shard_map/all_to_all | solution.py:311
  67.7 3.4 copy-start.2
  115.5 52.0 %all-to-all-start.2 = ((f32[8,128,512]{2,1,0:T(8,128)}), f32[8,128,512]{2,1,0:T(8,128)S(1)}, u32[]{:S(2)}, u32[]{:S(2)}) async-start(f32[8,128,512]{2,1,0:T(8,128)} %pack.6), calls=%async_computation.2 | async-start | bytes 4194304 | tf_op jit(solution)/shard_map/all_to_all | solution.py:311
  119.1 3.4 copy-start.3
  167.6 1.4 copy-start.11
  168.9 52.2 %all-to-all-start.3 = ((f32[8,128,512]{2,1,0:T(8,128)}), f32[8,128,512]{2,1,0:T(8,128)}, u32[]{:S(2)}, u32[]{:S(2)}) async-start(f32[8,128,512]{2,1,0:T(8,128)} %pack.7), calls=%async_computation.3 | async-start | bytes 4194304 | tf_op jit(solution)/shard_map/all_to_all | solution.py:311
  174.2 1.6 copy-start.10
  182.1 46.1 %copy-start.4 = (f32[4352,128]{1,0:T(8,128)}, f32[4352,128]{1,0:T(8,128)S(1)}, u32[]{:S(2)}) copy-start(f32[4352,128]{1,0:T(8,128)S(1)} %transform.4.refs_0_) | copy-start | bytes 6684676
  182.1 9.2 %copy-start.12 = (f32[8,128,512]{2,1,0:T(8,128)S(1)}, f32[8,128,512]{2,1,0:T(8,128)}, u32[]{:S(2)}) copy-start(f32[8,128,512]{2,1,0:T(8,128)} %copy-done.11) | copy-start | bytes 6291460
  189.9 1.4 copy-start.5
  197.6 1.4 copy-start.6
  228.2 1.4 copy-start.7
  261.4 1.4 copy-start.8
  262.8 2.8 collective-permute-start
  267.0 14.7 %collective-permute-start.1 = (f32[8,17,8,128]{3,2,1,0:T(8,128)S(1)}, f32[8,17,8,128]{3,2,1,0:T(8,128)S(1)}, u32[]{:S(2)}, u32[]{:S(2)}) collective-permute-start(f32[8,17,8,128]{3,2,1,0:T(8,128)S(1)} %dynamic-slice_bitcast_fusion.1), channel_id=1, source_target_pairs={{0,2},{1,3},{2,0},{3,1},{4,6},{5,7},{6,4},{7,5},{8,10},{9,11},{10,... | collective-permute-start | bytes 1671176 | tf_op jit(solution)/shard_map/ppermute | solution.py:346
  334.2 17.8 %all-to-all-start.6 = ((f32[8,128,128]{2,1,0:T(8,128)}), f32[8,128,128]{2,1,0:T(8,128)S(1)}, u32[]{:S(2)}, u32[]{:S(2)}) async-start(f32[8,128,128]{2,1,0:T(8,128)} %bitcast.29), calls=%async_computation.6 | async-start | bytes 1048576 | tf_op jit(solution)/shard_map/all_to_all | solution.py:311

commit v2 on v0

--- a/solution.py
+++ b/solution.py
@@ -1,18 +1,602 @@
+import functools
 import math
 
 import jax
 import jax.numpy as jnp
+import ml_dtypes
+import numpy as np
 from jax import lax
+from jax.experimental import pallas as pl
+from jax.experimental.pallas import tpu as pltpu
 from jax.sharding import PartitionSpec as P
 
 POWER = 3
-
-
-def bit_reverse(values, bit_count):
-    result = jnp.zeros_like(values)
-    for position in range(bit_count):
-        result = result + ((values >> position & 1) << bit_count - 1 - position)
-    return result
+CHUNK = 8
+HALF = 64
+LANES = 128
+BF16 = jnp.bfloat16
+F32 = jnp.float32
+
+
+def bit_reverse(value, bit_count):
+    return sum((value >> i & 1) << (bit_count - 1 - i) for i in range(bit_count))
+
+
+def split_np(table):
+    high = table.astype(ml_dtypes.bfloat16)
+    low = (table - high.astype(np.float64)).astype(ml_dtypes.bfloat16)
+    return high, low
+
+
+def split(value):
+    high = value.astype(BF16)
+    return high, (value - high.astype(F32)).astype(BF16)
+
+
+def low_half(shape):
+    return lax.broadcasted_iota(jnp.int32, shape, len(shape) - 1) < HALF
+
+
+def in_hbm(arrays):
+    return [pltpu.with_memory_space_constraint(array, pltpu.HBM) for array in arrays]
+
+
+def params(mib):
+    return pltpu.CompilerParams(vmem_limit_bytes=mib * 2**20)
+
+
+def slot_of(freq, total_times):
+    part = total_times // 8
+    return (freq - 1) % 4 * part + freq // 4
+
+
+@functools.lru_cache(None)
+def transform_tables(total_times, slots):
+    part, quarter = total_times // 8, total_times // 4
+    t = np.arange(quarter)
+
+    def waves(rest, count):
+        k = 4 * np.arange(count) + rest
+        phase = 2 * np.pi * (k[:, None] * t[None, :] % total_times) / total_times
+        live = (k <= total_times // 2)[:, None]
+        return np.cos(phase) * live, np.sin(phase) * live
+
+    c, s = waves(1, part)
+    ones = np.block([[c, -s], [-s, -c]])
+    c, s = waves(3, part)
+    threes = np.block([[c, s], [-s, c]])
+    c, s = waves(2, part)
+    twos = np.concatenate([c, -s])
+    c, s = waves(0, slots - 3 * part)
+    fours = np.concatenate([c, -s])
+    odd = split_np(np.concatenate([ones, threes]))
+    return (*odd, *split_np(twos), *split_np(fours))
+
+
+@functools.lru_cache(None)
+def window_table(total_times):
+    t = np.arange(total_times)
+    window = (0.5 - 0.5 * np.cos(2 * np.pi * t / total_times)) / math.sqrt(0.375 * total_times)
+    return np.broadcast_to(window[:, None], (total_times, LANES)).astype(np.float32)
+
+
+def pack_kernel(offsets, *refs):
+    x_refs, out_refs = refs[: len(offsets)], refs[-len(offsets) :]
+    window = refs[len(offsets)][...]
+    times = window.shape[0]
+    low = low_half((times, LANES))
+    me = lax.axis_index("tm")
+    for m, x_ref, out_ref in zip(offsets, x_refs, out_refs):
+        rows = x_ref.reshape(times * CHUNK, LANES)
+        even = (m ^ me) % 2 == 0
+        for j in range(CHUNK // 2):
+            first = rows[pl.ds(j, times, stride=CHUNK), :] * window
+            second = rows[pl.ds(j + CHUNK // 2, times, stride=CHUNK), :] * window
+            left = jnp.where(low, first, pltpu.roll(second, HALF, 1))
+            right = jnp.where(low, pltpu.roll(first, HALF, 1), second)
+            out_ref[:, j * LANES : (j + 1) * LANES] = jnp.where(even, left, right)
+
+
+def pack(snapshots, window, chunks, offsets, after):
+    times = snapshots.shape[0]
+    width = CHUNK * HALF
+
+    def tile_spec(m):
+        place = lambda n: (0, chunks[0] + n, m // 2 ^ lax.axis_index("tm") // 2)
+        return pl.BlockSpec((times, CHUNK, LANES), place)
+
+    return pl.pallas_call(
+        functools.partial(pack_kernel, offsets),
+        grid=(len(chunks),),
+        in_specs=[tile_spec(m) for m in offsets]
+        + [pl.BlockSpec((times, LANES), lambda _: (lax.axis_index("tm"), 0))]
+        + [pl.BlockSpec(memory_space=pl.ANY)] * len(after),
+        out_specs=[pl.BlockSpec((None, times, width), lambda n: (n, 0, 0))] * len(offsets),
+        out_shape=[pltpu.HBM((len(chunks), times, width), F32)] * len(offsets),
+        compiler_params=params(24),
+        name="pack",
+    )(*in_hbm([snapshots] * len(offsets)), window, *in_hbm(after))
+
+
+def transform_kernel(*refs):
+    odd_high, odd_low, two_high, two_low, four_high, four_low = refs[:6]
+    piece_refs, (out_ref, x_ref, odd_ref, two_ref, four_ref) = refs[6:-5], refs[-5:]
+    me = lax.axis_index("tm")
+    for m, piece_ref in enumerate(piece_refs):
+        times = piece_ref.shape[0]
+        rows = pl.ds(pl.multiple_of((me ^ m) * times, times), times)
+        x_ref[rows, :] = piece_ref[...]
+    total, width = x_ref.shape
+    quarter, part = total // 4, total // 8
+
+    def keep(ref, rows, cols, value):
+        ref[0, rows, cols], ref[1, rows, cols] = split(value)
+
+    for first in range(0, quarter, part):
+        for j in range(width // LANES):
+            cols = slice(j * LANES, (j + 1) * LANES)
+            rows = slice(first, first + part)
+            x = [x_ref[n * quarter + first : n * quarter + first + part, cols] for n in range(4)]
+            keep(odd_ref, rows, cols, x[0] - x[2])
+            keep(odd_ref, slice(quarter + first, quarter + first + part), cols, x[1] - x[3])
+            left, right = x[0] + x[2], x[1] + x[3]
+            keep(two_ref, rows, cols, left - right)
+            keep(four_ref, rows, cols, left + right)
+
+    dot = functools.partial(jnp.dot, preferred_element_type=F32)
+
+    def product(high, low, values):
+        return dot(high, values[0]) + dot(high, values[1]) + dot(low, values[0])
+
+    def store(start, both):
+        count = both.shape[0] // 2
+        low = low_half((count, LANES))
+        for j in range(CHUNK // 2):
+            cols = slice(j * LANES, (j + 1) * LANES)
+            real, imag = both[:count, cols], both[count:, cols]
+            first = jnp.where(low, real, pltpu.roll(imag, HALF, 1))
+            second = jnp.where(low, pltpu.roll(real, HALF, 1), imag)
+            for b, value in ((j, first), (j + CHUNK // 2, second)):
+                out_ref[pl.ds(start * CHUNK + b, count, stride=CHUNK), :] = value
+
+    for n in range(2):
+        rows = slice(2 * n * part, 2 * (n + 1) * part)
+        store(2 * n * part, product(odd_high[rows, :], odd_low[rows, :], odd_ref))
+    store(part, product(two_high[...], two_low[...], two_ref))
+    store(3 * part, product(four_high[...], four_low[...], four_ref))
+
+
+def transform(pieces, tables, slots):
+    chunks, times, width = pieces[0].shape
+    total = times * len(pieces)
+    quarter = total // 4
+    return pl.pallas_call(
+        transform_kernel,
+        grid=(chunks,),
+        in_specs=[pl.BlockSpec(table.shape, lambda n: (0, 0)) for table in tables]
+        + [pl.BlockSpec((None, times, width), lambda n: (n, 0, 0))] * len(pieces),
+        out_specs=pl.BlockSpec((None, slots * CHUNK, LANES), lambda n: (n, 0, 0)),
+        out_shape=pltpu.HBM((chunks, slots * CHUNK, LANES), F32),
+        scratch_shapes=[
+            pltpu.VMEM((total, width), F32),
+            pltpu.VMEM((2, 2 * quarter, width), BF16),
+            pltpu.VMEM((2, quarter, width), BF16),
+            pltpu.VMEM((2, quarter, width), BF16),
+        ],
+        compiler_params=params(40),
+        name="transform",
+    )(*tables, *in_hbm(pieces))
+
+
+def first_lane(chunk, chunks):
+    return sum(16 * i + 8 for i in range(chunk + 1, chunks))
+
+
+GROUP = 8
+
+
+def chunk_tiles(chunk, chunks, weight, parts, before):
+    flipped = jnp.where(low_half(weight.shape), weight, -weight)
+    width = CHUNK * (chunk + 1)
+    stride = width if LANES % width == 0 else 32
+    left, right = [], []
+    for row in parts:
+        row = row[: chunk + 1]
+        right.extend((row + row[-1:])[: stride // CHUNK])
+        left.append(row[-1] * weight)
+        left.append(pltpu.roll(row[-1], HALF, 1) * flipped)
+    lh, ll = split(jnp.concatenate(left, axis=0))
+    rh, rl = split(jnp.concatenate(right, axis=0))
+    full = lax.dot_general(
+        jnp.concatenate([lh, ll, lh], axis=1),
+        jnp.concatenate([rh, rh, rl], axis=1),
+        (((1,), (1,)), ((), ())),
+        preferred_element_type=F32,
+    )
+    if full.shape[1] < LANES:
+        full = jnp.concatenate([full] * (LANES // full.shape[1]), axis=1)
+    start = first_lane(chunk, chunks)
+    row = lax.broadcasted_iota(jnp.int32, (CHUNK, LANES), 0)
+    own = lax.broadcasted_iota(jnp.int32, (CHUNK, LANES), 1) - start
+    past = own >= width
+    corner = (own >= width - CHUNK) & (own < width) & (own - (width - CHUNK) > row)
+    valid = (own >= 0) & (own < width + CHUNK * chunk)
+    tiles = []
+    for k in range(GROUP):
+        first = k * stride // LANES * LANES
+        real = full[16 * k : 16 * k + 8, first : first + LANES]
+        imag = full[16 * k + 8 : 16 * k + 16, first : first + LANES]
+        shift = (start - (k * stride - first)) % LANES
+        out = pltpu.roll(real, shift, 1)
+        out = jnp.where(corner, pltpu.roll(imag, shift, 1), out)
+        out = jnp.where(past, pltpu.roll(imag, (shift + width) % LANES, 1), out)
+        tiles.append(jnp.where(valid, out, before[k]))
+    return tiles
+
+
+def early_gram_kernel(tile, chunks, scale, z_ref, w_ref, out_ref):
+    weight = w_ref[...] * scale
+
+    def step(g, carry):
+        parts = []
+        for k in range(GROUP):
+            rows = pl.ds(pl.multiple_of((g * GROUP + k) * CHUNK, CHUNK), CHUNK)
+            parts.append([z_ref[n, rows, :] for n in range(chunks - 1)])
+        tiles = [jnp.zeros((CHUNK, LANES), F32)] * GROUP
+        for chunk in range(chunks - 1):
+            tiles = chunk_tiles(chunk, chunks, weight, parts, tiles)
+        for k in range(GROUP):
+            out_ref[g * GROUP + k] = tiles[k]
+        return carry
+
+    lax.fori_loop(0, tile // GROUP, step, 0, unroll=True)
+
+
+def early_gram(spectra, weights, slots, tile, total_points):
+    chunks = spectra.shape[0] + 1
+    return pl.pallas_call(
+        functools.partial(early_gram_kernel, tile, chunks, 1.0 / total_points),
+        grid=(slots // tile,),
+        in_specs=[
+            pl.BlockSpec((chunks - 1, tile * CHUNK, LANES), lambda i: (0, i, 0)),
+            pl.BlockSpec((1, LANES), lambda i: (0, 0)),
+        ],
+        out_specs=pl.BlockSpec((tile, 8, LANES), lambda i: (i, 0, 0)),
+        out_shape=pltpu.HBM((slots, 8, LANES), F32),
+        compiler_params=params(24),
+        name="early_gram",
+    )(*in_hbm([spectra]), weights)
+
+
+def late_gram_kernel(tile, half, scale, *refs):
+    sources, w_ref, out_ref = refs[:3], refs[3], refs[4]
+    (early_ref, late_ref, before_ref), sems = refs[5:8], refs[8]
+    chunks = early_ref.shape[0] + 1
+    weight = w_ref[...] * scale
+    count = out_ref.shape[0]
+    base = pl.multiple_of((lax.axis_index("space") % 2 ^ half) * count, GROUP)
+
+    def copies(t):
+        there = pl.ds(pl.multiple_of((base + t * tile) * CHUNK, 8), tile * CHUNK)
+        here = pl.ds(pl.multiple_of(t * tile * CHUNK, 8), tile * CHUNK)
+        there_tile = pl.ds(pl.multiple_of(base + t * tile, 8), tile)
+        here_tile = pl.ds(pl.multiple_of(t * tile, 8), tile)
+        return [
+            pltpu.make_async_copy(sources[0].at[:, there], early_ref.at[:, here], sems.at[0, t]),
+            pltpu.make_async_copy(sources[1].at[:, there], late_ref.at[:, here], sems.at[1, t]),
+            pltpu.make_async_copy(
+                sources[2].at[there_tile], before_ref.at[here_tile], sems.at[2, t]
+            ),
+        ]
+
+    for t in range(count // tile):
+        for copy in copies(t):
+            copy.start()
+
+    def step(g, carry):
+        parts, before = [], []
+        for k in range(GROUP):
+            rows = pl.ds(pl.multiple_of((g * GROUP + k) * CHUNK, CHUNK), CHUNK)
+            parts.append([early_ref[n, rows, :] for n in range(chunks - 1)])
+            parts[-1].append(late_ref[0, rows, :])
+            before.append(before_ref[g * GROUP + k])
+        tiles = chunk_tiles(chunks - 1, chunks, weight, parts, before)
+        for k in range(GROUP):
+            out_ref[g * GROUP + k] = tiles[k]
+        return carry
+
+    groups = tile // GROUP
+
+    def one_tile(t, carry):
+        for copy in copies(t):
+            copy.wait()
+        return lax.fori_loop(0, groups, lambda g, c: step(t * groups + g, c), carry, unroll=True)
+
+    lax.fori_loop(0, count // tile, one_tile, 0)
+
+
+def late_gram(early, late, weights, before, slots, tile, total_points, half):
+    count = slots // 2
+    sizes = [(z.shape[0], count * CHUNK, LANES) for z in (early, late)] + [(count, 8, LANES)]
+    return pl.pallas_call(
+        functools.partial(late_gram_kernel, tile, half, 1.0 / total_points),
+        in_specs=[pl.BlockSpec(memory_space=pl.ANY)] * 3
+        + [pl.BlockSpec(memory_space=pltpu.VMEM)],
+        out_shape=pltpu.HBM((count, 8, LANES), F32),
+        scratch_shapes=[pltpu.VMEM(size, F32) for size in sizes]
+        + [pltpu.SemaphoreType.DMA((3, count // tile))],
+        compiler_params=params(24),
+        name="late_gram",
+    )(*in_hbm([early, late, before]), weights)
+
+
+def power_kernel(blocks, x_ref, out_ref):
+    count = x_ref.shape[2]
+    chunks = blocks // CHUNK
+    real = [[None] * chunks for _ in range(chunks)]
+    imag = [[None] * chunks for _ in range(chunks)]
+    for c in range(chunks):
+        start = first_lane(c, chunks)
+        for d in range(c):
+            x = x_ref[start + CHUNK * d : start + CHUNK * (d + 1)]
+            y = x_ref[start + CHUNK * (c + 1 + d) : start + CHUNK * (c + 2 + d)]
+            real[d][c], real[c][d] = x, jnp.swapaxes(x, 0, 1)
+            imag[d][c], imag[c][d] = y, -jnp.swapaxes(y, 0, 1)
+        x = x_ref[start + CHUNK * c : start + CHUNK * (c + 1)]
+        flip = jnp.swapaxes(x, 0, 1)
+        b = lax.broadcasted_iota(jnp.int32, x.shape, 0)
+        s = lax.broadcasted_iota(jnp.int32, x.shape, 1)
+        real[c][c] = jnp.where(b <= s, x, flip)
+        imag[c][c] = jnp.where(b > s, x, jnp.where(b < s, -flip, 0.0))
+    whole = lambda m: jnp.concatenate([jnp.concatenate(r, axis=1) for r in m], axis=0)
+    real, imag = whole(real), -whole(imag)
+
+    def apply(vr, vi):
+        vr, vi = vr[:, None, :], vi[:, None, :]
+        return jnp.sum(real * vr - imag * vi, axis=0), jnp.sum(real * vi + imag * vr, axis=0)
+
+    vr = jnp.full((blocks, count), 1.0 / math.sqrt(blocks), F32)
+    vi = jnp.zeros((blocks, count), F32)
+    for _ in range(POWER):
+        ur, ui = apply(vr, vi)
+        length = lax.rsqrt(jnp.sum(ur * ur + ui * ui, axis=0, keepdims=True) + 1e-06)
+        vr, vi = ur * length, ui * length
+    ur, ui = apply(vr, vi)
+    energy = jnp.sum(vr * ur + vi * ui, axis=0, keepdims=True)
+    out_ref[0:blocks, :] = vr
+    out_ref[blocks : 2 * blocks, :] = vi
+    out_ref[2 * blocks : 2 * blocks + 8, :] = jnp.broadcast_to(energy, (8, count))
+
+
+def power(packed, blocks):
+    return pl.pallas_call(
+        functools.partial(power_kernel, blocks),
+        out_shape=jax.ShapeDtypeStruct((2 * blocks + 8, packed.shape[2]), F32),
+        compiler_params=params(32),
+        name="power",
+    )(packed)
+
+
+def reverse_rows(value):
+    row = lax.broadcasted_iota(jnp.int32, (8, LANES), 0)
+    tiles = []
+    for start in range(0, value.shape[0], 8):
+        tile = value[start : start + 8]
+        for span in (1, 2, 4):
+            upper = (row & span) == 0
+            tile = jnp.where(upper, pltpu.roll(tile, 8 - span, 0), pltpu.roll(tile, span, 0))
+        tiles.append(tile)
+    return jnp.concatenate(tiles[::-1], axis=0)
+
+
+def modes_kernel(tile, classes, total_times, *refs):
+    early, late, v_ref, out_ref, energy_ref, z_ref, s_ref, e_ref, sems = refs
+    chunks = z_ref.shape[0]
+    blocks = CHUNK * z_ref.shape[0]
+    group = 8
+    lane = lax.broadcasted_iota(jnp.int32, (group, LANES), 1)
+    row = lax.broadcasted_iota(jnp.int32, (group, LANES), 0)
+    per_tile = LANES // blocks
+    low = low_half((group, LANES))
+
+    def spread(vector):
+        vector = jnp.where(lane < blocks, vector, 0.0)
+        span = blocks
+        while span < LANES:
+            vector = vector + pltpu.roll(vector, span, 1)
+            span *= 2
+        parts = []
+        for first in range(0, group, per_tile):
+            parts.append(jnp.where(lane // blocks + first == row, vector, 0.0))
+        return jnp.concatenate(parts, axis=1)
+
+    def step(g, carry):
+        start = pl.multiple_of(g * group, group)
+        vec = v_ref[pl.ds(start, group), :]
+        both = jnp.concatenate([spread(vec), spread(pltpu.roll(vec, LANES - blocks, 1))], axis=0)
+        vh, vl = split(both)
+        z = []
+        for k in range(group):
+            rows = pl.ds(pl.multiple_of((g * group + k) * CHUNK, CHUNK), CHUNK)
+            z.append(z_ref[:, rows, :].reshape(blocks, LANES))
+        zh, zl = split(jnp.concatenate(z, axis=0))
+        full = jnp.dot(
+            jnp.concatenate([vh, vl], axis=0),
+            jnp.concatenate([zh, zl], axis=1),
+            preferred_element_type=F32,
+        )
+        sums = full[:16, :LANES] + full[:16, LANES:] + full[16:, :LANES]
+        turned = pltpu.roll(sums[8:], HALF, 1)
+        value = sums[:8] + jnp.where(low, -turned, turned)
+        energy = jnp.broadcast_to(vec[:, 2 * blocks : 2 * blocks + 1], (group, LANES))
+        s_ref[pl.ds(start, group), :] = value * lax.rsqrt(energy + 1e-06)
+        e_ref[pl.ds(start, group), :] = energy
+        return carry
+
+    groups = tile // group
+    tiles = v_ref.shape[0] // tile
+
+    def copies(t):
+        rows = pl.ds(pl.multiple_of(t * tile * CHUNK, CHUNK), tile * CHUNK)
+        first, second = z_ref.at[: chunks - 1, rows], z_ref.at[chunks - 1 :, rows]
+        return (
+            pltpu.make_async_copy(early.at[:, rows], first, sems.at[0, t]),
+            pltpu.make_async_copy(late.at[:, rows], second, sems.at[1, t]),
+        )
+
+    for t in range(tiles):
+        for copy in copies(t):
+            copy.start()
+
+    def one_tile(t, carry):
+        for copy in copies(t):
+            copy.wait()
+        return lax.fori_loop(0, groups, lambda g, c: step(t * groups + g, c), carry, unroll=True)
+
+    lax.fori_loop(0, tiles, one_tile, 0)
+
+    half = out_ref.shape[0] // classes // 2
+    bits = classes.bit_length() - 1
+    low = low_half((half, LANES))
+    for d in range(classes):
+        r = bit_reverse(d, bits)
+        direct = pl.ds(slot_of(r, total_times), half, stride=classes // 4)
+        mirror = pl.ds(slot_of(classes - r, total_times), half, stride=classes // 4)
+        start = 2 * half * d
+        out_ref[start : start + half, :] = s_ref[direct, :]
+        energy_ref[start : start + half, :] = e_ref[direct, :]
+        turned = reverse_rows(s_ref[mirror, :])
+        out_ref[start + half : start + 2 * half, :] = jnp.where(low, turned, -turned)
+        energy_ref[start + half : start + 2 * half, :] = reverse_rows(e_ref[mirror, :])
+
+
+def modes(early, late, vectors, total, classes, slots, tile):
+    return pl.pallas_call(
+        functools.partial(modes_kernel, tile, classes, total),
+        in_specs=[
+            pl.BlockSpec(memory_space=pl.ANY),
+            pl.BlockSpec(memory_space=pl.ANY),
+            pl.BlockSpec(memory_space=pltpu.VMEM),
+        ],
+        out_shape=[jax.ShapeDtypeStruct((total, LANES), F32)] * 2,
+        scratch_shapes=[
+            pltpu.VMEM((early.shape[0] + 1, *early.shape[1:]), F32),
+            pltpu.VMEM((slots, LANES), F32),
+            pltpu.VMEM((slots, LANES), F32),
+            pltpu.SemaphoreType.DMA((2, slots // tile)),
+        ],
+        compiler_params=params(24),
+        name="modes",
+    )(*in_hbm([early, late]), vectors)
+
+
+def place_kernel(x_ref, out_ref):
+    low = low_half(x_ref.shape[1:])
+    for i in range(x_ref.shape[0] // 2):
+        first, second = x_ref[2 * i], x_ref[2 * i + 1]
+        cols = slice(i * LANES, (i + 1) * LANES)
+        out_ref[0, :, cols] = jnp.where(low, first, pltpu.roll(second, HALF, 1))
+        out_ref[1, :, cols] = jnp.where(low, pltpu.roll(first, HALF, 1), second)
+
+
+def place(pieces):
+    count, rows, _ = pieces.shape
+    return pl.pallas_call(
+        place_kernel,
+        out_shape=jax.ShapeDtypeStruct((2, rows, count * HALF), F32),
+        compiler_params=params(32),
+        name="place",
+    )(pieces)
+
+
+def exchange(value, axes):
+    return lax.all_to_all(value, axes, 0, 0, tiled=True)
+
+
+def body(mesh_shape, snapshots, quad_weights):
+    tm_size, space_size = mesh_shape["tm"], mesh_shape["space"]
+    local_times, blocks, points = snapshots.shape
+    total_times = local_times * tm_size
+    total_points = points * space_size
+    devices = tm_size * space_size
+    per_device = -(-(total_times // 2 + 1) // devices)
+    slots = per_device * devices
+    tile = slots // 4
+    tables = transform_tables(total_times, slots)
+    window = window_table(total_times)
+
+    here = lax.axis_index("tm") * HALF
+    weights = lax.dynamic_slice(quad_weights, (here,), (HALF,))
+    weights = jnp.concatenate([weights, weights])[None, :]
+
+    chunks = blocks // CHUNK
+
+    def send(group, offsets, after):
+        sent = dict(zip(offsets, pack(snapshots, window, group, tuple(offsets), after)))
+        flying = {}
+        for m, part in sent.items():
+            pairs = [(d, d ^ m) for d in range(tm_size)]
+            flying[m] = lax.ppermute(part, "tm", pairs) if m else part
+        return sent, flying
+
+    half, quarter = tm_size // 2, tm_size // 4
+    first = [*range(half, half + quarter), *range(quarter)]
+    second = [*range(half + quarter, tm_size), *range(quarter, half)]
+    group = range(chunks - 1)
+    sent, pieces = send(group, first, [])
+    pieces |= send(group, second, [sent[0]])[1]
+    group = range(chunks - 1, chunks)
+    sent, last = send(group, first, [pieces[half]])
+    last |= send(group, second, [sent[0], pieces[half + quarter]])[1]
+    ordered = lambda pieces: [pieces[m] for m in range(tm_size)]
+    early = transform(ordered(pieces), tables, slots)
+    matrices = early_gram(early, weights, slots, tile, total_points)
+    late = transform(ordered(last), tables, slots)
+
+    space = lax.axis_index("space")
+
+    def swap(value, level):
+        pairs = [(i, i ^ (1 << level)) for i in range(space_size)]
+        return lax.ppermute(value, "space", pairs)
+
+    arriving = swap(late_gram(early, late, weights, matrices, slots, tile, total_points, 1), 0)
+    part = late_gram(early, late, weights, matrices, slots, tile, total_points, 0)
+    levels = space_size.bit_length() - 1
+    shape = (*[2] * (levels - 1), tm_size, per_device, *part.shape[1:])
+    part, arriving = part.reshape(shape), arriving.reshape(shape)
+    for level in range(1, levels):
+        bit = space >> level & 1
+        pick = lambda value, i: lax.dynamic_index_in_dim(value, i, 0, keepdims=False)
+        given = pick(part, 1 - bit) + pick(arriving, 1 - bit)
+        part = pick(part, bit) + pick(arriving, bit)
+        arriving = swap(given, level)
+    part = exchange(part + arriving, "tm").sum(axis=0)
+
+    vectors = power(part.transpose(2, 1, 0), blocks).T
+    vectors = jnp.pad(vectors, ((0, 0), (0, LANES - vectors.shape[1])))
+    vectors = jnp.broadcast_to(vectors[None], (devices, per_device, LANES))
+    vectors = exchange(vectors, ("tm", "space"))
+    vectors = vectors.reshape(tm_size, *[2] * levels, per_device, LANES)
+    vectors = vectors.transpose(*range(levels, -1, -1), levels + 1, levels + 2)
+    vectors = vectors.reshape(slots, LANES)
+
+    pieces, energies = modes(early, late, vectors, total_times, tm_size, slots, tile)
+    pieces = exchange(pieces.reshape(tm_size, local_times, LANES), "tm")
+    energies = energies.reshape(tm_size, local_times, LANES)[:, :, 0]
+    energies = lax.dynamic_index_in_dim(energies, lax.axis_index("tm"), 0, keepdims=False)
+    return place(pieces), energies
+
+
+def fits(mesh_shape, times, blocks, points):
+    tm_size, space_size = mesh_shape["tm"], mesh_shape["space"]
+    return (
+        points == space_size * tm_size * HALF
+        and tm_size == 8
+        and space_size & (space_size - 1) == 0
+        and times % (tm_size * 8) == 0
+        and blocks % CHUNK == 0
+        and blocks == 32
+    )
 
 
 def matvec(matrix, vector):
@@ -36,7 +620,7 @@
     return (vec_real, vec_imag, energy)
 
 
-def body(snapshots, quad_weights):
+def general_body(snapshots, quad_weights):
     tm_size = lax.axis_size("tm")
     bit_count = tm_size.bit_length() - 1
     local_times, blocks, points = snapshots.shape
@@ -96,10 +680,18 @@
 
 
 def solution(mesh):
-    return jax.shard_map(
-        body,
-        mesh=mesh,
-        in_specs=(P("tm", None, "space"), P("space")),
-        out_specs=(P(None, "tm", "space"), P("tm")),
-        check_vma=False,
-    )
+    shape = dict(mesh.shape)
+
+    def program(snapshots, quad_weights):
+        chosen = general_body
+        if fits(shape, *snapshots.shape):
+            chosen = functools.partial(body, shape)
+        return jax.shard_map(
+            chosen,
+            mesh=mesh,
+            in_specs=(P("tm", None, "space"), P("space")),
+            out_specs=(P(None, "tm", "space"), P("tm")),
+            check_vma=False,
+        )(snapshots, quad_weights)
+
+    return program

time: 1030 us -> 290 us (0.28)
  blocking collectives: 367 us -> 45.5 us
  matrix products: 191 us -> 0 us
  local copies, waits for them, and re-layouts: 164 us -> 3.08 us
  waiting for transfers between devices: 236 us -> 109 us
  Pallas kernels: 0 us -> 62.8 us
  starting transfers between devices: 7.32 us -> 65.9 us
  other arithmetic: 39.7 us -> 2.52 us
  between operations: 14.5 us -> 0.87 us
    all_to_all x1 -> x2, blocking collectives: 367 us -> 45.5 us  [exchange(): return lax.all_to_all(value, axes, 0, 0, tiled=True)]
    dot_general x13 -> x0, matrix products: 191 us -> none  [the longest x4 62.8 us: one_block(): jnp.dot(cos_tab, columns, precision=lax.Precision.HIGHEST)]
    all_to_all x1, waiting for transfers between devices: 183 us -> 13.7 us  [exchange(): return lax.all_to_all(value, axes, 0, 0, tiled=True)]
    ppermute x0 -> x16, waiting for transfers between devices: none -> 94.8 us  [the longest x14 81.2 us: send(): flying[m] = lax.ppermute(part, 'tm', pairs) if m else part]
    pallas_call x0 -> x12, Pallas kernels: none -> 62.8 us  [the longest x4 18.3 us: pack(): pl.pallas_call(functools.partial(pack_kernel, offsets), grid=(len(chunks)...]
    ppermute x0 -> x16, starting transfers between devices: none -> 62.4 us  [the longest x14 60.7 us: send(): flying[m] = lax.ppermute(part, 'tm', pairs) if m else part]
    all_to_all x4 -> x1, local copies, waits for them, and re-layouts: 56.6 us -> 0.05 us  [exchange(): return lax.all_to_all(value, axes, 0, 0, tiled=True)]
    psum x1 -> x0, waiting for transfers between devices: 53.3 us -> none  [body(): real_gram, imag_gram = lax.psum((real_gram, imag_gram), 'space')]
  transfers between devices with their start and end apart: 2 -> 17, of which waited for: 2 -> 5; matrix products, arithmetic and copies ran while one was open for 3% -> 0% of each run, Pallas kernels for 0% -> 13%
where the time goes in v2:
time: 290 us; the launch traced here: 289 us
  waiting for transfers between devices  109 us (38%)
  starting transfers between devices  65.9 us (23%)
  Pallas kernels  62.8 us (22%)
  blocking collectives  45.5 us (16%)
  local copies, waits for them, and re-layouts  3.08 us (1%)
    ppermute x14, waiting for transfers between devices, send(): flying[m] = lax.ppermute(part, 'tm', pairs) if m else part  81.2 us
    ppermute x14, starting transfers between devices, send(): flying[m] = lax.ppermute(part, 'tm', pairs) if m else part  60.7 us
    all_to_all x2, blocking collectives, exchange(): return lax.all_to_all(value, axes, 0, 0, tiled=True)  45.5 us
    pallas_call x4, Pallas kernels, pack(): pl.pallas_call(functools.partial(pack_kernel, offsets), grid=(len(chunks)...  18.3 us
    pallas_call x2, Pallas kernels, transform(): pl.pallas_call(transform_kernel, grid=(chunks,), in_specs=[pl.BlockSpec(t...  14.3 us
    all_to_all x1, waiting for transfers between devices, exchange(): return lax.all_to_all(value, axes, 0, 0, tiled=True)  13.7 us
    ppermute x2, waiting for transfers between devices, swap(): return lax.ppermute(value, 'space', pairs)  13.6 us
    pallas_call x1, Pallas kernels, early_gram(): pl.pallas_call(functools.partial(early_gram_kernel, tile, chunks, 1.0 / t...  11.3 us
  transfers between devices with their start and end apart: 17, of which 5 were waited for; matrix products, arithmetic and copies ran while one was open for 0% of the time, Pallas kernels for 13%

profile of v2, /device:TPU:0, one launch (start us, length us, event | category | flops | bytes accessed | tf_op | source)
XLA Modules:
  0.0 289.1 jit_solution(651709879133922941)
XLA Ops:
  0.6 1.0 copy-done
  1.7 6.0 %pack.4 = (f32[3,128,512]{2,1,0:T(8,128)}, f32[3,128,512]{2,1,0:T(8,128)}, f32[3,128,512]{2,1,0:T(8,128)}, f32[3,128,512]{2,1,0:T(8,128)}) custom-call(f32[128,32,512]{2,1,0:T(8,128)} %refs_3_.9, f32[128,32,512]{2,1,0:T(8,128)} %refs_3_.9, f32[128,32,512]{2,1,0:T(8,128)} %refs_3_.9, f32[128,32,512]{2,1,0:T(8,128)} %refs_3_.9, f32[1024,128]{1,0:T(8,128)S(1)} %copy-done), custom_call_target="tpu_custom_call" | custom-call | tf_op jit(solution)/shard_map/pack/pallas_call | solution.py:108
  7.7 4.0 %collective-permute-start.3 = (f32[3,128,512]{2,1,0:T(8,128)}, f32[3,128,512]{2,1,0:T(8,128)S(1)}, u32[]{:S(2)}, u32[]{:S(2)}) collective-permute-start(f32[3,128,512]{2,1,0:T(8,128)} %get-tuple-element.24), channel_id=1, source_target_pairs={{0,16},{4,20},{8,24},{12,28},{16,0},{20,4},{24,8},{28,12},{1,17},{... | collective-permute-start | bytes 2359304 | tf_op jit(solution)/shard_map/ppermute | solution.py:539
  11.7 6.2 %pack.5 = (f32[3,128,512]{2,1,0:T(8,128)}, f32[3,128,512]{2,1,0:T(8,128)}, f32[3,128,512]{2,1,0:T(8,128)}, f32[3,128,512]{2,1,0:T(8,128)}) custom-call(f32[128,32,512]{2,1,0:T(8,128)} %refs_3_.9, f32[128,32,512]{2,1,0:T(8,128)} %refs_3_.9, f32[128,32,512]{2,1,0:T(8,128)} %refs_3_.9, f32[128,32,512]{2,1,0:T(8,128)} %refs_3_.9, f32[1024,128]{1,0:T(8,128)S(1)} %copy-done, ...), custom_call_target="tpu_custom_call" | custom-call | tf_op jit(solution)/shard_map/pack/pallas_call | solution.py:108
  17.9 1.3 collective-permute-start.5
  19.2 1.5 collective-permute-start
  21.0 1.7 collective-permute-start.2
  22.7 41.4 %collective-permute-done.3.refs_10_.refs_5_ = f32[3,128,512]{2,1,0:T(8,128)S(1)} collective-permute-done((f32[3,128,512]{2,1,0:T(8,128)}, f32[3,128,512]{2,1,0:T(8,128)S(1)}, u32[]{:S(2)}, u32[]{:S(2)}) %collective-permute-start.3) | collective-permute-done | bytes 786464 | tf_op jit(solution)/shard_map/ppermute | solution.py:539
  65.0 2.9 %collective-permute-start.6 = (f32[3,128,512]{2,1,0:T(8,128)}, f32[3,128,512]{2,1,0:T(8,128)}, u32[]{:S(2)}, u32[]{:S(2)}) collective-permute-start(f32[3,128,512]{2,1,0:T(8,128)} %get-tuple-element.27), channel_id=1, source_target_pairs={{0,28},{4,24},{8,20},{12,16},{16,12},{20,8},{24,4},{28,0},{1,29},{... | collective-permute-start | bytes 2359304 | tf_op jit(solution)/shard_map/ppermute | solution.py:539
  67.9 3.0 %pack.6 = (f32[1,128,512]{2,1,0:T(8,128)}, f32[1,128,512]{2,1,0:T(8,128)}, f32[1,128,512]{2,1,0:T(8,128)}, f32[1,128,512]{2,1,0:T(8,128)}) custom-call(f32[128,32,512]{2,1,0:T(8,128)} %refs_3_.9, f32[128,32,512]{2,1,0:T(8,128)} %refs_3_.9, f32[128,32,512]{2,1,0:T(8,128)} %refs_3_.9, f32[128,32,512]{2,1,0:T(8,128)} %refs_3_.9, f32[1024,128]{1,0:T(8,128)S(1)} %copy-done, ...), custom_call_target="tpu_custom_call" | custom-call | tf_op jit(solution)/shard_map/pack/pallas_call | solution.py:108
  71.0 3.1 %pack.7 = (f32[1,128,512]{2,1,0:T(8,128)}, f32[1,128,512]{2,1,0:T(8,128)}, f32[1,128,512]{2,1,0:T(8,128)}, f32[1,128,512]{2,1,0:T(8,128)}) custom-call(f32[128,32,512]{2,1,0:T(8,128)} %refs_3_.9, f32[128,32,512]{2,1,0:T(8,128)} %refs_3_.9, f32[128,32,512]{2,1,0:T(8,128)} %refs_3_.9, f32[128,32,512]{2,1,0:T(8,128)} %refs_3_.9, f32[1024,128]{1,0:T(8,128)S(1)} %copy-done, ...), custom_call_target="tpu_custom_call" | custom-call | tf_op jit(solution)/shard_map/pack/pallas_call | solution.py:108
  74.1 1.1 collective-permute-start.7
  75.2 17.1 %collective-permute-start.8 = (f32[1,128,512]{2,1,0:T(8,128)}, f32[1,128,512]{2,1,0:T(8,128)}, u32[]{:S(2)}, u32[]{:S(2)}) collective-permute-start(f32[1,128,512]{2,1,0:T(8,128)} %get-tuple-element.30), channel_id=1, source_target_pairs={{0,8},{4,12},{8,0},{12,4},{16,24},{20,28},{24,16},{28,20},{1,9},{5... | collective-permute-start | bytes 786440 | tf_op jit(solution)/shard_map/ppermute | solution.py:539
  92.4 1.0 collective-permute-start.9
  93.4 39.5 %collective-permute-done.4.refs_11_ = f32[3,128,512]{2,1,0:T(8,128)} collective-permute-done((f32[3,128,512]{2,1,0:T(8,128)S(1)}, f32[3,128,512]{2,1,0:T(8,128)}, u32[]{:S(2)}, u32[]{:S(2)}) %collective-permute-start.4) | collective-permute-done | bytes 786464 | tf_op jit(solution)/shard_map/ppermute | solution.py:539
  132.9 24.0 %collective-permute-start.11 = (f32[1,128,512]{2,1,0:T(8,128)}, f32[1,128,512]{2,1,0:T(8,128)}, u32[]{:S(2)}, u32[]{:S(2)}) collective-permute-start(f32[1,128,512]{2,1,0:T(8,128)} %get-tuple-element.33), channel_id=1, source_target_pairs={{0,20},{4,16},{8,28},{12,24},{16,4},{20,0},{24,12},{28,8},{1,21},{... | collective-permute-start | bytes 786440 | tf_op jit(solution)/shard_map/ppermute | solution.py:539
  157.9 3.8 %collective-permute-start.13 = (f32[1,128,512]{2,1,0:T(8,128)}, f32[1,128,512]{2,1,0:T(8,128)}, u32[]{:S(2)}, u32[]{:S(2)}) collective-permute-start(f32[1,128,512]{2,1,0:T(8,128)} %get-tuple-element.35), channel_id=1, source_target_pairs={{0,28},{4,24},{8,20},{12,16},{16,12},{20,8},{24,4},{28,0},{1,29},{... | collective-permute-start | bytes 786440 | tf_op jit(solution)/shard_map/ppermute | solution.py:539
  162.6 9.3 %transform.2.z_ref.refs_0_ = f32[3,4352,128]{2,1,0:T(8,128)} custom-call(bf16[512,512]{1,0:T(8,128)(2,1)S(1)} %copy-done.1, bf16[512,512]{1,0:T(8,128)(2,1)S(1)} %copy-done.2, bf16[256,256]{1,0:T(8,128)(2,1)S(1)} %copy-done.5, bf16[256,256]{1,0:T(8,128)(2,1)S(1)} %copy-done.6, bf16[320,256]{1,0:T(8,128)(2,1)S(1)} %copy-done.3, ...), custom_call_target="tpu_custom_call" | custom-call | tf_op jit(solution)/shard_map/transform/pallas_call | solution.py:173
  171.9 11.3 %early_gram.1.refs_2_ = f32[544,8,128]{2,1,0:T(8,128)} custom-call(f32[3,4352,128]{2,1,0:T(8,128)} %transform.2.z_ref.refs_0_, f32[1,128]{1,0:T(1,128)S(1)} %maximum_bitcast_fusion.w_ref.refs_3_), custom_call_target="tpu_custom_call" | custom-call | tf_op jit(solution)/shard_map/early_gram/pallas_call | solution.py:257
  183.4 4.9 %transform.3.refs_1_ = f32[1,4352,128]{2,1,0:T(8,128)} custom-call(bf16[512,512]{1,0:T(8,128)(2,1)S(1)} %copy-done.1, bf16[512,512]{1,0:T(8,128)(2,1)S(1)} %copy-done.2, bf16[256,256]{1,0:T(8,128)(2,1)S(1)} %copy-done.5, bf16[256,256]{1,0:T(8,128)(2,1)S(1)} %copy-done.6, bf16[320,256]{1,0:T(8,128)(2,1)S(1)} %copy-done.3, bf16[320,256]{1,0:T(8,128)(2,1)S(1)} %copy-done.4, ...), custom_call_target="tpu_custom_call" | custom-call | tf_op jit(solution)/shard_map/transform/pallas_call | solution.py:173
  188.4 5.5 %late_gram.3 = f32[272,8,128]{2,1,0:T(8,128)} custom-call(f32[3,4352,128]{2,1,0:T(8,128)} %transform.2.z_ref.refs_0_, f32[1,4352,128]{2,1,0:T(8,128)} %transform.3.refs_1_, f32[544,8,128]{2,1,0:T(8,128)} %early_gram.1.refs_2_, f32[1,128]{1,0:T(1,128)S(1)} %maximum_bitcast_fusion.w_ref.refs_3_), custom_call_target="tpu_custom_call" | custom-call | tf_op jit(solution)/shard_map/late_gram/pallas_call | solution.py:321
  193.9 5.5 %late_gram.2 = f32[272,8,128]{2,1,0:T(8,128)} custom-call(f32[3,4352,128]{2,1,0:T(8,128)} %transform.2.z_ref.refs_0_, f32[1,4352,128]{2,1,0:T(8,128)} %transform.3.refs_1_, f32[544,8,128]{2,1,0:T(8,128)} %early_gram.1.refs_2_, f32[1,128]{1,0:T(1,128)S(1)} %maximum_bitcast_fusion.w_ref.refs_3_), custom_call_target="tpu_custom_call" | custom-call | tf_op jit(solution)/shard_map/late_gram/pallas_call | solution.py:321
  199.4 1.2 add_bitcast_fusion
  200.7 1.6 collective-permute-start.15
  202.2 13.6 %collective-permute-done.15 = f32[8,17,8,128]{3,2,1,0:T(8,128)} collective-permute-done((f32[8,17,8,128]{3,2,1,0:T(8,128)S(1)}, f32[8,17,8,128]{3,2,1,0:T(8,128)}, u32[]{:S(2)}, u32[]{:S(2)}) %collective-permute-start.15) | collective-permute-done | bytes 557088 | tf_op jit(solution)/shard_map/ppermute | solution.py:560
  215.9 1.2 bitcast_add_fusion
  217.0 29.7 %all_to_all.15 = f32[8,17,8,128]{3,2,1,0:T(8,128)S(1)} all-to-all(f32[8,17,8,128]{3,2,1,0:T(8,128)S(1)} %bitcast_add_fusion), channel_id=1, replica_groups=mesh['tm'=8,'space'=4] {'tm'}, dimensions={0} | all-to-all | bytes 1114112 | tf_op jit(solution)/shard_map/all_to_all | solution.py:513
  247.0 1.3 power.1
  248.4 15.8 %all_to_all.16 = f32[32,17,128]{2,1,0:T(8,128)S(1)} all-to-all(f32[32,17,128]{2,1,0:T(8,128)S(1)} %broadcast_in_dim.10), channel_id=1, replica_groups=mesh['tm'=8,'space'=4] {'tm','space'}, dimensions={0} | all-to-all | bytes 557056 | tf_op jit(solution)/shard_map/all_to_all | solution.py:513
  264.5 5.8 %modes.1 = (f32[1024,128]{1,0:T(8,128)}, f32[1024,128]{1,0:T(8,128)S(1)}) custom-call(f32[3,4352,128]{2,1,0:T(8,128)} %transform.2.z_ref.refs_0_, f32[1,4352,128]{2,1,0:T(8,128)} %transform.3.refs_1_, f32[544,128]{1,0:T(8,128)S(1)} %reshape.30.refs_2_), custom_call_target="tpu_custom_call" | custom-call | tf_op jit(solution)/shard_map/modes/pallas_call | solution.py:474
  270.3 3.5 %all-to-all-start.2 = ((f32[8,128,128]{2,1,0:T(8,128)}), f32[8,128,128]{2,1,0:T(8,128)S(1)}, u32[]{:S(2)}, u32[]{:S(2)}) async-start(f32[8,128,128]{2,1,0:T(8,128)} %bitcast.9), calls=%async_computation.2 | async-start | bytes 1048576 | tf_op jit(solution)/shard_map/all_to_all | solution.py:513
  274.4 13.7 %all-to-all-done.2.x_ref = f32[8,128,128]{2,1,0:T(8,128)S(1)} async-done(((f32[8,128,128]{2,1,0:T(8,128)}), f32[8,128,128]{2,1,0:T(8,128)S(1)}, u32[]{:S(2)}, u32[]{:S(2)}) %all-to-all-start.2) | async-done | bytes 524320 | tf_op jit(solution)/shard_map/all_to_all | solution.py:513
  (62 shorter events, 5.8 us)
Async XLA Ops:
  7.7 56.4 %collective-permute-start.3 = (f32[3,128,512]{2,1,0:T(8,128)}, f32[3,128,512]{2,1,0:T(8,128)S(1)}, u32[]{:S(2)}, u32[]{:S(2)}) collective-permute-start(f32[3,128,512]{2,1,0:T(8,128)} %get-tuple-element.24), channel_id=1, source_target_pairs={{0,16},{4,20},{8,24},{12,28},{16,0},{20,4},{24,8},{28,12},{1,17},{... | collective-permute-start | bytes 2359304 | tf_op jit(solution)/shard_map/ppermute | solution.py:539
  11.7 7.5 %copy-start.14 = (f32[3,128,512]{2,1,0:T(8,128)S(1)}, f32[3,128,512]{2,1,0:T(8,128)}, u32[]{:S(2)}) copy-start(f32[3,128,512]{2,1,0:T(8,128)} %get-tuple-element.21) | copy-start | bytes 2359300
  11.7 52.3 %copy-start.13 = (f32[3,128,512]{2,1,0:T(8,128)S(1)}, f32[3,128,512]{2,1,0:T(8,128)}, u32[]{:S(2)}) copy-start(f32[3,128,512]{2,1,0:T(8,128)} %get-tuple-element.25) | copy-start | bytes 2359300
  17.9 47.1 %collective-permute-start.5 = (f32[3,128,512]{2,1,0:T(8,128)}, f32[3,128,512]{2,1,0:T(8,128)S(1)}, u32[]{:S(2)}, u32[]{:S(2)}) collective-permute-start(f32[3,128,512]{2,1,0:T(8,128)} %get-tuple-element.26), channel_id=1, source_target_pairs={{0,24},{4,28},{8,16},{12,20},{16,8},{20,12},{24,0},{28,4},{1,25},{... | collective-permute-start | bytes 2359304 | tf_op jit(solution)/shard_map/ppermute | solution.py:539
  19.2 54.9 %collective-permute-start = (f32[3,128,512]{2,1,0:T(8,128)S(1)}, f32[3,128,512]{2,1,0:T(8,128)S(1)}, u32[]{:S(2)}, u32[]{:S(2)}) collective-permute-start(f32[3,128,512]{2,1,0:T(8,128)S(1)} %copy-done.14), channel_id=1, source_target_pairs={{0,4},{4,0},{8,12},{12,8},{16,20},{20,16},{24,28},{28,24},{1,5},{5... | collective-permute-start | bytes 2359304 | tf_op jit(solution)/shard_map/ppermute | solution.py:539
  20.7 54.5 %collective-permute-start.1 = (f32[3,128,512]{2,1,0:T(8,128)}, f32[3,128,512]{2,1,0:T(8,128)S(1)}, u32[]{:S(2)}, u32[]{:S(2)}) collective-permute-start(f32[3,128,512]{2,1,0:T(8,128)} %get-tuple-element.22), channel_id=1, source_target_pairs={{0,8},{4,12},{8,0},{12,4},{16,24},{20,28},{24,16},{28,20},{1,9},{5... | collective-permute-start | bytes 2359304 | tf_op jit(solution)/shard_map/ppermute | solution.py:539
  21.0 71.3 %collective-permute-start.2 = (f32[3,128,512]{2,1,0:T(8,128)}, f32[3,128,512]{2,1,0:T(8,128)}, u32[]{:S(2)}, u32[]{:S(2)}) collective-permute-start(f32[3,128,512]{2,1,0:T(8,128)} %get-tuple-element.23), channel_id=1, source_target_pairs={{0,12},{4,8},{8,4},{12,0},{16,28},{20,24},{24,20},{28,16},{1,13},{... | collective-permute-start | bytes 2359304 | tf_op jit(solution)/shard_map/ppermute | solution.py:539
  64.1 3.9 %copy-start.8 = (f32[3,128,512]{2,1,0:T(8,128)}, f32[3,128,512]{2,1,0:T(8,128)S(1)}, u32[]{:S(2)}) copy-start(f32[3,128,512]{2,1,0:T(8,128)S(1)} %collective-permute-done.3.refs_10_.refs_5_) | copy-start | bytes 2359300
  64.1 68.8 %collective-permute-start.4 = (f32[3,128,512]{2,1,0:T(8,128)S(1)}, f32[3,128,512]{2,1,0:T(8,128)}, u32[]{:S(2)}, u32[]{:S(2)}) collective-permute-start(f32[3,128,512]{2,1,0:T(8,128)S(1)} %copy-done.13), channel_id=1, source_target_pairs={{0,20},{4,16},{8,28},{12,24},{16,4},{20,0},{24,12},{28,8},{1,21},{... | collective-permute-start | bytes 2359304 | tf_op jit(solution)/shard_map/ppermute | solution.py:539
  65.0 5.9 %copy-start.9 = (f32[3,128,512]{2,1,0:T(8,128)}, f32[3,128,512]{2,1,0:T(8,128)S(1)}, u32[]{:S(2)}) copy-start(f32[3,128,512]{2,1,0:T(8,128)S(1)} %collective-permute-done.5.refs_12_.refs_6_) | copy-start | bytes 2359300
  65.0 67.9 %collective-permute-start.6 = (f32[3,128,512]{2,1,0:T(8,128)}, f32[3,128,512]{2,1,0:T(8,128)}, u32[]{:S(2)}, u32[]{:S(2)}) collective-permute-start(f32[3,128,512]{2,1,0:T(8,128)} %get-tuple-element.27), channel_id=1, source_target_pairs={{0,28},{4,24},{8,20},{12,16},{16,12},{20,8},{24,4},{28,0},{1,29},{... | collective-permute-start | bytes 2359304 | tf_op jit(solution)/shard_map/ppermute | solution.py:539
  70.9 3.2 %copy-start.15 = (f32[1,128,512]{2,1,0:T(8,128)S(1)}, f32[1,128,512]{2,1,0:T(8,128)}, u32[]{:S(2)}) copy-start(f32[1,128,512]{2,1,0:T(8,128)} %get-tuple-element.29) | copy-start | bytes 786436
  70.9 91.6 %copy-start.1 = (bf16[512,512]{1,0:T(8,128)(2,1)S(1)}, bf16[512,512]{1,0:T(8,128)(2,1)}, u32[]{:S(2)}) copy-start(bf16[512,512]{1,0:T(8,128)(2,1)} %constant.54.clone.refs_0_) | copy-start | bytes 1572868
  70.9 91.6 %copy-start.2 = (bf16[512,512]{1,0:T(8,128)(2,1)S(1)}, bf16[512,512]{1,0:T(8,128)(2,1)}, u32[]{:S(2)}) copy-start(bf16[512,512]{1,0:T(8,128)(2,1)} %constant.55.clone.refs_1_) | copy-start | bytes 1572868
  70.9 91.6 %copy-start.3 = (bf16[320,256]{1,0:T(8,128)(2,1)S(1)}, bf16[320,256]{1,0:T(8,128)(2,1)}, u32[]{:S(2)}) copy-start(bf16[320,256]{1,0:T(8,128)(2,1)} %constant.58.clone.refs_4_) | copy-start | bytes 491524
  70.9 91.6 %copy-start.4 = (bf16[320,256]{1,0:T(8,128)(2,1)S(1)}, bf16[320,256]{1,0:T(8,128)(2,1)}, u32[]{:S(2)}) copy-start(bf16[320,256]{1,0:T(8,128)(2,1)} %constant.59.clone.refs_5_) | copy-start | bytes 491524
  71.0 91.6 %copy-start.5 = (bf16[256,256]{1,0:T(8,128)(2,1)S(1)}, bf16[256,256]{1,0:T(8,128)(2,1)}, u32[]{:S(2)}) copy-start(bf16[256,256]{1,0:T(8,128)(2,1)} %constant.56.clone.refs_2_) | copy-start | bytes 393220
  71.0 91.6 %copy-start.6 = (bf16[256,256]{1,0:T(8,128)(2,1)S(1)}, bf16[256,256]{1,0:T(8,128)(2,1)}, u32[]{:S(2)}) copy-start(bf16[256,256]{1,0:T(8,128)(2,1)} %constant.57.clone.refs_3_) | copy-start | bytes 393220
  74.1 88.4 %copy-start.10 = (f32[3,128,512]{2,1,0:T(8,128)}, f32[3,128,512]{2,1,0:T(8,128)S(1)}, u32[]{:S(2)}) copy-start(f32[3,128,512]{2,1,0:T(8,128)S(1)} %collective-permute-done.refs_7_) | copy-start | bytes 2359300
  74.1 82.8 %collective-permute-start.7 = (f32[1,128,512]{2,1,0:T(8,128)S(1)}, f32[1,128,512]{2,1,0:T(8,128)S(1)}, u32[]{:S(2)}, u32[]{:S(2)}) collective-permute-start(f32[1,128,512]{2,1,0:T(8,128)S(1)} %copy-done.15), channel_id=1, source_target_pairs={{0,4},{4,0},{8,12},{12,8},{16,20},{20,16},{24,28},{28,24},{1,5},{5... | collective-permute-start | bytes 786440 | tf_op jit(solution)/shard_map/ppermute | solution.py:539
  75.2 87.3 %copy-start.11 = (f32[3,128,512]{2,1,0:T(8,128)}, f32[3,128,512]{2,1,0:T(8,128)S(1)}, u32[]{:S(2)}) copy-start(f32[3,128,512]{2,1,0:T(8,128)S(1)} %collective-permute-done.1.refs_8_) | copy-start | bytes 2359300
  75.2 82.7 %collective-permute-start.8 = (f32[1,128,512]{2,1,0:T(8,128)}, f32[1,128,512]{2,1,0:T(8,128)}, u32[]{:S(2)}, u32[]{:S(2)}) collective-permute-start(f32[1,128,512]{2,1,0:T(8,128)} %get-tuple-element.30), channel_id=1, source_target_pairs={{0,8},{4,12},{8,0},{12,4},{16,24},{20,28},{24,16},{28,20},{1,9},{5... | collective-permute-start | bytes 786440 | tf_op jit(solution)/shard_map/ppermute | solution.py:539
  92.4 90.8 %collective-permute-start.9 = (f32[1,128,512]{2,1,0:T(8,128)}, f32[1,128,512]{2,1,0:T(8,128)}, u32[]{:S(2)}, u32[]{:S(2)}) collective-permute-start(f32[1,128,512]{2,1,0:T(8,128)} %get-tuple-element.31), channel_id=1, source_target_pairs={{0,12},{4,8},{8,4},{12,0},{16,28},{20,24},{24,20},{28,16},{1,13},{... | collective-permute-start | bytes 786440 | tf_op jit(solution)/shard_map/ppermute | solution.py:539
  132.9 50.3 %collective-permute-start.10 = (f32[1,128,512]{2,1,0:T(8,128)}, f32[1,128,512]{2,1,0:T(8,128)}, u32[]{:S(2)}, u32[]{:S(2)}) collective-permute-start(f32[1,128,512]{2,1,0:T(8,128)} %get-tuple-element.32), channel_id=1, source_target_pairs={{0,16},{4,20},{8,24},{12,28},{16,0},{20,4},{24,8},{28,12},{1,17},{... | collective-permute-start | bytes 786440 | tf_op jit(solution)/shard_map/ppermute | solution.py:539
  132.9 50.6 %collective-permute-start.11 = (f32[1,128,512]{2,1,0:T(8,128)}, f32[1,128,512]{2,1,0:T(8,128)}, u32[]{:S(2)}, u32[]{:S(2)}) collective-permute-start(f32[1,128,512]{2,1,0:T(8,128)} %get-tuple-element.33), channel_id=1, source_target_pairs={{0,20},{4,16},{8,28},{12,24},{16,4},{20,0},{24,12},{28,8},{1,21},{... | collective-permute-start | bytes 786440 | tf_op jit(solution)/shard_map/ppermute | solution.py:539
  156.9 15.0 %copy-start.12 = (f32[1,128,512]{2,1,0:T(8,128)}, f32[1,128,512]{2,1,0:T(8,128)S(1)}, u32[]{:S(2)}) copy-start(f32[1,128,512]{2,1,0:T(8,128)S(1)} %collective-permute-done.7.refs_7_) | copy-start | bytes 786436
  156.9 26.5 %collective-permute-start.12 = (f32[1,128,512]{2,1,0:T(8,128)}, f32[1,128,512]{2,1,0:T(8,128)}, u32[]{:S(2)}, u32[]{:S(2)}) collective-permute-start(f32[1,128,512]{2,1,0:T(8,128)} %get-tuple-element.34), channel_id=1, source_target_pairs={{0,24},{4,28},{8,16},{12,20},{16,8},{20,12},{24,0},{28,4},{1,25},{... | collective-permute-start | bytes 786440 | tf_op jit(solution)/shard_map/ppermute | solution.py:539
  157.9 25.5 %collective-permute-start.13 = (f32[1,128,512]{2,1,0:T(8,128)}, f32[1,128,512]{2,1,0:T(8,128)}, u32[]{:S(2)}, u32[]{:S(2)}) collective-permute-start(f32[1,128,512]{2,1,0:T(8,128)} %get-tuple-element.35), channel_id=1, source_target_pairs={{0,28},{4,24},{8,20},{12,16},{16,12},{20,8},{24,4},{28,0},{1,29},{... | collective-permute-start | bytes 786440 | tf_op jit(solution)/shard_map/ppermute | solution.py:539
  193.9 5.6 %collective-permute-start.14 = (f32[272,8,128]{2,1,0:T(8,128)}, f32[272,8,128]{2,1,0:T(8,128)S(1)}, u32[]{:S(2)}, u32[]{:S(2)}) collective-permute-start(f32[272,8,128]{2,1,0:T(8,128)} %late_gram.3), channel_id=1, source_target_pairs={{0,1},{1,0},{2,3},{3,2},{4,5},{5,4},{6,7},{7,6},{8,9},{9,8},{10,11... | collective-permute-start | bytes 3342344 | tf_op jit(solution)/shard_map/ppermute | solution.py:560
  199.4 16.4 %copy-start.7 = (f32[272,8,128]{2,1,0:T(8,128)S(1)}, f32[272,8,128]{2,1,0:T(8,128)}, u32[]{:S(2)}) copy-start(f32[272,8,128]{2,1,0:T(8,128)} %late_gram.2) | copy-start | bytes 3342340
  200.7 15.2 %collective-permute-start.15 = (f32[8,17,8,128]{3,2,1,0:T(8,128)S(1)}, f32[8,17,8,128]{3,2,1,0:T(8,128)}, u32[]{:S(2)}, u32[]{:S(2)}) collective-permute-start(f32[8,17,8,128]{3,2,1,0:T(8,128)S(1)} %add_bitcast_fusion), channel_id=1, source_target_pairs={{0,2},{1,3},{2,0},{3,1},{4,6},{5,7},{6,4},{7,5},{8,10},{9,11},{10,... | collective-permute-start | bytes 1671176 | tf_op jit(solution)/shard_map/ppermute | solution.py:560
  270.3 17.8 %all-to-all-start.2 = ((f32[8,128,128]{2,1,0:T(8,128)}), f32[8,128,128]{2,1,0:T(8,128)S(1)}, u32[]{:S(2)}, u32[]{:S(2)}) async-start(f32[8,128,128]{2,1,0:T(8,128)} %bitcast.9), calls=%async_computation.2 | async-start | bytes 1048576 | tf_op jit(solution)/shard_map/all_to_all | solution.py:513
  (1 other events, 1.0 us)

commit v3 on v2

--- a/solution.py
+++ b/solution.py
@@ -87,45 +87,42 @@
     low = low_half((times, LANES))
     me = lax.axis_index("tm")
     for m, x_ref, out_ref in zip(offsets, x_refs, out_refs):
-        rows = x_ref.reshape(times * CHUNK, LANES)
+        blocks = x_ref.shape[1]
+        rows = x_ref.reshape(times * blocks, LANES)
         even = (m ^ me) % 2 == 0
-        for j in range(CHUNK // 2):
-            first = rows[pl.ds(j, times, stride=CHUNK), :] * window
-            second = rows[pl.ds(j + CHUNK // 2, times, stride=CHUNK), :] * window
-            left = jnp.where(low, first, pltpu.roll(second, HALF, 1))
-            right = jnp.where(low, pltpu.roll(first, HALF, 1), second)
-            out_ref[:, j * LANES : (j + 1) * LANES] = jnp.where(even, left, right)
+        for n in range(out_ref.shape[0]):
+            for j in range(CHUNK // 2):
+                b = n * CHUNK + j
+                first = rows[pl.ds(b, times, stride=blocks), :] * window
+                second = rows[pl.ds(b + CHUNK // 2, times, stride=blocks), :] * window
+                left = jnp.where(low, first, pltpu.roll(second, HALF, 1))
+                right = jnp.where(low, pltpu.roll(first, HALF, 1), second)
+                out_ref[n, :, j * LANES : (j + 1) * LANES] = jnp.where(even, left, right)
 
 
 def pack(snapshots, window, chunks, offsets, after):
     times = snapshots.shape[0]
-    width = CHUNK * HALF
+    count, width = len(chunks), CHUNK * HALF
 
     def tile_spec(m):
-        place = lambda n: (0, chunks[0] + n, m // 2 ^ lax.axis_index("tm") // 2)
-        return pl.BlockSpec((times, CHUNK, LANES), place)
+        place = lambda _: (0, chunks[0] // count, m // 2 ^ lax.axis_index("tm") // 2)
+        return pl.BlockSpec((times, CHUNK * count, LANES), place)
 
     return pl.pallas_call(
         functools.partial(pack_kernel, offsets),
-        grid=(len(chunks),),
+        grid=(1,),
         in_specs=[tile_spec(m) for m in offsets]
         + [pl.BlockSpec((times, LANES), lambda _: (lax.axis_index("tm"), 0))]
         + [pl.BlockSpec(memory_space=pl.ANY)] * len(after),
-        out_specs=[pl.BlockSpec((None, times, width), lambda n: (n, 0, 0))] * len(offsets),
-        out_shape=[pltpu.HBM((len(chunks), times, width), F32)] * len(offsets),
-        compiler_params=params(24),
+        out_specs=[pl.BlockSpec((count, times, width), lambda _: (0, 0, 0))] * len(offsets),
+        out_shape=[pltpu.HBM((count, times, width), F32)] * len(offsets),
+        compiler_params=params(40),
         name="pack",
-    )(*in_hbm([snapshots] * len(offsets)), window, *in_hbm(after))
-
-
-def transform_kernel(*refs):
-    odd_high, odd_low, two_high, two_low, four_high, four_low = refs[:6]
-    piece_refs, (out_ref, x_ref, odd_ref, two_ref, four_ref) = refs[6:-5], refs[-5:]
-    me = lax.axis_index("tm")
-    for m, piece_ref in enumerate(piece_refs):
-        times = piece_ref.shape[0]
-        rows = pl.ds(pl.multiple_of((me ^ m) * times, times), times)
-        x_ref[rows, :] = piece_ref[...]
+    )(*in_hbm([snapshots] * len(offsets) + [window, *after]))
+
+
+def transform_columns(tables, x_ref, odd_ref, two_ref, four_ref, out_ref):
+    odd_high, odd_low, two_high, two_low, four_high, four_low = tables
     total, width = x_ref.shape
     quarter, part = total // 4, total // 8
 
@@ -166,10 +163,28 @@
     store(3 * part, product(four_high[...], four_low[...], four_ref))
 
 
+def transform_scratch(total, width):
+    return [
+        pltpu.VMEM((total, width), F32),
+        pltpu.VMEM((2, total // 2, width), BF16),
+        pltpu.VMEM((2, total // 4, width), BF16),
+        pltpu.VMEM((2, total // 4, width), BF16),
+    ]
+
+
+def transform_kernel(*refs):
+    tables, piece_refs, (out_ref, x_ref, *folded) = refs[:6], refs[6:-5], refs[-5:]
+    me = lax.axis_index("tm")
+    for m, piece_ref in enumerate(piece_refs):
+        times = piece_ref.shape[0]
+        rows = pl.ds(pl.multiple_of((me ^ m) * times, times), times)
+        x_ref[rows, :] = piece_ref[...]
+    transform_columns(tables, x_ref, *folded, out_ref)
+
+
 def transform(pieces, tables, slots):
     chunks, times, width = pieces[0].shape
     total = times * len(pieces)
-    quarter = total // 4
     return pl.pallas_call(
         transform_kernel,
         grid=(chunks,),
@@ -177,12 +192,7 @@
         + [pl.BlockSpec((None, times, width), lambda n: (n, 0, 0))] * len(pieces),
         out_specs=pl.BlockSpec((None, slots * CHUNK, LANES), lambda n: (n, 0, 0)),
         out_shape=pltpu.HBM((chunks, slots * CHUNK, LANES), F32),
-        scratch_shapes=[
-            pltpu.VMEM((total, width), F32),
-            pltpu.VMEM((2, 2 * quarter, width), BF16),
-            pltpu.VMEM((2, quarter, width), BF16),
-            pltpu.VMEM((2, quarter, width), BF16),
-        ],
+        scratch_shapes=transform_scratch(total, width),
         compiler_params=params(40),
         name="transform",
     )(*tables, *in_hbm(pieces))
@@ -268,37 +278,27 @@
     )(*in_hbm([spectra]), weights)
 
 
-def late_gram_kernel(tile, half, scale, *refs):
-    sources, w_ref, out_ref = refs[:3], refs[3], refs[4]
-    (early_ref, late_ref, before_ref), sems = refs[5:8], refs[8]
+def copy_tile(source, buffer, sem, base, size, t):
+    there = pl.ds(pl.multiple_of(base + t * size, 8), size)
+    here = pl.ds(pl.multiple_of(t * size, 8), size)
+    if len(source.shape) == 3 and size % CHUNK == 0 and source.shape[1] != CHUNK:
+        return pltpu.make_async_copy(source.at[:, there], buffer.at[:, here], sem)
+    return pltpu.make_async_copy(source.at[there], buffer.at[here], sem)
+
+
+def half_base(half, count):
+    return pl.multiple_of((lax.axis_index("space") % 2 ^ half) * count, GROUP)
+
+
+def late_tiles(tile, weight, early_ref, late_at, before_ref, out_ref, wait):
     chunks = early_ref.shape[0] + 1
-    weight = w_ref[...] * scale
-    count = out_ref.shape[0]
-    base = pl.multiple_of((lax.axis_index("space") % 2 ^ half) * count, GROUP)
-
-    def copies(t):
-        there = pl.ds(pl.multiple_of((base + t * tile) * CHUNK, 8), tile * CHUNK)
-        here = pl.ds(pl.multiple_of(t * tile * CHUNK, 8), tile * CHUNK)
-        there_tile = pl.ds(pl.multiple_of(base + t * tile, 8), tile)
-        here_tile = pl.ds(pl.multiple_of(t * tile, 8), tile)
-        return [
-            pltpu.make_async_copy(sources[0].at[:, there], early_ref.at[:, here], sems.at[0, t]),
-            pltpu.make_async_copy(sources[1].at[:, there], late_ref.at[:, here], sems.at[1, t]),
-            pltpu.make_async_copy(
-                sources[2].at[there_tile], before_ref.at[here_tile], sems.at[2, t]
-            ),
-        ]
-
-    for t in range(count // tile):
-        for copy in copies(t):
-            copy.start()
 
     def step(g, carry):
         parts, before = [], []
         for k in range(GROUP):
-            rows = pl.ds(pl.multiple_of((g * GROUP + k) * CHUNK, CHUNK), CHUNK)
-            parts.append([early_ref[n, rows, :] for n in range(chunks - 1)])
-            parts[-1].append(late_ref[0, rows, :])
+            start = pl.multiple_of((g * GROUP + k) * CHUNK, CHUNK)
+            parts.append([early_ref[n, pl.ds(start, CHUNK), :] for n in range(chunks - 1)])
+            parts[-1].append(late_at(start))
             before.append(before_ref[g * GROUP + k])
         tiles = chunk_tiles(chunks - 1, chunks, weight, parts, before)
         for k in range(GROUP):
@@ -308,25 +308,118 @@
     groups = tile // GROUP
 
     def one_tile(t, carry):
+        wait(t)
+        return lax.fori_loop(0, groups, lambda g, c: step(t * groups + g, c), carry, unroll=True)
+
+    lax.fori_loop(0, out_ref.shape[0] // tile, one_tile, 0)
+
+
+def late_first_kernel(tile, scale, *refs):
+    tables, w_ref, early, before = refs[:6], refs[6], refs[7], refs[8]
+    late_ref, out_ref = refs[-12:-10]
+    piece_refs = refs[9:-12]
+    x_ref, odd_ref, two_ref, four_ref, z_ref, early_ref, before_ref = refs[-10:-3]
+    piece_sems, tile_sems, late_sem = refs[-3:]
+    count = out_ref.shape[0]
+    base = half_base(1, count)
+    me = lax.axis_index("tm")
+    arrivals = []
+    for m, piece_ref in enumerate(piece_refs):
+        times = piece_ref.shape[1]
+        rows = pl.ds(pl.multiple_of((me ^ m) * times, times), times)
+        arrivals.append(pltpu.make_async_copy(piece_ref.at[0], x_ref.at[rows], piece_sems.at[m]))
+        arrivals[-1].start()
+
+    def copies(t):
+        first = copy_tile(early, early_ref, tile_sems.at[0, t], base * CHUNK, tile * CHUNK, t)
+        return first, copy_tile(before, before_ref, tile_sems.at[1, t], base, tile, t)
+
+    for t in range(count // tile):
+        for copy in copies(t):
+            copy.start()
+    for copy in arrivals:
+        copy.wait()
+    transform_columns(tables, x_ref, odd_ref, two_ref, four_ref, z_ref)
+    keep = pltpu.make_async_copy(z_ref, late_ref.at[0], late_sem)
+    keep.start()
+
+    def wait(t):
         for copy in copies(t):
             copy.wait()
-        return lax.fori_loop(0, groups, lambda g, c: step(t * groups + g, c), carry, unroll=True)
-
-    lax.fori_loop(0, count // tile, one_tile, 0)
-
-
-def late_gram(early, late, weights, before, slots, tile, total_points, half):
+
+    late_at = lambda start: z_ref[pl.ds(pl.multiple_of(base * CHUNK + start, 8), CHUNK), :]
+    late_tiles(tile, w_ref[...] * scale, early_ref, late_at, before_ref, out_ref, wait)
+    keep.wait()
+
+
+def late_first(pieces, tables, early, weights, before, slots, tile, total_points):
+    _, times, width = pieces[0].shape
+    total, count = times * len(pieces), slots // 2
+    return pl.pallas_call(
+        functools.partial(late_first_kernel, tile, 1.0 / total_points),
+        in_specs=[pl.BlockSpec(memory_space=pltpu.VMEM)] * (len(tables) + 1)
+        + [pl.BlockSpec(memory_space=pl.ANY)] * (2 + len(pieces)),
+        out_specs=[
+            pl.BlockSpec(memory_space=pl.ANY),
+            pl.BlockSpec(memory_space=pltpu.VMEM),
+        ],
+        out_shape=[
+            pltpu.HBM((1, slots * CHUNK, LANES), F32),
+            pltpu.HBM((count, CHUNK, LANES), F32),
+        ],
+        scratch_shapes=transform_scratch(total, width)
+        + [
+            pltpu.VMEM((slots * CHUNK, LANES), F32),
+            pltpu.VMEM((early.shape[0], count * CHUNK, LANES), F32),
+            pltpu.VMEM((count, CHUNK, LANES), F32),
+            pltpu.SemaphoreType.DMA((len(pieces),)),
+            pltpu.SemaphoreType.DMA((2, count // tile)),
+            pltpu.SemaphoreType.DMA(()),
+        ],
+        compiler_params=params(40),
+        name="late_first",
+    )(*tables, weights, *in_hbm([early, before, *pieces]))
+
+
+def late_second_kernel(tile, scale, *refs):
+    sources, w_ref, out_ref = refs[:3], refs[3], refs[4]
+    buffers, sems = refs[5:8], refs[8]
+    count = out_ref.shape[0]
+    base = half_base(0, count)
+    sizes = (tile * CHUNK, tile * CHUNK, tile)
+
+    def copies(t):
+        bases = (base * CHUNK, base * CHUNK, base)
+        return [
+            copy_tile(sources[n], buffers[n], sems.at[n, t], bases[n], sizes[n], t)
+            for n in range(3)
+        ]
+
+    for t in range(count // tile):
+        for copy in copies(t):
+            copy.start()
+
+    def wait(t):
+        for copy in copies(t):
+            copy.wait()
+
+    late_at = lambda start: buffers[1][0, pl.ds(start, CHUNK), :]
+    late_tiles(tile, w_ref[...] * scale, buffers[0], late_at, buffers[2], out_ref, wait)
+
+
+def late_second(early, late, weights, before, slots, tile, total_points):
     count = slots // 2
-    sizes = [(z.shape[0], count * CHUNK, LANES) for z in (early, late)] + [(count, 8, LANES)]
+    sizes = [(z.shape[0], count * CHUNK, LANES) for z in (early, late)]
+    sizes.append((count, CHUNK, LANES))
     return pl.pallas_call(
-        functools.partial(late_gram_kernel, tile, half, 1.0 / total_points),
+        functools.partial(late_second_kernel, tile, 1.0 / total_points),
         in_specs=[pl.BlockSpec(memory_space=pl.ANY)] * 3
         + [pl.BlockSpec(memory_space=pltpu.VMEM)],
-        out_shape=pltpu.HBM((count, 8, LANES), F32),
+        out_shape=pltpu.HBM((count, CHUNK, LANES), F32),
         scratch_shapes=[pltpu.VMEM(size, F32) for size in sizes]
         + [pltpu.SemaphoreType.DMA((3, count // tile))],
         compiler_params=params(24),
-        name="late_gram",
+        name="late_second",
     )(*in_hbm([early, late, before]), weights)
 
 
@@ -523,7 +616,7 @@
     slots = per_device * devices
     tile = slots // 4
     tables = transform_tables(total_times, slots)
-    window = window_table(total_times)
+    window = jnp.asarray(window_table(total_times))
 
     here = lax.axis_index("tm") * HALF
     weights = lax.dynamic_slice(quad_weights, (here,), (HALF,))
@@ -543,7 +636,9 @@
     first = [*range(half, half + quarter), *range(quarter)]
     second = [*range(half + quarter, tm_size), *range(quarter, half)]
     group = range(chunks - 1)
-    sent, pieces = send(group, first, [])
+    sent, pieces = send(group, first[:1], [])
+    sent, more = send(group, first[1:], [sent[half]])
+    pieces |= more
     pieces |= send(group, second, [sent[0]])[1]
     group = range(chunks - 1, chunks)
     sent, last = send(group, first, [pieces[half]])
@@ -551,7 +646,9 @@
     ordered = lambda pieces: [pieces[m] for m in range(tm_size)]
     early = transform(ordered(pieces), tables, slots)
     matrices = early_gram(early, weights, slots, tile, total_points)
-    late = transform(ordered(last), tables, slots)
+    late, given = late_first(
+        ordered(last), tables, early, weights, matrices, slots, tile, total_points
+    )
 
     space = lax.axis_index("space")
 
@@ -559,18 +656,22 @@
         pairs = [(i, i ^ (1 << level)) for i in range(space_size)]
         return lax.ppermute(value, "space", pairs)
 
-    arriving = swap(late_gram(early, late, weights, matrices, slots, tile, total_points, 1), 0)
-    part = late_gram(early, late, weights, matrices, slots, tile, total_points, 0)
+    arriving = swap(given, 0)
+    part = late_second(early, late, weights, matrices, slots, tile, total_points)
     levels = space_size.bit_length() - 1
     shape = (*[2] * (levels - 1), tm_size, per_device, *part.shape[1:])
     part, arriving = part.reshape(shape), arriving.reshape(shape)
-    for level in range(1, levels):
-        bit = space >> level & 1
-        pick = lambda value, i: lax.dynamic_index_in_dim(value, i, 0, keepdims=False)
-        given = pick(part, 1 - bit) + pick(arriving, 1 - bit)
-        part = pick(part, bit) + pick(arriving, bit)
-        arriving = swap(given, level)
-    part = exchange(part + arriving, "tm").sum(axis=0)
+    bit = space // 2
+    pick = lambda value, i: lax.dynamic_index_in_dim(value, i, 0, keepdims=False)
+    cut = 2 * per_device // 3
+    given = pick(part, 1 - bit)[:, :cut] + pick(arriving, 1 - bit)[:, :cut]
+    kept = pick(part, bit)[:, :cut] + pick(arriving, bit)[:, :cut]
+    given = swap(given, 1)
+    rest = part[:, :, cut:] + arriving[:, :, cut:]
+    rest = lax.all_to_all(rest, "tm", 1, 1, tiled=True).sum(axis=1)
+    rest = pick(rest, bit) + swap(pick(rest, 1 - bit), 1)
+    part = exchange(kept + given, "tm").sum(axis=0)
+    part = jnp.concatenate([part, rest], axis=0)
 
     vectors = power(part.transpose(2, 1, 0), blocks).T
     vectors = jnp.pad(vectors, ((0, 0), (0, LANES - vectors.shape[1])))
@@ -591,7 +692,7 @@
     tm_size, space_size = mesh_shape["tm"], mesh_shape["space"]
     return (
         points == space_size * tm_size * HALF
-        and tm_size == 8
+        and (tm_size, space_size) == (8, 4)
         and space_size & (space_size - 1) == 0
         and times % (tm_size * 8) == 0
         and blocks % CHUNK == 0

time: 290 us -> 282 us (0.972)
  blocking collectives: 45.5 us -> 16.6 us
  starting transfers between devices: 65.9 us -> 80.9 us
  waiting for transfers between devices: 109 us -> 113 us
    all_to_all x2 -> x1, blocking collectives: 45.5 us -> 16.6 us  [exchange(): return lax.all_to_all(value, axes, 0, 0, tiled=True)]
    all_to_all x0 -> x1, starting transfers between devices: none -> 13.1 us  [body(): rest = lax.all_to_all(rest, 'tm', 1, 1, tiled=True).sum(axis=1)]
    all_to_all x1 -> x2, waiting for transfers between devices: 13.7 us -> 20 us  [exchange(): return lax.all_to_all(value, axes, 0, 0, tiled=True)]
    all_to_all x1 -> x2, starting transfers between devices: 3.51 us -> 8.31 us  [exchange(): return lax.all_to_all(value, axes, 0, 0, tiled=True)]
    pallas_call x2 -> x1, Pallas kernels: 14.3 us -> 9.49 us  [transform(): pl.pallas_call(transform_kernel, grid=(chunks,), in_specs=[pl.BlockSpec(t...]
    ppermute x14, starting transfers between devices: 60.7 us -> 56.4 us  [send(): flying[m] = lax.ppermute(part, 'tm', pairs) if m else part]
    pallas_call x6 -> x7, Pallas kernels: 29.2 us -> 33 us  [the longest x5 19.2 us: pack(): pl.pallas_call(functools.partial(pack_kernel, offsets), grid=(1,), in_spe...]
    ppermute x2 -> x3, waiting for transfers between devices: 13.6 us -> 11.3 us  [swap(): return lax.ppermute(value, 'space', pairs)]
  transfers between devices with their start and end apart: 17 -> 20, of which waited for: 5 -> 9; matrix products, arithmetic and copies ran while one was open for 0% -> 1% of each run, Pallas kernels for 13% -> 15%
where the time goes in v3:
time: 282 us; the launch traced here: 281 us
  waiting for transfers between devices  113 us (40%)
  starting transfers between devices  80.9 us (29%)
  Pallas kernels  61.8 us (22%)
  blocking collectives  16.6 us (6%)
  local copies, waits for them, and re-layouts  5.02 us (2%)
    ppermute x14, waiting for transfers between devices, send(): flying[m] = lax.ppermute(part, 'tm', pairs) if m else part  81.2 us
    ppermute x14, starting transfers between devices, send(): flying[m] = lax.ppermute(part, 'tm', pairs) if m else part  56.4 us
    all_to_all x2, waiting for transfers between devices, exchange(): return lax.all_to_all(value, axes, 0, 0, tiled=True)  20 us
    pallas_call x5, Pallas kernels, pack(): pl.pallas_call(functools.partial(pack_kernel, offsets), grid=(1,), in_spe...  19.2 us
    all_to_all x1, blocking collectives, exchange(): return lax.all_to_all(value, axes, 0, 0, tiled=True)  16.6 us
    all_to_all x1, starting transfers between devices, body(): rest = lax.all_to_all(rest, 'tm', 1, 1, tiled=True).sum(axis=1)  13.1 us
    ppermute x3, waiting for transfers between devices, swap(): return lax.ppermute(value, 'space', pairs)  11.3 us
    pallas_call x1, Pallas kernels, early_gram(): pl.pallas_call(functools.partial(early_gram_kernel, tile, chunks, 1.0 / t...  11.3 us
  transfers between devices with their start and end apart: 20, of which 9 were waited for; matrix products, arithmetic and copies ran while one was open for 1% of the time, Pallas kernels for 15%

profile of v3, /device:TPU:0, one launch (start us, length us, event | category | flops | bytes accessed | tf_op | source)
XLA Modules:
  0.0 281.5 jit_solution(11242275133097345933)
XLA Ops:
  0.6 2.9 %pack.5.refs_4_ = f32[3,128,512]{2,1,0:T(8,128)} custom-call(f32[128,32,512]{2,1,0:T(8,128)} %refs_3_.8, f32[1024,128]{1,0:T(8,128)} %constant.71.clone.refs_1_.refs_3_.refs_4_), custom_call_target="tpu_custom_call" | custom-call | tf_op jit(solution)/shard_map/pack/pallas_call | solution.py:111
  3.5 4.0 %collective-permute-start.3 = (f32[3,128,512]{2,1,0:T(8,128)}, f32[3,128,512]{2,1,0:T(8,128)S(1)}, u32[]{:S(2)}, u32[]{:S(2)}) collective-permute-start(f32[3,128,512]{2,1,0:T(8,128)} %pack.5.refs_4_), channel_id=1, source_target_pairs={{0,16},{4,20},{8,24},{12,28},{16,0},{20,4},{24,8},{28,12},{1,17},{... | collective-permute-start | bytes 2359304 | tf_op jit(solution)/shard_map/ppermute | solution.py:632
  7.5 4.7 %pack.6 = (f32[3,128,512]{2,1,0:T(8,128)}, f32[3,128,512]{2,1,0:T(8,128)}, f32[3,128,512]{2,1,0:T(8,128)}) custom-call(f32[128,32,512]{2,1,0:T(8,128)} %refs_3_.8, f32[128,32,512]{2,1,0:T(8,128)} %refs_3_.8, f32[128,32,512]{2,1,0:T(8,128)} %refs_3_.8, f32[1024,128]{1,0:T(8,128)} %constant.71.clone.refs_1_.refs_3_.refs_4_, f32[3,128,512]{2,1,0:T(8,128)} %pack.5.refs_4_), custom_call_target="tpu_custom_call" | custom-call | tf_op jit(solution)/shard_map/pack/pallas_call | solution.py:111
  12.2 5.7 %pack.7 = (f32[3,128,512]{2,1,0:T(8,128)}, f32[3,128,512]{2,1,0:T(8,128)}, f32[3,128,512]{2,1,0:T(8,128)}, f32[3,128,512]{2,1,0:T(8,128)}) custom-call(f32[128,32,512]{2,1,0:T(8,128)} %refs_3_.8, f32[128,32,512]{2,1,0:T(8,128)} %refs_3_.8, f32[128,32,512]{2,1,0:T(8,128)} %refs_3_.8, f32[128,32,512]{2,1,0:T(8,128)} %refs_3_.8, ...), custom_call_target="tpu_custom_call" | custom-call | tf_op jit(solution)/shard_map/pack/pallas_call | solution.py:111
  19.3 1.5 collective-permute-start
  21.1 1.7 collective-permute-start.2
  22.8 37.0 %collective-permute-done.3.refs_10_.refs_5_ = f32[3,128,512]{2,1,0:T(8,128)S(1)} collective-permute-done((f32[3,128,512]{2,1,0:T(8,128)}, f32[3,128,512]{2,1,0:T(8,128)S(1)}, u32[]{:S(2)}, u32[]{:S(2)}) %collective-permute-start.3) | collective-permute-done | bytes 786464 | tf_op jit(solution)/shard_map/ppermute | solution.py:632
  60.8 2.9 %collective-permute-start.6 = (f32[3,128,512]{2,1,0:T(8,128)}, f32[3,128,512]{2,1,0:T(8,128)}, u32[]{:S(2)}, u32[]{:S(2)}) collective-permute-start(f32[3,128,512]{2,1,0:T(8,128)} %get-tuple-element.27), channel_id=1, source_target_pairs={{0,28},{4,24},{8,20},{12,16},{16,12},{20,8},{24,4},{28,0},{1,29},{... | collective-permute-start | bytes 2359304 | tf_op jit(solution)/shard_map/ppermute | solution.py:632
  63.7 2.9 %pack.8 = (f32[1,128,512]{2,1,0:T(8,128)}, f32[1,128,512]{2,1,0:T(8,128)}, f32[1,128,512]{2,1,0:T(8,128)}, f32[1,128,512]{2,1,0:T(8,128)}) custom-call(f32[128,32,512]{2,1,0:T(8,128)} %refs_3_.8, f32[128,32,512]{2,1,0:T(8,128)} %refs_3_.8, f32[128,32,512]{2,1,0:T(8,128)} %refs_3_.8, f32[128,32,512]{2,1,0:T(8,128)} %refs_3_.8, ...), custom_call_target="tpu_custom_call" | custom-call | tf_op jit(solution)/shard_map/pack/pallas_call | solution.py:111
  66.7 3.0 %pack.9 = (f32[1,128,512]{2,1,0:T(8,128)}, f32[1,128,512]{2,1,0:T(8,128)}, f32[1,128,512]{2,1,0:T(8,128)}, f32[1,128,512]{2,1,0:T(8,128)}) custom-call(f32[128,32,512]{2,1,0:T(8,128)} %refs_3_.8, f32[128,32,512]{2,1,0:T(8,128)} %refs_3_.8, f32[128,32,512]{2,1,0:T(8,128)} %refs_3_.8, f32[128,32,512]{2,1,0:T(8,128)} %refs_3_.8, ...), custom_call_target="tpu_custom_call" | custom-call | tf_op jit(solution)/shard_map/pack/pallas_call | solution.py:111
  70.8 3.4 %collective-permute-done.1.refs_8_ = f32[3,128,512]{2,1,0:T(8,128)} collective-permute-done((f32[3,128,512]{2,1,0:T(8,128)}, f32[3,128,512]{2,1,0:T(8,128)}, u32[]{:S(2)}, u32[]{:S(2)}) %collective-permute-start.1) | collective-permute-done | bytes 786464 | tf_op jit(solution)/shard_map/ppermute | solution.py:632
  74.2 13.8 %collective-permute-start.8 = (f32[1,128,512]{2,1,0:T(8,128)}, f32[1,128,512]{2,1,0:T(8,128)S(1)}, u32[]{:S(2)}, u32[]{:S(2)}) collective-permute-start(f32[1,128,512]{2,1,0:T(8,128)} %get-tuple-element.30), channel_id=1, source_target_pairs={{0,8},{4,12},{8,0},{12,4},{16,24},{20,28},{24,16},{28,20},{1,9},{5... | collective-permute-start | bytes 786440 | tf_op jit(solution)/shard_map/ppermute | solution.py:632
  88.0 3.0 %collective-permute-done.2.refs_9_ = f32[3,128,512]{2,1,0:T(8,128)} collective-permute-done((f32[3,128,512]{2,1,0:T(8,128)}, f32[3,128,512]{2,1,0:T(8,128)}, u32[]{:S(2)}, u32[]{:S(2)}) %collective-permute-start.2) | collective-permute-done | bytes 786464 | tf_op jit(solution)/shard_map/ppermute | solution.py:632
  91.0 37.7 %collective-permute-done.4.refs_11_ = f32[3,128,512]{2,1,0:T(8,128)} collective-permute-done((f32[3,128,512]{2,1,0:T(8,128)S(1)}, f32[3,128,512]{2,1,0:T(8,128)}, u32[]{:S(2)}, u32[]{:S(2)}) %collective-permute-start.4) | collective-permute-done | bytes 786464 | tf_op jit(solution)/shard_map/ppermute | solution.py:632
  128.7 24.0 %collective-permute-start.11 = (f32[1,128,512]{2,1,0:T(8,128)}, f32[1,128,512]{2,1,0:T(8,128)S(1)}, u32[]{:S(2)}, u32[]{:S(2)}) collective-permute-start(f32[1,128,512]{2,1,0:T(8,128)} %get-tuple-element.33), channel_id=1, source_target_pairs={{0,20},{4,16},{8,28},{12,24},{16,4},{20,0},{24,12},{28,8},{1,21},{... | collective-permute-start | bytes 786440 | tf_op jit(solution)/shard_map/ppermute | solution.py:632
  153.7 3.8 %collective-permute-start.13 = (f32[1,128,512]{2,1,0:T(8,128)}, f32[1,128,512]{2,1,0:T(8,128)S(1)}, u32[]{:S(2)}, u32[]{:S(2)}) collective-permute-start(f32[1,128,512]{2,1,0:T(8,128)} %get-tuple-element.35), channel_id=1, source_target_pairs={{0,28},{4,24},{8,20},{12,16},{16,12},{20,8},{24,4},{28,0},{1,29},{... | collective-permute-start | bytes 786440 | tf_op jit(solution)/shard_map/ppermute | solution.py:632
  158.4 9.5 %transform.1.z_ref.refs_7_.refs_0_ = f32[3,4352,128]{2,1,0:T(8,128)} custom-call(bf16[512,512]{1,0:T(8,128)(2,1)S(1)} %copy-done, bf16[512,512]{1,0:T(8,128)(2,1)S(1)} %copy-done.1, bf16[256,256]{1,0:T(8,128)(2,1)S(1)} %copy-done.4, bf16[256,256]{1,0:T(8,128)(2,1)S(1)} %copy-done.5, bf16[320,256]{1,0:T(8,128)(2,1)S(1)} %copy-done.2, ...), custom_call_target="tpu_custom_call" | custom-call | tf_op jit(solution)/shard_map/transform/pallas_call | solution.py:188
  167.9 11.3 %early_gram.1.refs_8_.refs_2_ = f32[544,8,128]{2,1,0:T(8,128)} custom-call(f32[3,4352,128]{2,1,0:T(8,128)} %transform.1.z_ref.refs_7_.refs_0_, f32[1,128]{1,0:T(1,128)S(1)} %maximum_bitcast_fusion.w_ref.refs_6_.refs_3_), custom_call_target="tpu_custom_call" | custom-call | tf_op jit(solution)/shard_map/early_gram/pallas_call | solution.py:267
  180.8 8.3 %late_first.1 = (f32[1,4352,128]{2,1,0:T(8,128)}, f32[272,8,128]{2,1,0:T(8,128)}) custom-call(bf16[512,512]{1,0:T(8,128)(2,1)S(1)} %copy-done, bf16[512,512]{1,0:T(8,128)(2,1)S(1)} %copy-done.1, bf16[256,256]{1,0:T(8,128)(2,1)S(1)} %copy-done.4, bf16[256,256]{1,0:T(8,128)(2,1)S(1)} %copy-done.5, bf16[320,256]{1,0:T(8,128)(2,1)S(1)} %copy-done.2, ...), custom_call_target="tpu_custom_call" | custom-call | tf_op jit(solution)/shard_map/late_first/pallas_call | solution.py:358
  189.2 5.5 %late_second.1 = f32[272,8,128]{2,1,0:T(8,128)} custom-call(f32[3,4352,128]{2,1,0:T(8,128)} %transform.1.z_ref.refs_7_.refs_0_, f32[1,4352,128]{2,1,0:T(8,128)} %get-tuple-element.36.refs_1_, f32[544,8,128]{2,1,0:T(8,128)} %early_gram.1.refs_8_.refs_2_, f32[1,128]{1,0:T(1,128)S(1)} %maximum_bitcast_fusion.w_ref.refs_6_.refs_3_), custom_call_target="tpu_custom_call" | custom-call | tf_op jit(solution)/shard_map/late_second/pallas_call | solution.py:414
  196.1 1.8 copy_add_fusion
  197.9 13.1 %all-to-all-start.1 = ((f32[2,8,6,8,128]{4,3,2,0,1:T(8,128)}), f32[2,8,6,8,128]{4,3,2,0,1:T(8,128)S(1)}, u32[]{:S(2)}, u32[]{:S(2)}) async-start(f32[2,8,6,8,128]{4,3,2,0,1:T(8,128)} %copy_add_fusion), calls=%async_computation.1 | async-start | bytes 786432 | tf_op jit(solution)/shard_map/all_to_all | solution.py:671
  211.0 1.6 collective-permute-start.15
  212.6 9.0 %collective-permute-done.15 = f32[8,11,8,128]{3,2,1,0:T(8,128)S(1)} collective-permute-done((f32[8,11,8,128]{3,2,1,0:T(8,128)S(1)}, f32[8,11,8,128]{3,2,1,0:T(8,128)S(1)}, u32[]{:S(2)}, u32[]{:S(2)}) %collective-permute-start.15) | collective-permute-done | bytes 360480 | tf_op jit(solution)/shard_map/ppermute | solution.py:657
  223.3 4.8 %all-to-all-start = ((f32[8,11,8,128]{3,2,1,0:T(8,128)}), f32[8,11,8,128]{3,2,1,0:T(8,128)S(1)}, u32[]{:S(2)}, u32[]{:S(2)}) async-start(f32[8,11,8,128]{3,2,1,0:T(8,128)} %fusion), calls=%async_computation | async-start | bytes 720896 | tf_op jit(solution)/shard_map/all_to_all | solution.py:606
  228.1 1.6 collective-permute-start.16
  229.7 2.3 collective-permute-done.16
  232.0 6.2 %all-to-all-done = f32[8,11,8,128]{3,2,1,0:T(8,128)S(1)} async-done(((f32[8,11,8,128]{3,2,1,0:T(8,128)}), f32[8,11,8,128]{3,2,1,0:T(8,128)S(1)}, u32[]{:S(2)}, u32[]{:S(2)}) %all-to-all-start) | async-done | bytes 360480 | tf_op jit(solution)/shard_map/all_to_all | solution.py:606
  240.0 16.6 %all_to_all.20 = f32[32,17,128]{2,1,0:T(8,128)S(1)} all-to-all(f32[32,17,128]{2,1,0:T(8,128)S(1)} %broadcast_in_dim.10), channel_id=1, replica_groups=mesh['tm'=8,'space'=4] {'tm','space'}, dimensions={0} | all-to-all | bytes 557056 | tf_op jit(solution)/shard_map/all_to_all | solution.py:606
  256.9 5.8 %modes.1 = (f32[1024,128]{1,0:T(8,128)}, f32[1024,128]{1,0:T(8,128)S(1)}) custom-call(f32[3,4352,128]{2,1,0:T(8,128)} %transform.1.z_ref.refs_7_.refs_0_, f32[1,4352,128]{2,1,0:T(8,128)} %get-tuple-element.36.refs_1_, f32[544,128]{1,0:T(8,128)S(1)} %reshape.28.refs_2_), custom_call_target="tpu_custom_call" | custom-call | tf_op jit(solution)/shard_map/modes/pallas_call | solution.py:567
  262.6 3.5 %all-to-all-start.3 = ((f32[8,128,128]{2,1,0:T(8,128)}), f32[8,128,128]{2,1,0:T(8,128)S(1)}, u32[]{:S(2)}, u32[]{:S(2)}) async-start(f32[8,128,128]{2,1,0:T(8,128)} %bitcast.13), calls=%async_computation.3 | async-start | bytes 1048576 | tf_op jit(solution)/shard_map/all_to_all | solution.py:606
  266.8 13.7 %all-to-all-done.3.x_ref = f32[8,128,128]{2,1,0:T(8,128)S(1)} async-done(((f32[8,128,128]{2,1,0:T(8,128)}), f32[8,128,128]{2,1,0:T(8,128)S(1)}, u32[]{:S(2)}, u32[]{:S(2)}) %all-to-all-start.3) | async-done | bytes 524320 | tf_op jit(solution)/shard_map/all_to_all | solution.py:606
  (78 shorter events, 13.9 us)
Async XLA Ops:
  3.5 56.4 %collective-permute-start.3 = (f32[3,128,512]{2,1,0:T(8,128)}, f32[3,128,512]{2,1,0:T(8,128)S(1)}, u32[]{:S(2)}, u32[]{:S(2)}) collective-permute-start(f32[3,128,512]{2,1,0:T(8,128)} %pack.5.refs_4_), channel_id=1, source_target_pairs={{0,16},{4,20},{8,24},{12,28},{16,0},{20,4},{24,8},{28,12},{1,17},{... | collective-permute-start | bytes 2359304 | tf_op jit(solution)/shard_map/ppermute | solution.py:632
  12.2 7.1 %copy-start.16 = (f32[3,128,512]{2,1,0:T(8,128)S(1)}, f32[3,128,512]{2,1,0:T(8,128)}, u32[]{:S(2)}) copy-start(f32[3,128,512]{2,1,0:T(8,128)} %get-tuple-element.22) | copy-start | bytes 2359300
  12.2 47.6 %copy-start.15 = (f32[3,128,512]{2,1,0:T(8,128)S(1)}, f32[3,128,512]{2,1,0:T(8,128)}, u32[]{:S(2)}) copy-start(f32[3,128,512]{2,1,0:T(8,128)} %get-tuple-element.25) | copy-start | bytes 2359300
  18.0 42.9 %collective-permute-start.5 = (f32[3,128,512]{2,1,0:T(8,128)}, f32[3,128,512]{2,1,0:T(8,128)S(1)}, u32[]{:S(2)}, u32[]{:S(2)}) collective-permute-start(f32[3,128,512]{2,1,0:T(8,128)} %get-tuple-element.26), channel_id=1, source_target_pairs={{0,24},{4,28},{8,16},{12,20},{16,8},{20,12},{24,0},{28,4},{1,25},{... | collective-permute-start | bytes 2359304 | tf_op jit(solution)/shard_map/ppermute | solution.py:632
  19.3 50.4 %collective-permute-start = (f32[3,128,512]{2,1,0:T(8,128)S(1)}, f32[3,128,512]{2,1,0:T(8,128)}, u32[]{:S(2)}, u32[]{:S(2)}) collective-permute-start(f32[3,128,512]{2,1,0:T(8,128)S(1)} %copy-done.16), channel_id=1, source_target_pairs={{0,4},{4,0},{8,12},{12,8},{16,20},{20,16},{24,28},{28,24},{1,5},{5... | collective-permute-start | bytes 2359304 | tf_op jit(solution)/shard_map/ppermute | solution.py:632
  20.8 53.3 %collective-permute-start.1 = (f32[3,128,512]{2,1,0:T(8,128)}, f32[3,128,512]{2,1,0:T(8,128)}, u32[]{:S(2)}, u32[]{:S(2)}) collective-permute-start(f32[3,128,512]{2,1,0:T(8,128)} %get-tuple-element.23), channel_id=1, source_target_pairs={{0,8},{4,12},{8,0},{12,4},{16,24},{20,28},{24,16},{28,20},{1,9},{5... | collective-permute-start | bytes 2359304 | tf_op jit(solution)/shard_map/ppermute | solution.py:632
  21.1 69.9 %collective-permute-start.2 = (f32[3,128,512]{2,1,0:T(8,128)}, f32[3,128,512]{2,1,0:T(8,128)}, u32[]{:S(2)}, u32[]{:S(2)}) collective-permute-start(f32[3,128,512]{2,1,0:T(8,128)} %get-tuple-element.24), channel_id=1, source_target_pairs={{0,12},{4,8},{8,4},{12,0},{16,28},{20,24},{24,20},{28,16},{1,13},{... | collective-permute-start | bytes 2359304 | tf_op jit(solution)/shard_map/ppermute | solution.py:632
  59.9 3.9 %copy-start.6 = (f32[3,128,512]{2,1,0:T(8,128)}, f32[3,128,512]{2,1,0:T(8,128)S(1)}, u32[]{:S(2)}) copy-start(f32[3,128,512]{2,1,0:T(8,128)S(1)} %collective-permute-done.3.refs_10_.refs_5_) | copy-start | bytes 2359300
  59.9 68.9 %collective-permute-start.4 = (f32[3,128,512]{2,1,0:T(8,128)S(1)}, f32[3,128,512]{2,1,0:T(8,128)}, u32[]{:S(2)}, u32[]{:S(2)}) collective-permute-start(f32[3,128,512]{2,1,0:T(8,128)S(1)} %copy-done.15), channel_id=1, source_target_pairs={{0,20},{4,16},{8,28},{12,24},{16,4},{20,0},{24,12},{28,8},{1,21},{... | collective-permute-start | bytes 2359304 | tf_op jit(solution)/shard_map/ppermute | solution.py:632
  60.8 5.8 %copy-start.7 = (f32[3,128,512]{2,1,0:T(8,128)}, f32[3,128,512]{2,1,0:T(8,128)S(1)}, u32[]{:S(2)}) copy-start(f32[3,128,512]{2,1,0:T(8,128)S(1)} %collective-permute-done.5.refs_12_.refs_6_) | copy-start | bytes 2359300
  60.8 67.9 %collective-permute-start.6 = (f32[3,128,512]{2,1,0:T(8,128)}, f32[3,128,512]{2,1,0:T(8,128)}, u32[]{:S(2)}, u32[]{:S(2)}) collective-permute-start(f32[3,128,512]{2,1,0:T(8,128)} %get-tuple-element.27), channel_id=1, source_target_pairs={{0,28},{4,24},{8,20},{12,16},{16,12},{20,8},{24,4},{28,0},{1,29},{... | collective-permute-start | bytes 2359304 | tf_op jit(solution)/shard_map/ppermute | solution.py:632
  66.6 91.7 %copy-start = (bf16[512,512]{1,0:T(8,128)(2,1)S(1)}, bf16[512,512]{1,0:T(8,128)(2,1)}, u32[]{:S(2)}) copy-start(bf16[512,512]{1,0:T(8,128)(2,1)} %constant.72.clone.refs_0_) | copy-start | bytes 1572868
  66.6 91.7 %copy-start.1 = (bf16[512,512]{1,0:T(8,128)(2,1)S(1)}, bf16[512,512]{1,0:T(8,128)(2,1)}, u32[]{:S(2)}) copy-start(bf16[512,512]{1,0:T(8,128)(2,1)} %constant.73.clone.refs_1_) | copy-start | bytes 1572868
  66.6 91.7 %copy-start.2 = (bf16[320,256]{1,0:T(8,128)(2,1)S(1)}, bf16[320,256]{1,0:T(8,128)(2,1)}, u32[]{:S(2)}) copy-start(bf16[320,256]{1,0:T(8,128)(2,1)} %constant.76.clone.refs_4_) | copy-start | bytes 491524
  66.7 91.7 %copy-start.3 = (bf16[320,256]{1,0:T(8,128)(2,1)S(1)}, bf16[320,256]{1,0:T(8,128)(2,1)}, u32[]{:S(2)}) copy-start(bf16[320,256]{1,0:T(8,128)(2,1)} %constant.77.clone.refs_5_) | copy-start | bytes 491524
  66.7 91.7 %copy-start.4 = (bf16[256,256]{1,0:T(8,128)(2,1)S(1)}, bf16[256,256]{1,0:T(8,128)(2,1)}, u32[]{:S(2)}) copy-start(bf16[256,256]{1,0:T(8,128)(2,1)} %constant.74.clone.refs_2_) | copy-start | bytes 393220
  66.7 91.7 %copy-start.5 = (bf16[256,256]{1,0:T(8,128)(2,1)S(1)}, bf16[256,256]{1,0:T(8,128)(2,1)}, u32[]{:S(2)}) copy-start(bf16[256,256]{1,0:T(8,128)(2,1)} %constant.75.clone.refs_3_) | copy-start | bytes 393220
  69.7 83.0 %collective-permute-start.7 = (f32[1,128,512]{2,1,0:T(8,128)S(1)}, f32[1,128,512]{2,1,0:T(8,128)S(1)}, u32[]{:S(2)}, u32[]{:S(2)}) collective-permute-start(f32[1,128,512]{2,1,0:T(8,128)S(1)} %copy-done.17), channel_id=1, source_target_pairs={{0,4},{4,0},{8,12},{12,8},{16,20},{20,16},{24,28},{28,24},{1,5},{5... | collective-permute-start | bytes 786440 | tf_op jit(solution)/shard_map/ppermute | solution.py:632
  74.2 79.5 %collective-permute-start.8 = (f32[1,128,512]{2,1,0:T(8,128)}, f32[1,128,512]{2,1,0:T(8,128)S(1)}, u32[]{:S(2)}, u32[]{:S(2)}) collective-permute-start(f32[1,128,512]{2,1,0:T(8,128)} %get-tuple-element.30), channel_id=1, source_target_pairs={{0,8},{4,12},{8,0},{12,4},{16,24},{20,28},{24,16},{28,20},{1,9},{5... | collective-permute-start | bytes 786440 | tf_op jit(solution)/shard_map/ppermute | solution.py:632
  91.0 88.1 %collective-permute-start.9 = (f32[1,128,512]{2,1,0:T(8,128)}, f32[1,128,512]{2,1,0:T(8,128)S(1)}, u32[]{:S(2)}, u32[]{:S(2)}) collective-permute-start(f32[1,128,512]{2,1,0:T(8,128)} %get-tuple-element.31), channel_id=1, source_target_pairs={{0,12},{4,8},{8,4},{12,0},{16,28},{20,24},{24,20},{28,16},{1,13},{... | collective-permute-start | bytes 786440 | tf_op jit(solution)/shard_map/ppermute | solution.py:632
  128.7 50.4 %collective-permute-start.10 = (f32[1,128,512]{2,1,0:T(8,128)}, f32[1,128,512]{2,1,0:T(8,128)S(1)}, u32[]{:S(2)}, u32[]{:S(2)}) collective-permute-start(f32[1,128,512]{2,1,0:T(8,128)} %get-tuple-element.32), channel_id=1, source_target_pairs={{0,16},{4,20},{8,24},{12,28},{16,0},{20,4},{24,8},{28,12},{1,17},{... | collective-permute-start | bytes 786440 | tf_op jit(solution)/shard_map/ppermute | solution.py:632
  128.7 50.5 %collective-permute-start.11 = (f32[1,128,512]{2,1,0:T(8,128)}, f32[1,128,512]{2,1,0:T(8,128)S(1)}, u32[]{:S(2)}, u32[]{:S(2)}) collective-permute-start(f32[1,128,512]{2,1,0:T(8,128)} %get-tuple-element.33), channel_id=1, source_target_pairs={{0,20},{4,16},{8,28},{12,24},{16,4},{20,0},{24,12},{28,8},{1,21},{... | collective-permute-start | bytes 786440 | tf_op jit(solution)/shard_map/ppermute | solution.py:632
  152.7 15.1 %copy-start.8 = (f32[1,128,512]{2,1,0:T(8,128)}, f32[1,128,512]{2,1,0:T(8,128)S(1)}, u32[]{:S(2)}) copy-start(f32[1,128,512]{2,1,0:T(8,128)S(1)} %collective-permute-done.7.refs_10_) | copy-start | bytes 786436
  152.7 26.5 %collective-permute-start.12 = (f32[1,128,512]{2,1,0:T(8,128)}, f32[1,128,512]{2,1,0:T(8,128)S(1)}, u32[]{:S(2)}, u32[]{:S(2)}) collective-permute-start(f32[1,128,512]{2,1,0:T(8,128)} %get-tuple-element.34), channel_id=1, source_target_pairs={{0,24},{4,28},{8,16},{12,20},{16,8},{20,12},{24,0},{28,4},{1,25},{... | collective-permute-start | bytes 786440 | tf_op jit(solution)/shard_map/ppermute | solution.py:632
  153.7 14.1 %copy-start.9 = (f32[1,128,512]{2,1,0:T(8,128)}, f32[1,128,512]{2,1,0:T(8,128)S(1)}, u32[]{:S(2)}) copy-start(f32[1,128,512]{2,1,0:T(8,128)S(1)} %collective-permute-done.8.refs_11_) | copy-start | bytes 786436
  153.7 25.5 %collective-permute-start.13 = (f32[1,128,512]{2,1,0:T(8,128)}, f32[1,128,512]{2,1,0:T(8,128)S(1)}, u32[]{:S(2)}, u32[]{:S(2)}) collective-permute-start(f32[1,128,512]{2,1,0:T(8,128)} %get-tuple-element.35), channel_id=1, source_target_pairs={{0,28},{4,24},{8,20},{12,16},{16,12},{20,8},{24,4},{28,0},{1,29},{... | collective-permute-start | bytes 786440 | tf_op jit(solution)/shard_map/ppermute | solution.py:632
  189.1 6.9 %collective-permute-start.14 = (f32[272,8,128]{2,1,0:T(8,128)}, f32[272,8,128]{2,1,0:T(8,128)S(1)}, u32[]{:S(2)}, u32[]{:S(2)}) collective-permute-start(f32[272,8,128]{2,1,0:T(8,128)} %get-tuple-element.37), channel_id=1, source_target_pairs={{0,1},{1,0},{2,3},{3,2},{4,5},{5,4},{6,7},{7,6},{8,9},{9,8},{10,11... | collective-permute-start | bytes 3342344 | tf_op jit(solution)/shard_map/ppermute | solution.py:657
  197.9 25.4 %all-to-all-start.1 = ((f32[2,8,6,8,128]{4,3,2,0,1:T(8,128)}), f32[2,8,6,8,128]{4,3,2,0,1:T(8,128)S(1)}, u32[]{:S(2)}, u32[]{:S(2)}) async-start(f32[2,8,6,8,128]{4,3,2,0,1:T(8,128)} %copy_add_fusion), calls=%async_computation.1 | async-start | bytes 786432 | tf_op jit(solution)/shard_map/all_to_all | solution.py:671
  211.0 10.6 %collective-permute-start.15 = (f32[8,11,8,128]{3,2,1,0:T(8,128)S(1)}, f32[8,11,8,128]{3,2,1,0:T(8,128)S(1)}, u32[]{:S(2)}, u32[]{:S(2)}) collective-permute-start(f32[8,11,8,128]{3,2,1,0:T(8,128)S(1)} %slice_add_fusion), channel_id=1, source_target_pairs={{0,2},{1,3},{2,0},{3,1},{4,6},{5,7},{6,4},{7,5},{8,10},{9,11},{10,... | collective-permute-start | bytes 1081352 | tf_op jit(solution)/shard_map/ppermute | solution.py:657
  223.3 15.0 %all-to-all-start = ((f32[8,11,8,128]{3,2,1,0:T(8,128)}), f32[8,11,8,128]{3,2,1,0:T(8,128)S(1)}, u32[]{:S(2)}, u32[]{:S(2)}) async-start(f32[8,11,8,128]{3,2,1,0:T(8,128)} %fusion), calls=%async_computation | async-start | bytes 720896 | tf_op jit(solution)/shard_map/all_to_all | solution.py:606
  228.1 3.9 %collective-permute-start.16 = (f32[6,8,128]{2,1,0:T(8,128)S(1)}, f32[6,8,128]{2,1,0:T(8,128)S(1)}, u32[]{:S(2)}, u32[]{:S(2)}) collective-permute-start(f32[6,8,128]{2,1,0:T(8,128)S(1)} %dynamic-slice_bitcast_fusion.4), channel_id=1, source_target_pairs={{0,2},{1,3},{2,0},{3,1},{4,6},{5,7},{6,4},{7,5},{8,10},{9,11},{10,... | collective-permute-start | bytes 73736 | tf_op jit(solution)/shard_map/ppermute | solution.py:657
  262.6 17.8 %all-to-all-start.3 = ((f32[8,128,128]{2,1,0:T(8,128)}), f32[8,128,128]{2,1,0:T(8,128)S(1)}, u32[]{:S(2)}, u32[]{:S(2)}) async-start(f32[8,128,128]{2,1,0:T(8,128)} %bitcast.13), calls=%async_computation.3 | async-start | bytes 1048576 | tf_op jit(solution)/shard_map/all_to_all | solution.py:606
  (6 other events, 7.1 us)

commit v4 on v3

--- a/solution.py
+++ b/solution.py
@@ -456,15 +456,24 @@
         vr, vi = ur * length, ui * length
     ur, ui = apply(vr, vi)
     energy = jnp.sum(vr * ur + vi * ui, axis=0, keepdims=True)
-    out_ref[0:blocks, :] = vr
-    out_ref[blocks : 2 * blocks, :] = vi
-    out_ref[2 * blocks : 2 * blocks + 8, :] = jnp.broadcast_to(energy, (8, count))
+    columns = jnp.concatenate([vr, vi, jnp.broadcast_to(energy, (8, count))], axis=0)
+    columns = jnp.pad(columns, ((0, LANES - columns.shape[0]), (0, LANES - count)))
+    rows = columns.T
+    half = count // 2
+    low = low_half((half, LANES))
+    lane = lax.broadcasted_iota(jnp.int32, (half, LANES), 1)
+    first, second = rows[:half], rows[half : 2 * half]
+    last = jnp.broadcast_to(rows[2 * half : count], (half, LANES))
+    ends = jnp.where(lane == 2, pltpu.roll(last, HALF + 2, 1), pltpu.roll(last, HALF, 1))
+    ends = jnp.where(lane == 1, pltpu.roll(second, HALF + 1, 1), ends)
+    out_ref[half:] = jnp.where(lane == 0, pltpu.roll(first, HALF, 1), ends)
+    out_ref[:half] = jnp.where(low, first, pltpu.roll(second, HALF, 1))
 
 
 def power(packed, blocks):
     return pl.pallas_call(
         functools.partial(power_kernel, blocks),
-        out_shape=jax.ShapeDtypeStruct((2 * blocks + 8, packed.shape[2]), F32),
+        out_shape=jax.ShapeDtypeStruct((packed.shape[2] // 2 * 2, LANES), F32),
         compiler_params=params(32),
         name="power",
     )(packed)
@@ -482,8 +491,27 @@
     return jnp.concatenate(tiles[::-1], axis=0)
 
 
+def unpack_vectors(packed_ref, v_ref, classes):
+    devices, rows, _ = packed_ref.shape
+    half = rows // 2
+    count = v_ref.shape[0] // devices
+    spaces = devices // classes
+    low = low_half((half, LANES))
+    for device in range(devices):
+        tau, space = divmod(device, spaces)
+        order = bit_reverse(space, spaces.bit_length() - 1)
+        start = (order * classes + tau) * count
+        vector, ends = packed_ref[device, :half, :], packed_ref[device, half:, :]
+        turned = pltpu.roll(ends, HALF, 1)
+        v_ref[start : start + half, :] = jnp.where(low, vector, turned)
+        second = jnp.where(low, pltpu.roll(vector, HALF, 1), pltpu.roll(ends, HALF - 1, 1))
+        v_ref[start + half : start + 2 * half, :] = second
+        last = jnp.where(low, turned, pltpu.roll(ends, HALF - 2, 1))
+        v_ref[start + 2 * half : start + count, :] = last[:1]
+
+
 def modes_kernel(tile, classes, total_times, *refs):
-    early, late, v_ref, out_ref, energy_ref, z_ref, s_ref, e_ref, sems = refs
+    early, late, packed_ref, out_ref, energy_ref, z_ref, s_ref, e_ref, v_ref, sems = refs
     chunks = z_ref.shape[0]
     blocks = CHUNK * z_ref.shape[0]
     group = 8
@@ -540,6 +568,7 @@
     for t in range(tiles):
         for copy in copies(t):
             copy.start()
+    unpack_vectors(packed_ref, v_ref, classes)
 
     def one_tile(t, carry):
         for copy in copies(t):
@@ -574,6 +603,7 @@
         out_shape=[jax.ShapeDtypeStruct((total, LANES), F32)] * 2,
         scratch_shapes=[
             pltpu.VMEM((early.shape[0] + 1, *early.shape[1:]), F32),
+            pltpu.VMEM((slots, LANES), F32),
             pltpu.VMEM((slots, LANES), F32),
             pltpu.VMEM((slots, LANES), F32),
             pltpu.SemaphoreType.DMA((2, slots // tile)),
@@ -663,7 +693,7 @@
     part, arriving = part.reshape(shape), arriving.reshape(shape)
     bit = space // 2
     pick = lambda value, i: lax.dynamic_index_in_dim(value, i, 0, keepdims=False)
-    cut = 2 * per_device // 3
+    cut = 3 * per_device // 4
     given = pick(part, 1 - bit)[:, :cut] + pick(arriving, 1 - bit)[:, :cut]
     kept = pick(part, bit)[:, :cut] + pick(arriving, bit)[:, :cut]
     given = swap(given, 1)
@@ -673,13 +703,9 @@
     part = exchange(kept + given, "tm").sum(axis=0)
     part = jnp.concatenate([part, rest], axis=0)
 
-    vectors = power(part.transpose(2, 1, 0), blocks).T
-    vectors = jnp.pad(vectors, ((0, 0), (0, LANES - vectors.shape[1])))
-    vectors = jnp.broadcast_to(vectors[None], (devices, per_device, LANES))
+    vectors = power(part.transpose(2, 1, 0), blocks)
+    vectors = jnp.broadcast_to(vectors[None], (devices, *vectors.shape))
     vectors = exchange(vectors, ("tm", "space"))
-    vectors = vectors.reshape(tm_size, *[2] * levels, per_device, LANES)
-    vectors = vectors.transpose(*range(levels, -1, -1), levels + 1, levels + 2)
-    vectors = vectors.reshape(slots, LANES)
 
     pieces, energies = modes(early, late, vectors, total_times, tm_size, slots, tile)
     pieces = exchange(pieces.reshape(tm_size, local_times, LANES), "tm")
@@ -693,7 +719,6 @@
     return (
         points == space_size * tm_size * HALF
         and (tm_size, space_size) == (8, 4)
-        and space_size & (space_size - 1) == 0
         and times % (tm_size * 8) == 0
         and blocks % CHUNK == 0
         and blocks == 32

time: 282 us -> 279 us (0.989)
  blocking collectives: 16.6 us -> 13.1 us
  waiting for transfers between devices: 113 us -> 116 us
    all_to_all x1, waiting for transfers between devices: 0.92 us -> 9.81 us  [body(): rest = lax.all_to_all(rest, 'tm', 1, 1, tiled=True).sum(axis=1)]
    ppermute x3, waiting for transfers between devices: 11.3 us -> 3.25 us  [swap(): return lax.ppermute(value, 'space', pairs)]
    all_to_all x1, blocking collectives: 16.6 us -> 13.1 us  [exchange(): return lax.all_to_all(value, axes, 0, 0, tiled=True)]
  transfers between devices with their start and end apart: 20 -> 20, of which waited for: 9 -> 8; matrix products, arithmetic and copies ran while one was open for 1% -> 2% of each run, Pallas kernels for 15% -> 15%
where the time goes in v4:
time: 279 us; the launch traced here: 278 us
  waiting for transfers between devices  116 us (42%)
  starting transfers between devices  78.8 us (28%)
  Pallas kernels  62 us (22%)
  blocking collectives  13.1 us (5%)
  local copies, waits for them, and re-layouts  4.69 us (2%)
    ppermute x14, waiting for transfers between devices, send(): flying[m] = lax.ppermute(part, 'tm', pairs) if m else part  81.2 us
    ppermute x14, starting transfers between devices, send(): flying[m] = lax.ppermute(part, 'tm', pairs) if m else part  56.4 us
    all_to_all x2, waiting for transfers between devices, exchange(): return lax.all_to_all(value, axes, 0, 0, tiled=True)  22 us
    pallas_call x5, Pallas kernels, pack(): pl.pallas_call(functools.partial(pack_kernel, offsets), grid=(1,), in_spe...  19.2 us
    all_to_all x1, blocking collectives, exchange(): return lax.all_to_all(value, axes, 0, 0, tiled=True)  13.1 us
    all_to_all x1, starting transfers between devices, body(): rest = lax.all_to_all(rest, 'tm', 1, 1, tiled=True).sum(axis=1)  13.1 us
    pallas_call x1, Pallas kernels, early_gram(): pl.pallas_call(functools.partial(early_gram_kernel, tile, chunks, 1.0 / t...  11.3 us
    all_to_all x1, waiting for transfers between devices, body(): rest = lax.all_to_all(rest, 'tm', 1, 1, tiled=True).sum(axis=1)  9.81 us
  transfers between devices with their start and end apart: 20, of which 8 were waited for; matrix products, arithmetic and copies ran while one was open for 2% of the time, Pallas kernels for 15%

profile of v4, /device:TPU:0, one launch (start us, length us, event | category | flops | bytes accessed | tf_op | source)
XLA Modules:
  0.0 278.5 jit_solution(9490722520734232785)
XLA Ops:
  0.6 2.9 %pack.5.refs_4_ = f32[3,128,512]{2,1,0:T(8,128)} custom-call(f32[128,32,512]{2,1,0:T(8,128)} %refs_3_.8, f32[1024,128]{1,0:T(8,128)} %constant.70.clone.refs_1_.refs_3_.refs_4_), custom_call_target="tpu_custom_call" | custom-call | tf_op jit(solution)/shard_map/pack/pallas_call | solution.py:111
  3.5 4.0 %collective-permute-start.3 = (f32[3,128,512]{2,1,0:T(8,128)}, f32[3,128,512]{2,1,0:T(8,128)S(1)}, u32[]{:S(2)}, u32[]{:S(2)}) collective-permute-start(f32[3,128,512]{2,1,0:T(8,128)} %pack.5.refs_4_), channel_id=1, source_target_pairs={{0,16},{4,20},{8,24},{12,28},{16,0},{20,4},{24,8},{28,12},{1,17},{... | collective-permute-start | bytes 2359304 | tf_op jit(solution)/shard_map/ppermute | solution.py:662
  7.5 4.7 %pack.6 = (f32[3,128,512]{2,1,0:T(8,128)}, f32[3,128,512]{2,1,0:T(8,128)}, f32[3,128,512]{2,1,0:T(8,128)}) custom-call(f32[128,32,512]{2,1,0:T(8,128)} %refs_3_.8, f32[128,32,512]{2,1,0:T(8,128)} %refs_3_.8, f32[128,32,512]{2,1,0:T(8,128)} %refs_3_.8, f32[1024,128]{1,0:T(8,128)} %constant.70.clone.refs_1_.refs_3_.refs_4_, f32[3,128,512]{2,1,0:T(8,128)} %pack.5.refs_4_), custom_call_target="tpu_custom_call" | custom-call | tf_op jit(solution)/shard_map/pack/pallas_call | solution.py:111
  12.2 5.7 %pack.7 = (f32[3,128,512]{2,1,0:T(8,128)}, f32[3,128,512]{2,1,0:T(8,128)}, f32[3,128,512]{2,1,0:T(8,128)}, f32[3,128,512]{2,1,0:T(8,128)}) custom-call(f32[128,32,512]{2,1,0:T(8,128)} %refs_3_.8, f32[128,32,512]{2,1,0:T(8,128)} %refs_3_.8, f32[128,32,512]{2,1,0:T(8,128)} %refs_3_.8, f32[128,32,512]{2,1,0:T(8,128)} %refs_3_.8, ...), custom_call_target="tpu_custom_call" | custom-call | tf_op jit(solution)/shard_map/pack/pallas_call | solution.py:111
  19.3 1.5 collective-permute-start
  21.1 1.7 collective-permute-start.2
  22.8 37.0 %collective-permute-done.3.refs_10_.refs_5_ = f32[3,128,512]{2,1,0:T(8,128)S(1)} collective-permute-done((f32[3,128,512]{2,1,0:T(8,128)}, f32[3,128,512]{2,1,0:T(8,128)S(1)}, u32[]{:S(2)}, u32[]{:S(2)}) %collective-permute-start.3) | collective-permute-done | bytes 786464 | tf_op jit(solution)/shard_map/ppermute | solution.py:662
  60.8 2.9 %collective-permute-start.6 = (f32[3,128,512]{2,1,0:T(8,128)}, f32[3,128,512]{2,1,0:T(8,128)}, u32[]{:S(2)}, u32[]{:S(2)}) collective-permute-start(f32[3,128,512]{2,1,0:T(8,128)} %get-tuple-element.27), channel_id=1, source_target_pairs={{0,28},{4,24},{8,20},{12,16},{16,12},{20,8},{24,4},{28,0},{1,29},{... | collective-permute-start | bytes 2359304 | tf_op jit(solution)/shard_map/ppermute | solution.py:662
  63.7 2.9 %pack.8 = (f32[1,128,512]{2,1,0:T(8,128)}, f32[1,128,512]{2,1,0:T(8,128)}, f32[1,128,512]{2,1,0:T(8,128)}, f32[1,128,512]{2,1,0:T(8,128)}) custom-call(f32[128,32,512]{2,1,0:T(8,128)} %refs_3_.8, f32[128,32,512]{2,1,0:T(8,128)} %refs_3_.8, f32[128,32,512]{2,1,0:T(8,128)} %refs_3_.8, f32[128,32,512]{2,1,0:T(8,128)} %refs_3_.8, ...), custom_call_target="tpu_custom_call" | custom-call | tf_op jit(solution)/shard_map/pack/pallas_call | solution.py:111
  66.7 3.0 %pack.9 = (f32[1,128,512]{2,1,0:T(8,128)}, f32[1,128,512]{2,1,0:T(8,128)}, f32[1,128,512]{2,1,0:T(8,128)}, f32[1,128,512]{2,1,0:T(8,128)}) custom-call(f32[128,32,512]{2,1,0:T(8,128)} %refs_3_.8, f32[128,32,512]{2,1,0:T(8,128)} %refs_3_.8, f32[128,32,512]{2,1,0:T(8,128)} %refs_3_.8, f32[128,32,512]{2,1,0:T(8,128)} %refs_3_.8, ...), custom_call_target="tpu_custom_call" | custom-call | tf_op jit(solution)/shard_map/pack/pallas_call | solution.py:111
  70.8 3.4 %collective-permute-done.1.refs_8_ = f32[3,128,512]{2,1,0:T(8,128)} collective-permute-done((f32[3,128,512]{2,1,0:T(8,128)}, f32[3,128,512]{2,1,0:T(8,128)}, u32[]{:S(2)}, u32[]{:S(2)}) %collective-permute-start.1) | collective-permute-done | bytes 786464 | tf_op jit(solution)/shard_map/ppermute | solution.py:662
  74.2 13.8 %collective-permute-start.8 = (f32[1,128,512]{2,1,0:T(8,128)}, f32[1,128,512]{2,1,0:T(8,128)S(1)}, u32[]{:S(2)}, u32[]{:S(2)}) collective-permute-start(f32[1,128,512]{2,1,0:T(8,128)} %get-tuple-element.30), channel_id=1, source_target_pairs={{0,8},{4,12},{8,0},{12,4},{16,24},{20,28},{24,16},{28,20},{1,9},{5... | collective-permute-start | bytes 786440 | tf_op jit(solution)/shard_map/ppermute | solution.py:662
  88.0 3.0 %collective-permute-done.2.refs_9_ = f32[3,128,512]{2,1,0:T(8,128)} collective-permute-done((f32[3,128,512]{2,1,0:T(8,128)}, f32[3,128,512]{2,1,0:T(8,128)}, u32[]{:S(2)}, u32[]{:S(2)}) %collective-permute-start.2) | collective-permute-done | bytes 786464 | tf_op jit(solution)/shard_map/ppermute | solution.py:662
  91.0 37.7 %collective-permute-done.4.refs_11_ = f32[3,128,512]{2,1,0:T(8,128)} collective-permute-done((f32[3,128,512]{2,1,0:T(8,128)S(1)}, f32[3,128,512]{2,1,0:T(8,128)}, u32[]{:S(2)}, u32[]{:S(2)}) %collective-permute-start.4) | collective-permute-done | bytes 786464 | tf_op jit(solution)/shard_map/ppermute | solution.py:662
  128.7 24.0 %collective-permute-start.11 = (f32[1,128,512]{2,1,0:T(8,128)}, f32[1,128,512]{2,1,0:T(8,128)S(1)}, u32[]{:S(2)}, u32[]{:S(2)}) collective-permute-start(f32[1,128,512]{2,1,0:T(8,128)} %get-tuple-element.33), channel_id=1, source_target_pairs={{0,20},{4,16},{8,28},{12,24},{16,4},{20,0},{24,12},{28,8},{1,21},{... | collective-permute-start | bytes 786440 | tf_op jit(solution)/shard_map/ppermute | solution.py:662
  153.7 3.8 %collective-permute-start.13 = (f32[1,128,512]{2,1,0:T(8,128)}, f32[1,128,512]{2,1,0:T(8,128)S(1)}, u32[]{:S(2)}, u32[]{:S(2)}) collective-permute-start(f32[1,128,512]{2,1,0:T(8,128)} %get-tuple-element.35), channel_id=1, source_target_pairs={{0,28},{4,24},{8,20},{12,16},{16,12},{20,8},{24,4},{28,0},{1,29},{... | collective-permute-start | bytes 786440 | tf_op jit(solution)/shard_map/ppermute | solution.py:662
  158.4 9.5 %transform.1.z_ref.refs_7_.refs_0_ = f32[3,4352,128]{2,1,0:T(8,128)} custom-call(bf16[512,512]{1,0:T(8,128)(2,1)S(1)} %copy-done, bf16[512,512]{1,0:T(8,128)(2,1)S(1)} %copy-done.1, bf16[256,256]{1,0:T(8,128)(2,1)S(1)} %copy-done.4, bf16[256,256]{1,0:T(8,128)(2,1)S(1)} %copy-done.5, bf16[320,256]{1,0:T(8,128)(2,1)S(1)} %copy-done.2, ...), custom_call_target="tpu_custom_call" | custom-call | tf_op jit(solution)/shard_map/transform/pallas_call | solution.py:188
  167.9 11.3 %early_gram.1.refs_8_.refs_2_ = f32[544,8,128]{2,1,0:T(8,128)} custom-call(f32[3,4352,128]{2,1,0:T(8,128)} %transform.1.z_ref.refs_7_.refs_0_, f32[1,128]{1,0:T(1,128)S(1)} %maximum_bitcast_fusion.w_ref.refs_6_.refs_3_), custom_call_target="tpu_custom_call" | custom-call | tf_op jit(solution)/shard_map/early_gram/pallas_call | solution.py:267
  180.8 8.3 %late_first.1 = (f32[1,4352,128]{2,1,0:T(8,128)}, f32[272,8,128]{2,1,0:T(8,128)}) custom-call(bf16[512,512]{1,0:T(8,128)(2,1)S(1)} %copy-done, bf16[512,512]{1,0:T(8,128)(2,1)S(1)} %copy-done.1, bf16[256,256]{1,0:T(8,128)(2,1)S(1)} %copy-done.4, bf16[256,256]{1,0:T(8,128)(2,1)S(1)} %copy-done.5, bf16[320,256]{1,0:T(8,128)(2,1)S(1)} %copy-done.2, ...), custom_call_target="tpu_custom_call" | custom-call | tf_op jit(solution)/shard_map/late_first/pallas_call | solution.py:358
  189.2 5.5 %late_second.1 = f32[272,8,128]{2,1,0:T(8,128)} custom-call(f32[3,4352,128]{2,1,0:T(8,128)} %transform.1.z_ref.refs_7_.refs_0_, f32[1,4352,128]{2,1,0:T(8,128)} %get-tuple-element.36.refs_1_, f32[544,8,128]{2,1,0:T(8,128)} %early_gram.1.refs_8_.refs_2_, f32[1,128]{1,0:T(1,128)S(1)} %maximum_bitcast_fusion.w_ref.refs_6_.refs_3_), custom_call_target="tpu_custom_call" | custom-call | tf_op jit(solution)/shard_map/late_second/pallas_call | solution.py:414
  196.2 1.6 collective-permute-start.15
  197.8 1.7 copy_add_fusion
  199.5 13.1 %all-to-all-start.1 = ((f32[2,8,5,8,128]{4,3,2,0,1:T(8,128)}), f32[2,8,5,8,128]{4,3,2,0,1:T(8,128)S(1)}, u32[]{:S(2)}, u32[]{:S(2)}) async-start(f32[2,8,5,8,128]{4,3,2,0,1:T(8,128)} %copy_add_fusion), calls=%async_computation.1 | async-start | bytes 655360 | tf_op jit(solution)/shard_map/all_to_all | solution.py:701
  213.4 9.8 %all-to-all-done.1 = f32[2,8,5,8,128]{4,3,2,0,1:T(8,128)S(1)} async-done(((f32[2,8,5,8,128]{4,3,2,0,1:T(8,128)}), f32[2,8,5,8,128]{4,3,2,0,1:T(8,128)S(1)}, u32[]{:S(2)}, u32[]{:S(2)}) %all-to-all-start.1) | async-done | bytes 327712 | tf_op jit(solution)/shard_map/all_to_all | solution.py:701
  223.2 3.6 %all-to-all-start = ((f32[8,12,8,128]{3,2,1,0:T(8,128)}), f32[8,12,8,128]{3,2,1,0:T(8,128)S(1)}, u32[]{:S(2)}, u32[]{:S(2)}) async-start(f32[8,12,8,128]{3,2,1,0:T(8,128)} %fusion), calls=%async_computation | async-start | bytes 786432 | tf_op jit(solution)/shard_map/all_to_all | solution.py:636
  227.4 3.2 %collective-permute-done.16 = f32[5,8,128]{2,1,0:T(8,128)S(1)} collective-permute-done((f32[5,8,128]{2,1,0:T(8,128)S(1)}, f32[5,8,128]{2,1,0:T(8,128)S(1)}, u32[]{:S(2)}, u32[]{:S(2)}) %collective-permute-start.16) | collective-permute-done | bytes 20512 | tf_op jit(solution)/shard_map/ppermute | solution.py:687
  230.7 7.9 %all-to-all-done = f32[8,12,8,128]{3,2,1,0:T(8,128)S(1)} async-done(((f32[8,12,8,128]{3,2,1,0:T(8,128)}), f32[8,12,8,128]{3,2,1,0:T(8,128)S(1)}, u32[]{:S(2)}, u32[]{:S(2)}) %all-to-all-start) | async-done | bytes 393248 | tf_op jit(solution)/shard_map/all_to_all | solution.py:636
  238.9 1.4 power.1
  240.3 13.1 %all_to_all.20.refs_2_ = f32[32,16,128]{2,1,0:T(8,128)S(1)} all-to-all(f32[32,16,128]{2,1,0:T(8,128)S(1)} %broadcast_in_dim.10), channel_id=1, replica_groups=mesh['tm'=8,'space'=4] {'tm','space'}, dimensions={0} | all-to-all | bytes 524288 | tf_op jit(solution)/shard_map/all_to_all | solution.py:636
  253.4 5.8 %modes.1 = (f32[1024,128]{1,0:T(8,128)}, f32[1024,128]{1,0:T(8,128)S(1)}) custom-call(f32[3,4352,128]{2,1,0:T(8,128)} %transform.1.z_ref.refs_7_.refs_0_, f32[1,4352,128]{2,1,0:T(8,128)} %get-tuple-element.36.refs_1_, f32[32,16,128]{2,1,0:T(8,128)S(1)} %all_to_all.20.refs_2_), custom_call_target="tpu_custom_call" | custom-call | tf_op jit(solution)/shard_map/modes/pallas_call | solution.py:596
  259.2 3.5 %all-to-all-start.3 = ((f32[8,128,128]{2,1,0:T(8,128)}), f32[8,128,128]{2,1,0:T(8,128)S(1)}, u32[]{:S(2)}, u32[]{:S(2)}) async-start(f32[8,128,128]{2,1,0:T(8,128)} %bitcast.10), calls=%async_computation.3 | async-start | bytes 1048576 | tf_op jit(solution)/shard_map/all_to_all | solution.py:636
  263.4 14.2 %all-to-all-done.3.x_ref = f32[8,128,128]{2,1,0:T(8,128)S(1)} async-done(((f32[8,128,128]{2,1,0:T(8,128)}), f32[8,128,128]{2,1,0:T(8,128)S(1)}, u32[]{:S(2)}, u32[]{:S(2)}) %all-to-all-start.3) | async-done | bytes 524320 | tf_op jit(solution)/shard_map/all_to_all | solution.py:636
  (73 shorter events, 12.1 us)
Async XLA Ops:
  3.5 56.4 %collective-permute-start.3 = (f32[3,128,512]{2,1,0:T(8,128)}, f32[3,128,512]{2,1,0:T(8,128)S(1)}, u32[]{:S(2)}, u32[]{:S(2)}) collective-permute-start(f32[3,128,512]{2,1,0:T(8,128)} %pack.5.refs_4_), channel_id=1, source_target_pairs={{0,16},{4,20},{8,24},{12,28},{16,0},{20,4},{24,8},{28,12},{1,17},{... | collective-permute-start | bytes 2359304 | tf_op jit(solution)/shard_map/ppermute | solution.py:662
  12.2 7.1 %copy-start.16 = (f32[3,128,512]{2,1,0:T(8,128)S(1)}, f32[3,128,512]{2,1,0:T(8,128)}, u32[]{:S(2)}) copy-start(f32[3,128,512]{2,1,0:T(8,128)} %get-tuple-element.22) | copy-start | bytes 2359300
  12.2 47.6 %copy-start.15 = (f32[3,128,512]{2,1,0:T(8,128)S(1)}, f32[3,128,512]{2,1,0:T(8,128)}, u32[]{:S(2)}) copy-start(f32[3,128,512]{2,1,0:T(8,128)} %get-tuple-element.25) | copy-start | bytes 2359300
  18.0 42.9 %collective-permute-start.5 = (f32[3,128,512]{2,1,0:T(8,128)}, f32[3,128,512]{2,1,0:T(8,128)S(1)}, u32[]{:S(2)}, u32[]{:S(2)}) collective-permute-start(f32[3,128,512]{2,1,0:T(8,128)} %get-tuple-element.26), channel_id=1, source_target_pairs={{0,24},{4,28},{8,16},{12,20},{16,8},{20,12},{24,0},{28,4},{1,25},{... | collective-permute-start | bytes 2359304 | tf_op jit(solution)/shard_map/ppermute | solution.py:662
  19.3 50.4 %collective-permute-start = (f32[3,128,512]{2,1,0:T(8,128)S(1)}, f32[3,128,512]{2,1,0:T(8,128)}, u32[]{:S(2)}, u32[]{:S(2)}) collective-permute-start(f32[3,128,512]{2,1,0:T(8,128)S(1)} %copy-done.16), channel_id=1, source_target_pairs={{0,4},{4,0},{8,12},{12,8},{16,20},{20,16},{24,28},{28,24},{1,5},{5... | collective-permute-start | bytes 2359304 | tf_op jit(solution)/shard_map/ppermute | solution.py:662
  20.8 53.3 %collective-permute-start.1 = (f32[3,128,512]{2,1,0:T(8,128)}, f32[3,128,512]{2,1,0:T(8,128)}, u32[]{:S(2)}, u32[]{:S(2)}) collective-permute-start(f32[3,128,512]{2,1,0:T(8,128)} %get-tuple-element.23), channel_id=1, source_target_pairs={{0,8},{4,12},{8,0},{12,4},{16,24},{20,28},{24,16},{28,20},{1,9},{5... | collective-permute-start | bytes 2359304 | tf_op jit(solution)/shard_map/ppermute | solution.py:662
  21.1 69.9 %collective-permute-start.2 = (f32[3,128,512]{2,1,0:T(8,128)}, f32[3,128,512]{2,1,0:T(8,128)}, u32[]{:S(2)}, u32[]{:S(2)}) collective-permute-start(f32[3,128,512]{2,1,0:T(8,128)} %get-tuple-element.24), channel_id=1, source_target_pairs={{0,12},{4,8},{8,4},{12,0},{16,28},{20,24},{24,20},{28,16},{1,13},{... | collective-permute-start | bytes 2359304 | tf_op jit(solution)/shard_map/ppermute | solution.py:662
  59.9 3.9 %copy-start.6 = (f32[3,128,512]{2,1,0:T(8,128)}, f32[3,128,512]{2,1,0:T(8,128)S(1)}, u32[]{:S(2)}) copy-start(f32[3,128,512]{2,1,0:T(8,128)S(1)} %collective-permute-done.3.refs_10_.refs_5_) | copy-start | bytes 2359300
  59.9 68.9 %collective-permute-start.4 = (f32[3,128,512]{2,1,0:T(8,128)S(1)}, f32[3,128,512]{2,1,0:T(8,128)}, u32[]{:S(2)}, u32[]{:S(2)}) collective-permute-start(f32[3,128,512]{2,1,0:T(8,128)S(1)} %copy-done.15), channel_id=1, source_target_pairs={{0,20},{4,16},{8,28},{12,24},{16,4},{20,0},{24,12},{28,8},{1,21},{... | collective-permute-start | bytes 2359304 | tf_op jit(solution)/shard_map/ppermute | solution.py:662
  60.8 5.8 %copy-start.7 = (f32[3,128,512]{2,1,0:T(8,128)}, f32[3,128,512]{2,1,0:T(8,128)S(1)}, u32[]{:S(2)}) copy-start(f32[3,128,512]{2,1,0:T(8,128)S(1)} %collective-permute-done.5.refs_12_.refs_6_) | copy-start | bytes 2359300
  60.8 67.9 %collective-permute-start.6 = (f32[3,128,512]{2,1,0:T(8,128)}, f32[3,128,512]{2,1,0:T(8,128)}, u32[]{:S(2)}, u32[]{:S(2)}) collective-permute-start(f32[3,128,512]{2,1,0:T(8,128)} %get-tuple-element.27), channel_id=1, source_target_pairs={{0,28},{4,24},{8,20},{12,16},{16,12},{20,8},{24,4},{28,0},{1,29},{... | collective-permute-start | bytes 2359304 | tf_op jit(solution)/shard_map/ppermute | solution.py:662
  66.6 91.7 %copy-start = (bf16[512,512]{1,0:T(8,128)(2,1)S(1)}, bf16[512,512]{1,0:T(8,128)(2,1)}, u32[]{:S(2)}) copy-start(bf16[512,512]{1,0:T(8,128)(2,1)} %constant.71.clone.refs_0_) | copy-start | bytes 1572868
  66.6 91.7 %copy-start.1 = (bf16[512,512]{1,0:T(8,128)(2,1)S(1)}, bf16[512,512]{1,0:T(8,128)(2,1)}, u32[]{:S(2)}) copy-start(bf16[512,512]{1,0:T(8,128)(2,1)} %constant.72.clone.refs_1_) | copy-start | bytes 1572868
  66.6 91.7 %copy-start.2 = (bf16[320,256]{1,0:T(8,128)(2,1)S(1)}, bf16[320,256]{1,0:T(8,128)(2,1)}, u32[]{:S(2)}) copy-start(bf16[320,256]{1,0:T(8,128)(2,1)} %constant.75.clone.refs_4_) | copy-start | bytes 491524
  66.7 91.7 %copy-start.3 = (bf16[320,256]{1,0:T(8,128)(2,1)S(1)}, bf16[320,256]{1,0:T(8,128)(2,1)}, u32[]{:S(2)}) copy-start(bf16[320,256]{1,0:T(8,128)(2,1)} %constant.76.clone.refs_5_) | copy-start | bytes 491524
  66.7 91.7 %copy-start.4 = (bf16[256,256]{1,0:T(8,128)(2,1)S(1)}, bf16[256,256]{1,0:T(8,128)(2,1)}, u32[]{:S(2)}) copy-start(bf16[256,256]{1,0:T(8,128)(2,1)} %constant.73.clone.refs_2_) | copy-start | bytes 393220
  66.7 91.7 %copy-start.5 = (bf16[256,256]{1,0:T(8,128)(2,1)S(1)}, bf16[256,256]{1,0:T(8,128)(2,1)}, u32[]{:S(2)}) copy-start(bf16[256,256]{1,0:T(8,128)(2,1)} %constant.74.clone.refs_3_) | copy-start | bytes 393220
  69.7 83.0 %collective-permute-start.7 = (f32[1,128,512]{2,1,0:T(8,128)S(1)}, f32[1,128,512]{2,1,0:T(8,128)S(1)}, u32[]{:S(2)}, u32[]{:S(2)}) collective-permute-start(f32[1,128,512]{2,1,0:T(8,128)S(1)} %copy-done.17), channel_id=1, source_target_pairs={{0,4},{4,0},{8,12},{12,8},{16,20},{20,16},{24,28},{28,24},{1,5},{5... | collective-permute-start | bytes 786440 | tf_op jit(solution)/shard_map/ppermute | solution.py:662
  74.2 79.5 %collective-permute-start.8 = (f32[1,128,512]{2,1,0:T(8,128)}, f32[1,128,512]{2,1,0:T(8,128)S(1)}, u32[]{:S(2)}, u32[]{:S(2)}) collective-permute-start(f32[1,128,512]{2,1,0:T(8,128)} %get-tuple-element.30), channel_id=1, source_target_pairs={{0,8},{4,12},{8,0},{12,4},{16,24},{20,28},{24,16},{28,20},{1,9},{5... | collective-permute-start | bytes 786440 | tf_op jit(solution)/shard_map/ppermute | solution.py:662
  91.0 88.1 %collective-permute-start.9 = (f32[1,128,512]{2,1,0:T(8,128)}, f32[1,128,512]{2,1,0:T(8,128)S(1)}, u32[]{:S(2)}, u32[]{:S(2)}) collective-permute-start(f32[1,128,512]{2,1,0:T(8,128)} %get-tuple-element.31), channel_id=1, source_target_pairs={{0,12},{4,8},{8,4},{12,0},{16,28},{20,24},{24,20},{28,16},{1,13},{... | collective-permute-start | bytes 786440 | tf_op jit(solution)/shard_map/ppermute | solution.py:662
  128.7 50.4 %collective-permute-start.10 = (f32[1,128,512]{2,1,0:T(8,128)}, f32[1,128,512]{2,1,0:T(8,128)S(1)}, u32[]{:S(2)}, u32[]{:S(2)}) collective-permute-start(f32[1,128,512]{2,1,0:T(8,128)} %get-tuple-element.32), channel_id=1, source_target_pairs={{0,16},{4,20},{8,24},{12,28},{16,0},{20,4},{24,8},{28,12},{1,17},{... | collective-permute-start | bytes 786440 | tf_op jit(solution)/shard_map/ppermute | solution.py:662
  128.7 50.5 %collective-permute-start.11 = (f32[1,128,512]{2,1,0:T(8,128)}, f32[1,128,512]{2,1,0:T(8,128)S(1)}, u32[]{:S(2)}, u32[]{:S(2)}) collective-permute-start(f32[1,128,512]{2,1,0:T(8,128)} %get-tuple-element.33), channel_id=1, source_target_pairs={{0,20},{4,16},{8,28},{12,24},{16,4},{20,0},{24,12},{28,8},{1,21},{... | collective-permute-start | bytes 786440 | tf_op jit(solution)/shard_map/ppermute | solution.py:662
  152.7 15.1 %copy-start.8 = (f32[1,128,512]{2,1,0:T(8,128)}, f32[1,128,512]{2,1,0:T(8,128)S(1)}, u32[]{:S(2)}) copy-start(f32[1,128,512]{2,1,0:T(8,128)S(1)} %collective-permute-done.7.refs_10_) | copy-start | bytes 786436
  152.7 26.5 %collective-permute-start.12 = (f32[1,128,512]{2,1,0:T(8,128)}, f32[1,128,512]{2,1,0:T(8,128)S(1)}, u32[]{:S(2)}, u32[]{:S(2)}) collective-permute-start(f32[1,128,512]{2,1,0:T(8,128)} %get-tuple-element.34), channel_id=1, source_target_pairs={{0,24},{4,28},{8,16},{12,20},{16,8},{20,12},{24,0},{28,4},{1,25},{... | collective-permute-start | bytes 786440 | tf_op jit(solution)/shard_map/ppermute | solution.py:662
  153.7 14.1 %copy-start.9 = (f32[1,128,512]{2,1,0:T(8,128)}, f32[1,128,512]{2,1,0:T(8,128)S(1)}, u32[]{:S(2)}) copy-start(f32[1,128,512]{2,1,0:T(8,128)S(1)} %collective-permute-done.8.refs_11_) | copy-start | bytes 786436
  153.7 25.5 %collective-permute-start.13 = (f32[1,128,512]{2,1,0:T(8,128)}, f32[1,128,512]{2,1,0:T(8,128)S(1)}, u32[]{:S(2)}, u32[]{:S(2)}) collective-permute-start(f32[1,128,512]{2,1,0:T(8,128)} %get-tuple-element.35), channel_id=1, source_target_pairs={{0,28},{4,24},{8,20},{12,16},{16,12},{20,8},{24,4},{28,0},{1,29},{... | collective-permute-start | bytes 786440 | tf_op jit(solution)/shard_map/ppermute | solution.py:662
  189.1 6.9 %collective-permute-start.14 = (f32[272,8,128]{2,1,0:T(8,128)}, f32[272,8,128]{2,1,0:T(8,128)S(1)}, u32[]{:S(2)}, u32[]{:S(2)}) collective-permute-start(f32[272,8,128]{2,1,0:T(8,128)} %get-tuple-element.37), channel_id=1, source_target_pairs={{0,1},{1,0},{2,3},{3,2},{4,5},{5,4},{6,7},{7,6},{8,9},{9,8},{10,11... | collective-permute-start | bytes 3342344 | tf_op jit(solution)/shard_map/ppermute | solution.py:687
  196.2 16.3 %collective-permute-start.15 = (f32[8,12,8,128]{3,2,1,0:T(8,128)S(1)}, f32[8,12,8,128]{3,2,1,0:T(8,128)S(1)}, u32[]{:S(2)}, u32[]{:S(2)}) collective-permute-start(f32[8,12,8,128]{3,2,1,0:T(8,128)S(1)} %slice_add_fusion), channel_id=1, source_target_pairs={{0,2},{1,3},{2,0},{3,1},{4,6},{5,7},{6,4},{7,5},{8,10},{9,11},{10,... | collective-permute-start | bytes 1179656 | tf_op jit(solution)/shard_map/ppermute | solution.py:687
  199.5 23.7 %all-to-all-start.1 = ((f32[2,8,5,8,128]{4,3,2,0,1:T(8,128)}), f32[2,8,5,8,128]{4,3,2,0,1:T(8,128)S(1)}, u32[]{:S(2)}, u32[]{:S(2)}) async-start(f32[2,8,5,8,128]{4,3,2,0,1:T(8,128)} %copy_add_fusion), calls=%async_computation.1 | async-start | bytes 655360 | tf_op jit(solution)/shard_map/all_to_all | solution.py:701
  223.2 15.4 %all-to-all-start = ((f32[8,12,8,128]{3,2,1,0:T(8,128)}), f32[8,12,8,128]{3,2,1,0:T(8,128)S(1)}, u32[]{:S(2)}, u32[]{:S(2)}) async-start(f32[8,12,8,128]{3,2,1,0:T(8,128)} %fusion), calls=%async_computation | async-start | bytes 786432 | tf_op jit(solution)/shard_map/all_to_all | solution.py:636
  226.8 3.8 %collective-permute-start.16 = (f32[5,8,128]{2,1,0:T(8,128)S(1)}, f32[5,8,128]{2,1,0:T(8,128)S(1)}, u32[]{:S(2)}, u32[]{:S(2)}) collective-permute-start(f32[5,8,128]{2,1,0:T(8,128)S(1)} %dynamic-slice_bitcast_fusion.4), channel_id=1, source_target_pairs={{0,2},{1,3},{2,0},{3,1},{4,6},{5,7},{6,4},{7,5},{8,10},{9,11},{10,... | collective-permute-start | bytes 61448 | tf_op jit(solution)/shard_map/ppermute | solution.py:687
  259.2 18.3 %all-to-all-start.3 = ((f32[8,128,128]{2,1,0:T(8,128)}), f32[8,128,128]{2,1,0:T(8,128)S(1)}, u32[]{:S(2)}, u32[]{:S(2)}) async-start(f32[8,128,128]{2,1,0:T(8,128)} %bitcast.10), calls=%async_computation.3 | async-start | bytes 1048576 | tf_op jit(solution)/shard_map/all_to_all | solution.py:636
  (6 other events, 7.1 us)

commit v5 on v4

--- a/solution.py
+++ b/solution.py
@@ -693,7 +693,7 @@
     part, arriving = part.reshape(shape), arriving.reshape(shape)
     bit = space // 2
     pick = lambda value, i: lax.dynamic_index_in_dim(value, i, 0, keepdims=False)
-    cut = 3 * per_device // 4
+    cut = 3 * per_device // 4 + 1
     given = pick(part, 1 - bit)[:, :cut] + pick(arriving, 1 - bit)[:, :cut]
     kept = pick(part, bit)[:, :cut] + pick(arriving, bit)[:, :cut]
     given = swap(given, 1)

time: 279 us -> 278 us (level)
  no operation moved by 1% of the time
where the time goes in v5:
time: 278 us; the launch traced here: 277 us
  waiting for transfers between devices  114 us (41%)
  starting transfers between devices  78.7 us (28%)
  Pallas kernels  62 us (22%)
  blocking collectives  13.1 us (5%)
  local copies, waits for them, and re-layouts  4.69 us (2%)
  other arithmetic  3.71 us (1%)
    ppermute x14, waiting for transfers between devices, send(): flying[m] = lax.ppermute(part, 'tm', pairs) if m else part  81.2 us
    ppermute x14, starting transfers between devices, send(): flying[m] = lax.ppermute(part, 'tm', pairs) if m else part  56.4 us
    all_to_all x2, waiting for transfers between devices, exchange(): return lax.all_to_all(value, axes, 0, 0, tiled=True)  22.4 us
    pallas_call x5, Pallas kernels, pack(): pl.pallas_call(functools.partial(pack_kernel, offsets), grid=(1,), in_spe...  19.2 us
    all_to_all x1, blocking collectives, exchange(): return lax.all_to_all(value, axes, 0, 0, tiled=True)  13.1 us
    all_to_all x1, starting transfers between devices, body(): rest = lax.all_to_all(rest, 'tm', 1, 1, tiled=True).sum(axis=1)  13.1 us
    pallas_call x1, Pallas kernels, early_gram(): pl.pallas_call(functools.partial(early_gram_kernel, tile, chunks, 1.0 / t...  11.3 us
    pallas_call x1, Pallas kernels, transform(): pl.pallas_call(transform_kernel, grid=(chunks,), in_specs=[pl.BlockSpec(t...  9.49 us
  transfers between devices with their start and end apart: 20, of which 8 were waited for; matrix products, arithmetic and copies ran while one was open for 2% of the time, Pallas kernels for 15%

profile of v5, /device:TPU:0, one launch (start us, length us, event | category | flops | bytes accessed | tf_op | source)
XLA Modules:
  0.0 277.4 jit_solution(8547189701391761313)
XLA Ops:
  0.6 2.9 %pack.5.refs_4_ = f32[3,128,512]{2,1,0:T(8,128)} custom-call(f32[128,32,512]{2,1,0:T(8,128)} %refs_3_.8, f32[1024,128]{1,0:T(8,128)} %constant.70.clone.refs_1_.refs_3_.refs_4_), custom_call_target="tpu_custom_call" | custom-call | tf_op jit(solution)/shard_map/pack/pallas_call | solution.py:111
  3.5 4.0 %collective-permute-start.3 = (f32[3,128,512]{2,1,0:T(8,128)}, f32[3,128,512]{2,1,0:T(8,128)S(1)}, u32[]{:S(2)}, u32[]{:S(2)}) collective-permute-start(f32[3,128,512]{2,1,0:T(8,128)} %pack.5.refs_4_), channel_id=1, source_target_pairs={{0,16},{4,20},{8,24},{12,28},{16,0},{20,4},{24,8},{28,12},{1,17},{... | collective-permute-start | bytes 2359304 | tf_op jit(solution)/shard_map/ppermute | solution.py:662
  7.5 4.7 %pack.6 = (f32[3,128,512]{2,1,0:T(8,128)}, f32[3,128,512]{2,1,0:T(8,128)}, f32[3,128,512]{2,1,0:T(8,128)}) custom-call(f32[128,32,512]{2,1,0:T(8,128)} %refs_3_.8, f32[128,32,512]{2,1,0:T(8,128)} %refs_3_.8, f32[128,32,512]{2,1,0:T(8,128)} %refs_3_.8, f32[1024,128]{1,0:T(8,128)} %constant.70.clone.refs_1_.refs_3_.refs_4_, f32[3,128,512]{2,1,0:T(8,128)} %pack.5.refs_4_), custom_call_target="tpu_custom_call" | custom-call | tf_op jit(solution)/shard_map/pack/pallas_call | solution.py:111
  12.2 5.7 %pack.7 = (f32[3,128,512]{2,1,0:T(8,128)}, f32[3,128,512]{2,1,0:T(8,128)}, f32[3,128,512]{2,1,0:T(8,128)}, f32[3,128,512]{2,1,0:T(8,128)}) custom-call(f32[128,32,512]{2,1,0:T(8,128)} %refs_3_.8, f32[128,32,512]{2,1,0:T(8,128)} %refs_3_.8, f32[128,32,512]{2,1,0:T(8,128)} %refs_3_.8, f32[128,32,512]{2,1,0:T(8,128)} %refs_3_.8, ...), custom_call_target="tpu_custom_call" | custom-call | tf_op jit(solution)/shard_map/pack/pallas_call | solution.py:111
  19.3 1.5 collective-permute-start
  21.1 1.7 collective-permute-start.2
  22.8 37.0 %collective-permute-done.3.refs_10_.refs_5_ = f32[3,128,512]{2,1,0:T(8,128)S(1)} collective-permute-done((f32[3,128,512]{2,1,0:T(8,128)}, f32[3,128,512]{2,1,0:T(8,128)S(1)}, u32[]{:S(2)}, u32[]{:S(2)}) %collective-permute-start.3) | collective-permute-done | bytes 786464 | tf_op jit(solution)/shard_map/ppermute | solution.py:662
  60.8 2.9 %collective-permute-start.6 = (f32[3,128,512]{2,1,0:T(8,128)}, f32[3,128,512]{2,1,0:T(8,128)}, u32[]{:S(2)}, u32[]{:S(2)}) collective-permute-start(f32[3,128,512]{2,1,0:T(8,128)} %get-tuple-element.27), channel_id=1, source_target_pairs={{0,28},{4,24},{8,20},{12,16},{16,12},{20,8},{24,4},{28,0},{1,29},{... | collective-permute-start | bytes 2359304 | tf_op jit(solution)/shard_map/ppermute | solution.py:662
  63.7 2.9 %pack.8 = (f32[1,128,512]{2,1,0:T(8,128)}, f32[1,128,512]{2,1,0:T(8,128)}, f32[1,128,512]{2,1,0:T(8,128)}, f32[1,128,512]{2,1,0:T(8,128)}) custom-call(f32[128,32,512]{2,1,0:T(8,128)} %refs_3_.8, f32[128,32,512]{2,1,0:T(8,128)} %refs_3_.8, f32[128,32,512]{2,1,0:T(8,128)} %refs_3_.8, f32[128,32,512]{2,1,0:T(8,128)} %refs_3_.8, ...), custom_call_target="tpu_custom_call" | custom-call | tf_op jit(solution)/shard_map/pack/pallas_call | solution.py:111
  66.7 3.0 %pack.9 = (f32[1,128,512]{2,1,0:T(8,128)}, f32[1,128,512]{2,1,0:T(8,128)}, f32[1,128,512]{2,1,0:T(8,128)}, f32[1,128,512]{2,1,0:T(8,128)}) custom-call(f32[128,32,512]{2,1,0:T(8,128)} %refs_3_.8, f32[128,32,512]{2,1,0:T(8,128)} %refs_3_.8, f32[128,32,512]{2,1,0:T(8,128)} %refs_3_.8, f32[128,32,512]{2,1,0:T(8,128)} %refs_3_.8, ...), custom_call_target="tpu_custom_call" | custom-call | tf_op jit(solution)/shard_map/pack/pallas_call | solution.py:111
  70.8 3.4 %collective-permute-done.1.refs_8_ = f32[3,128,512]{2,1,0:T(8,128)} collective-permute-done((f32[3,128,512]{2,1,0:T(8,128)}, f32[3,128,512]{2,1,0:T(8,128)}, u32[]{:S(2)}, u32[]{:S(2)}) %collective-permute-start.1) | collective-permute-done | bytes 786464 | tf_op jit(solution)/shard_map/ppermute | solution.py:662
  74.2 13.8 %collective-permute-start.8 = (f32[1,128,512]{2,1,0:T(8,128)}, f32[1,128,512]{2,1,0:T(8,128)S(1)}, u32[]{:S(2)}, u32[]{:S(2)}) collective-permute-start(f32[1,128,512]{2,1,0:T(8,128)} %get-tuple-element.30), channel_id=1, source_target_pairs={{0,8},{4,12},{8,0},{12,4},{16,24},{20,28},{24,16},{28,20},{1,9},{5... | collective-permute-start | bytes 786440 | tf_op jit(solution)/shard_map/ppermute | solution.py:662
  88.0 3.0 %collective-permute-done.2.refs_9_ = f32[3,128,512]{2,1,0:T(8,128)} collective-permute-done((f32[3,128,512]{2,1,0:T(8,128)}, f32[3,128,512]{2,1,0:T(8,128)}, u32[]{:S(2)}, u32[]{:S(2)}) %collective-permute-start.2) | collective-permute-done | bytes 786464 | tf_op jit(solution)/shard_map/ppermute | solution.py:662
  91.0 37.7 %collective-permute-done.4.refs_11_ = f32[3,128,512]{2,1,0:T(8,128)} collective-permute-done((f32[3,128,512]{2,1,0:T(8,128)S(1)}, f32[3,128,512]{2,1,0:T(8,128)}, u32[]{:S(2)}, u32[]{:S(2)}) %collective-permute-start.4) | collective-permute-done | bytes 786464 | tf_op jit(solution)/shard_map/ppermute | solution.py:662
  128.7 24.0 %collective-permute-start.11 = (f32[1,128,512]{2,1,0:T(8,128)}, f32[1,128,512]{2,1,0:T(8,128)S(1)}, u32[]{:S(2)}, u32[]{:S(2)}) collective-permute-start(f32[1,128,512]{2,1,0:T(8,128)} %get-tuple-element.33), channel_id=1, source_target_pairs={{0,20},{4,16},{8,28},{12,24},{16,4},{20,0},{24,12},{28,8},{1,21},{... | collective-permute-start | bytes 786440 | tf_op jit(solution)/shard_map/ppermute | solution.py:662
  153.7 3.8 %collective-permute-start.13 = (f32[1,128,512]{2,1,0:T(8,128)}, f32[1,128,512]{2,1,0:T(8,128)S(1)}, u32[]{:S(2)}, u32[]{:S(2)}) collective-permute-start(f32[1,128,512]{2,1,0:T(8,128)} %get-tuple-element.35), channel_id=1, source_target_pairs={{0,28},{4,24},{8,20},{12,16},{16,12},{20,8},{24,4},{28,0},{1,29},{... | collective-permute-start | bytes 786440 | tf_op jit(solution)/shard_map/ppermute | solution.py:662
  158.4 9.5 %transform.1.z_ref.refs_7_.refs_0_ = f32[3,4352,128]{2,1,0:T(8,128)} custom-call(bf16[512,512]{1,0:T(8,128)(2,1)S(1)} %copy-done, bf16[512,512]{1,0:T(8,128)(2,1)S(1)} %copy-done.1, bf16[256,256]{1,0:T(8,128)(2,1)S(1)} %copy-done.4, bf16[256,256]{1,0:T(8,128)(2,1)S(1)} %copy-done.5, bf16[320,256]{1,0:T(8,128)(2,1)S(1)} %copy-done.2, ...), custom_call_target="tpu_custom_call" | custom-call | tf_op jit(solution)/shard_map/transform/pallas_call | solution.py:188
  167.9 11.3 %early_gram.1.refs_8_.refs_2_ = f32[544,8,128]{2,1,0:T(8,128)} custom-call(f32[3,4352,128]{2,1,0:T(8,128)} %transform.1.z_ref.refs_7_.refs_0_, f32[1,128]{1,0:T(1,128)S(1)} %maximum_bitcast_fusion.w_ref.refs_6_.refs_3_), custom_call_target="tpu_custom_call" | custom-call | tf_op jit(solution)/shard_map/early_gram/pallas_call | solution.py:267
  180.8 8.3 %late_first.1 = (f32[1,4352,128]{2,1,0:T(8,128)}, f32[272,8,128]{2,1,0:T(8,128)}) custom-call(bf16[512,512]{1,0:T(8,128)(2,1)S(1)} %copy-done, bf16[512,512]{1,0:T(8,128)(2,1)S(1)} %copy-done.1, bf16[256,256]{1,0:T(8,128)(2,1)S(1)} %copy-done.4, bf16[256,256]{1,0:T(8,128)(2,1)S(1)} %copy-done.5, bf16[320,256]{1,0:T(8,128)(2,1)S(1)} %copy-done.2, ...), custom_call_target="tpu_custom_call" | custom-call | tf_op jit(solution)/shard_map/late_first/pallas_call | solution.py:358
  189.2 5.5 %late_second.1 = f32[272,8,128]{2,1,0:T(8,128)} custom-call(f32[3,4352,128]{2,1,0:T(8,128)} %transform.1.z_ref.refs_7_.refs_0_, f32[1,4352,128]{2,1,0:T(8,128)} %get-tuple-element.36.refs_1_, f32[544,8,128]{2,1,0:T(8,128)} %early_gram.1.refs_8_.refs_2_, f32[1,128]{1,0:T(1,128)S(1)} %maximum_bitcast_fusion.w_ref.refs_6_.refs_3_), custom_call_target="tpu_custom_call" | custom-call | tf_op jit(solution)/shard_map/late_second/pallas_call | solution.py:414
  196.2 1.6 collective-permute-start.15
  197.8 1.7 copy_add_fusion
  199.5 13.1 %all-to-all-start.1 = ((f32[2,8,4,8,128]{4,3,2,0,1:T(8,128)}), f32[2,8,4,8,128]{4,3,2,0,1:T(8,128)S(1)}, u32[]{:S(2)}, u32[]{:S(2)}) async-start(f32[2,8,4,8,128]{4,3,2,0,1:T(8,128)} %copy_add_fusion), calls=%async_computation.1 | async-start | bytes 524288 | tf_op jit(solution)/shard_map/all_to_all | solution.py:701
  212.5 1.8 fusion
  214.4 7.4 %all-to-all-done.1 = f32[2,8,4,8,128]{4,3,2,0,1:T(8,128)S(1)} async-done(((f32[2,8,4,8,128]{4,3,2,0,1:T(8,128)}), f32[2,8,4,8,128]{4,3,2,0,1:T(8,128)S(1)}, u32[]{:S(2)}, u32[]{:S(2)}) %all-to-all-start.1) | async-done | bytes 262176 | tf_op jit(solution)/shard_map/all_to_all | solution.py:701
  221.8 3.6 %all-to-all-start = ((f32[8,13,8,128]{3,2,1,0:T(8,128)}), f32[8,13,8,128]{3,2,1,0:T(8,128)S(1)}, u32[]{:S(2)}, u32[]{:S(2)}) async-start(f32[8,13,8,128]{3,2,1,0:T(8,128)} %fusion), calls=%async_computation | async-start | bytes 851968 | tf_op jit(solution)/shard_map/all_to_all | solution.py:636
  226.0 3.2 %collective-permute-done.16 = f32[4,8,128]{2,1,0:T(8,128)S(1)} collective-permute-done((f32[4,8,128]{2,1,0:T(8,128)S(1)}, f32[4,8,128]{2,1,0:T(8,128)S(1)}, u32[]{:S(2)}, u32[]{:S(2)}) %collective-permute-start.16) | collective-permute-done | bytes 16416 | tf_op jit(solution)/shard_map/ppermute | solution.py:687
  229.2 8.2 %all-to-all-done = f32[8,13,8,128]{3,2,1,0:T(8,128)S(1)} async-done(((f32[8,13,8,128]{3,2,1,0:T(8,128)}), f32[8,13,8,128]{3,2,1,0:T(8,128)S(1)}, u32[]{:S(2)}, u32[]{:S(2)}) %all-to-all-start) | async-done | bytes 426016 | tf_op jit(solution)/shard_map/all_to_all | solution.py:636
  239.2 13.1 %all_to_all.20.refs_2_ = f32[32,16,128]{2,1,0:T(8,128)S(1)} all-to-all(f32[32,16,128]{2,1,0:T(8,128)S(1)} %broadcast_in_dim.10), channel_id=1, replica_groups=mesh['tm'=8,'space'=4] {'tm','space'}, dimensions={0} | all-to-all | bytes 524288 | tf_op jit(solution)/shard_map/all_to_all | solution.py:636
  252.3 5.8 %modes.1 = (f32[1024,128]{1,0:T(8,128)}, f32[1024,128]{1,0:T(8,128)S(1)}) custom-call(f32[3,4352,128]{2,1,0:T(8,128)} %transform.1.z_ref.refs_7_.refs_0_, f32[1,4352,128]{2,1,0:T(8,128)} %get-tuple-element.36.refs_1_, f32[32,16,128]{2,1,0:T(8,128)S(1)} %all_to_all.20.refs_2_), custom_call_target="tpu_custom_call" | custom-call | tf_op jit(solution)/shard_map/modes/pallas_call | solution.py:596
  258.1 3.5 %all-to-all-start.3 = ((f32[8,128,128]{2,1,0:T(8,128)}), f32[8,128,128]{2,1,0:T(8,128)S(1)}, u32[]{:S(2)}, u32[]{:S(2)}) async-start(f32[8,128,128]{2,1,0:T(8,128)} %bitcast.10), calls=%async_computation.3 | async-start | bytes 1048576 | tf_op jit(solution)/shard_map/all_to_all | solution.py:636
  262.2 14.2 %all-to-all-done.3.x_ref = f32[8,128,128]{2,1,0:T(8,128)S(1)} async-done(((f32[8,128,128]{2,1,0:T(8,128)}), f32[8,128,128]{2,1,0:T(8,128)S(1)}, u32[]{:S(2)}, u32[]{:S(2)}) %all-to-all-start.3) | async-done | bytes 524320 | tf_op jit(solution)/shard_map/all_to_all | solution.py:636
  (73 shorter events, 12.7 us)
Async XLA Ops:
  3.5 56.4 %collective-permute-start.3 = (f32[3,128,512]{2,1,0:T(8,128)}, f32[3,128,512]{2,1,0:T(8,128)S(1)}, u32[]{:S(2)}, u32[]{:S(2)}) collective-permute-start(f32[3,128,512]{2,1,0:T(8,128)} %pack.5.refs_4_), channel_id=1, source_target_pairs={{0,16},{4,20},{8,24},{12,28},{16,0},{20,4},{24,8},{28,12},{1,17},{... | collective-permute-start | bytes 2359304 | tf_op jit(solution)/shard_map/ppermute | solution.py:662
  12.2 7.1 %copy-start.16 = (f32[3,128,512]{2,1,0:T(8,128)S(1)}, f32[3,128,512]{2,1,0:T(8,128)}, u32[]{:S(2)}) copy-start(f32[3,128,512]{2,1,0:T(8,128)} %get-tuple-element.22) | copy-start | bytes 2359300
  12.2 47.6 %copy-start.15 = (f32[3,128,512]{2,1,0:T(8,128)S(1)}, f32[3,128,512]{2,1,0:T(8,128)}, u32[]{:S(2)}) copy-start(f32[3,128,512]{2,1,0:T(8,128)} %get-tuple-element.25) | copy-start | bytes 2359300
  18.0 42.9 %collective-permute-start.5 = (f32[3,128,512]{2,1,0:T(8,128)}, f32[3,128,512]{2,1,0:T(8,128)S(1)}, u32[]{:S(2)}, u32[]{:S(2)}) collective-permute-start(f32[3,128,512]{2,1,0:T(8,128)} %get-tuple-element.26), channel_id=1, source_target_pairs={{0,24},{4,28},{8,16},{12,20},{16,8},{20,12},{24,0},{28,4},{1,25},{... | collective-permute-start | bytes 2359304 | tf_op jit(solution)/shard_map/ppermute | solution.py:662
  19.3 50.4 %collective-permute-start = (f32[3,128,512]{2,1,0:T(8,128)S(1)}, f32[3,128,512]{2,1,0:T(8,128)}, u32[]{:S(2)}, u32[]{:S(2)}) collective-permute-start(f32[3,128,512]{2,1,0:T(8,128)S(1)} %copy-done.16), channel_id=1, source_target_pairs={{0,4},{4,0},{8,12},{12,8},{16,20},{20,16},{24,28},{28,24},{1,5},{5... | collective-permute-start | bytes 2359304 | tf_op jit(solution)/shard_map/ppermute | solution.py:662
  20.8 53.3 %collective-permute-start.1 = (f32[3,128,512]{2,1,0:T(8,128)}, f32[3,128,512]{2,1,0:T(8,128)}, u32[]{:S(2)}, u32[]{:S(2)}) collective-permute-start(f32[3,128,512]{2,1,0:T(8,128)} %get-tuple-element.23), channel_id=1, source_target_pairs={{0,8},{4,12},{8,0},{12,4},{16,24},{20,28},{24,16},{28,20},{1,9},{5... | collective-permute-start | bytes 2359304 | tf_op jit(solution)/shard_map/ppermute | solution.py:662
  21.1 69.9 %collective-permute-start.2 = (f32[3,128,512]{2,1,0:T(8,128)}, f32[3,128,512]{2,1,0:T(8,128)}, u32[]{:S(2)}, u32[]{:S(2)}) collective-permute-start(f32[3,128,512]{2,1,0:T(8,128)} %get-tuple-element.24), channel_id=1, source_target_pairs={{0,12},{4,8},{8,4},{12,0},{16,28},{20,24},{24,20},{28,16},{1,13},{... | collective-permute-start | bytes 2359304 | tf_op jit(solution)/shard_map/ppermute | solution.py:662
  59.9 3.9 %copy-start.6 = (f32[3,128,512]{2,1,0:T(8,128)}, f32[3,128,512]{2,1,0:T(8,128)S(1)}, u32[]{:S(2)}) copy-start(f32[3,128,512]{2,1,0:T(8,128)S(1)} %collective-permute-done.3.refs_10_.refs_5_) | copy-start | bytes 2359300
  59.9 68.9 %collective-permute-start.4 = (f32[3,128,512]{2,1,0:T(8,128)S(1)}, f32[3,128,512]{2,1,0:T(8,128)}, u32[]{:S(2)}, u32[]{:S(2)}) collective-permute-start(f32[3,128,512]{2,1,0:T(8,128)S(1)} %copy-done.15), channel_id=1, source_target_pairs={{0,20},{4,16},{8,28},{12,24},{16,4},{20,0},{24,12},{28,8},{1,21},{... | collective-permute-start | bytes 2359304 | tf_op jit(solution)/shard_map/ppermute | solution.py:662
  60.8 5.8 %copy-start.7 = (f32[3,128,512]{2,1,0:T(8,128)}, f32[3,128,512]{2,1,0:T(8,128)S(1)}, u32[]{:S(2)}) copy-start(f32[3,128,512]{2,1,0:T(8,128)S(1)} %collective-permute-done.5.refs_12_.refs_6_) | copy-start | bytes 2359300
  60.8 67.9 %collective-permute-start.6 = (f32[3,128,512]{2,1,0:T(8,128)}, f32[3,128,512]{2,1,0:T(8,128)}, u32[]{:S(2)}, u32[]{:S(2)}) collective-permute-start(f32[3,128,512]{2,1,0:T(8,128)} %get-tuple-element.27), channel_id=1, source_target_pairs={{0,28},{4,24},{8,20},{12,16},{16,12},{20,8},{24,4},{28,0},{1,29},{... | collective-permute-start | bytes 2359304 | tf_op jit(solution)/shard_map/ppermute | solution.py:662
  66.6 91.7 %copy-start = (bf16[512,512]{1,0:T(8,128)(2,1)S(1)}, bf16[512,512]{1,0:T(8,128)(2,1)}, u32[]{:S(2)}) copy-start(bf16[512,512]{1,0:T(8,128)(2,1)} %constant.71.clone.refs_0_) | copy-start | bytes 1572868
  66.6 91.7 %copy-start.1 = (bf16[512,512]{1,0:T(8,128)(2,1)S(1)}, bf16[512,512]{1,0:T(8,128)(2,1)}, u32[]{:S(2)}) copy-start(bf16[512,512]{1,0:T(8,128)(2,1)} %constant.72.clone.refs_1_) | copy-start | bytes 1572868
  66.6 91.7 %copy-start.2 = (bf16[320,256]{1,0:T(8,128)(2,1)S(1)}, bf16[320,256]{1,0:T(8,128)(2,1)}, u32[]{:S(2)}) copy-start(bf16[320,256]{1,0:T(8,128)(2,1)} %constant.75.clone.refs_4_) | copy-start | bytes 491524
  66.7 91.7 %copy-start.3 = (bf16[320,256]{1,0:T(8,128)(2,1)S(1)}, bf16[320,256]{1,0:T(8,128)(2,1)}, u32[]{:S(2)}) copy-start(bf16[320,256]{1,0:T(8,128)(2,1)} %constant.76.clone.refs_5_) | copy-start | bytes 491524
  66.7 91.7 %copy-start.4 = (bf16[256,256]{1,0:T(8,128)(2,1)S(1)}, bf16[256,256]{1,0:T(8,128)(2,1)}, u32[]{:S(2)}) copy-start(bf16[256,256]{1,0:T(8,128)(2,1)} %constant.73.clone.refs_2_) | copy-start | bytes 393220
  66.7 91.7 %copy-start.5 = (bf16[256,256]{1,0:T(8,128)(2,1)S(1)}, bf16[256,256]{1,0:T(8,128)(2,1)}, u32[]{:S(2)}) copy-start(bf16[256,256]{1,0:T(8,128)(2,1)} %constant.74.clone.refs_3_) | copy-start | bytes 393220
  69.7 83.0 %collective-permute-start.7 = (f32[1,128,512]{2,1,0:T(8,128)S(1)}, f32[1,128,512]{2,1,0:T(8,128)S(1)}, u32[]{:S(2)}, u32[]{:S(2)}) collective-permute-start(f32[1,128,512]{2,1,0:T(8,128)S(1)} %copy-done.17), channel_id=1, source_target_pairs={{0,4},{4,0},{8,12},{12,8},{16,20},{20,16},{24,28},{28,24},{1,5},{5... | collective-permute-start | bytes 786440 | tf_op jit(solution)/shard_map/ppermute | solution.py:662
  74.2 79.5 %collective-permute-start.8 = (f32[1,128,512]{2,1,0:T(8,128)}, f32[1,128,512]{2,1,0:T(8,128)S(1)}, u32[]{:S(2)}, u32[]{:S(2)}) collective-permute-start(f32[1,128,512]{2,1,0:T(8,128)} %get-tuple-element.30), channel_id=1, source_target_pairs={{0,8},{4,12},{8,0},{12,4},{16,24},{20,28},{24,16},{28,20},{1,9},{5... | collective-permute-start | bytes 786440 | tf_op jit(solution)/shard_map/ppermute | solution.py:662
  91.0 88.1 %collective-permute-start.9 = (f32[1,128,512]{2,1,0:T(8,128)}, f32[1,128,512]{2,1,0:T(8,128)S(1)}, u32[]{:S(2)}, u32[]{:S(2)}) collective-permute-start(f32[1,128,512]{2,1,0:T(8,128)} %get-tuple-element.31), channel_id=1, source_target_pairs={{0,12},{4,8},{8,4},{12,0},{16,28},{20,24},{24,20},{28,16},{1,13},{... | collective-permute-start | bytes 786440 | tf_op jit(solution)/shard_map/ppermute | solution.py:662
  128.7 50.4 %collective-permute-start.10 = (f32[1,128,512]{2,1,0:T(8,128)}, f32[1,128,512]{2,1,0:T(8,128)S(1)}, u32[]{:S(2)}, u32[]{:S(2)}) collective-permute-start(f32[1,128,512]{2,1,0:T(8,128)} %get-tuple-element.32), channel_id=1, source_target_pairs={{0,16},{4,20},{8,24},{12,28},{16,0},{20,4},{24,8},{28,12},{1,17},{... | collective-permute-start | bytes 786440 | tf_op jit(solution)/shard_map/ppermute | solution.py:662
  128.7 50.5 %collective-permute-start.11 = (f32[1,128,512]{2,1,0:T(8,128)}, f32[1,128,512]{2,1,0:T(8,128)S(1)}, u32[]{:S(2)}, u32[]{:S(2)}) collective-permute-start(f32[1,128,512]{2,1,0:T(8,128)} %get-tuple-element.33), channel_id=1, source_target_pairs={{0,20},{4,16},{8,28},{12,24},{16,4},{20,0},{24,12},{28,8},{1,21},{... | collective-permute-start | bytes 786440 | tf_op jit(solution)/shard_map/ppermute | solution.py:662
  152.7 15.1 %copy-start.8 = (f32[1,128,512]{2,1,0:T(8,128)}, f32[1,128,512]{2,1,0:T(8,128)S(1)}, u32[]{:S(2)}) copy-start(f32[1,128,512]{2,1,0:T(8,128)S(1)} %collective-permute-done.7.refs_10_) | copy-start | bytes 786436
  152.7 26.5 %collective-permute-start.12 = (f32[1,128,512]{2,1,0:T(8,128)}, f32[1,128,512]{2,1,0:T(8,128)S(1)}, u32[]{:S(2)}, u32[]{:S(2)}) collective-permute-start(f32[1,128,512]{2,1,0:T(8,128)} %get-tuple-element.34), channel_id=1, source_target_pairs={{0,24},{4,28},{8,16},{12,20},{16,8},{20,12},{24,0},{28,4},{1,25},{... | collective-permute-start | bytes 786440 | tf_op jit(solution)/shard_map/ppermute | solution.py:662
  153.7 14.1 %copy-start.9 = (f32[1,128,512]{2,1,0:T(8,128)}, f32[1,128,512]{2,1,0:T(8,128)S(1)}, u32[]{:S(2)}) copy-start(f32[1,128,512]{2,1,0:T(8,128)S(1)} %collective-permute-done.8.refs_11_) | copy-start | bytes 786436
  153.7 25.5 %collective-permute-start.13 = (f32[1,128,512]{2,1,0:T(8,128)}, f32[1,128,512]{2,1,0:T(8,128)S(1)}, u32[]{:S(2)}, u32[]{:S(2)}) collective-permute-start(f32[1,128,512]{2,1,0:T(8,128)} %get-tuple-element.35), channel_id=1, source_target_pairs={{0,28},{4,24},{8,20},{12,16},{16,12},{20,8},{24,4},{28,0},{1,29},{... | collective-permute-start | bytes 786440 | tf_op jit(solution)/shard_map/ppermute | solution.py:662
  189.1 6.9 %collective-permute-start.14 = (f32[272,8,128]{2,1,0:T(8,128)}, f32[272,8,128]{2,1,0:T(8,128)S(1)}, u32[]{:S(2)}, u32[]{:S(2)}) collective-permute-start(f32[272,8,128]{2,1,0:T(8,128)} %get-tuple-element.37), channel_id=1, source_target_pairs={{0,1},{1,0},{2,3},{3,2},{4,5},{5,4},{6,7},{7,6},{8,9},{9,8},{10,11... | collective-permute-start | bytes 3342344 | tf_op jit(solution)/shard_map/ppermute | solution.py:687
  196.2 16.3 %collective-permute-start.15 = (f32[8,13,8,128]{3,2,1,0:T(8,128)S(1)}, f32[8,13,8,128]{3,2,1,0:T(8,128)}, u32[]{:S(2)}, u32[]{:S(2)}) collective-permute-start(f32[8,13,8,128]{3,2,1,0:T(8,128)S(1)} %slice_add_fusion), channel_id=1, source_target_pairs={{0,2},{1,3},{2,0},{3,1},{4,6},{5,7},{6,4},{7,5},{8,10},{9,11},{10,... | collective-permute-start | bytes 1277960 | tf_op jit(solution)/shard_map/ppermute | solution.py:687
  199.5 22.3 %all-to-all-start.1 = ((f32[2,8,4,8,128]{4,3,2,0,1:T(8,128)}), f32[2,8,4,8,128]{4,3,2,0,1:T(8,128)S(1)}, u32[]{:S(2)}, u32[]{:S(2)}) async-start(f32[2,8,4,8,128]{4,3,2,0,1:T(8,128)} %copy_add_fusion), calls=%async_computation.1 | async-start | bytes 524288 | tf_op jit(solution)/shard_map/all_to_all | solution.py:701
  221.8 15.7 %all-to-all-start = ((f32[8,13,8,128]{3,2,1,0:T(8,128)}), f32[8,13,8,128]{3,2,1,0:T(8,128)S(1)}, u32[]{:S(2)}, u32[]{:S(2)}) async-start(f32[8,13,8,128]{3,2,1,0:T(8,128)} %fusion), calls=%async_computation | async-start | bytes 851968 | tf_op jit(solution)/shard_map/all_to_all | solution.py:636
  225.4 3.8 %collective-permute-start.16 = (f32[4,8,128]{2,1,0:T(8,128)S(1)}, f32[4,8,128]{2,1,0:T(8,128)S(1)}, u32[]{:S(2)}, u32[]{:S(2)}) collective-permute-start(f32[4,8,128]{2,1,0:T(8,128)S(1)} %dynamic-slice_bitcast_fusion.4), channel_id=1, source_target_pairs={{0,2},{1,3},{2,0},{3,1},{4,6},{5,7},{6,4},{7,5},{8,10},{9,11},{10,... | collective-permute-start | bytes 49160 | tf_op jit(solution)/shard_map/ppermute | solution.py:687
  258.1 18.3 %all-to-all-start.3 = ((f32[8,128,128]{2,1,0:T(8,128)}), f32[8,128,128]{2,1,0:T(8,128)S(1)}, u32[]{:S(2)}, u32[]{:S(2)}) async-start(f32[8,128,128]{2,1,0:T(8,128)} %bitcast.10), calls=%async_computation.3 | async-start | bytes 1048576 | tf_op jit(solution)/shard_map/all_to_all | solution.py:636
  (6 other events, 7.1 us)

commit v6 on v5

--- a/solution.py
+++ b/solution.py
@@ -693,7 +693,7 @@
     part, arriving = part.reshape(shape), arriving.reshape(shape)
     bit = space // 2
     pick = lambda value, i: lax.dynamic_index_in_dim(value, i, 0, keepdims=False)
-    cut = 3 * per_device // 4 + 1
+    cut = 3 * per_device // 4 + 2
     given = pick(part, 1 - bit)[:, :cut] + pick(arriving, 1 - bit)[:, :cut]
     kept = pick(part, bit)[:, :cut] + pick(arriving, bit)[:, :cut]
     given = swap(given, 1)

time: 278 us -> 278 us (level)
  no operation moved by 1% of the time
where the time goes in v6:
time: 278 us
  waiting for transfers between devices  115 us (41%)
  starting transfers between devices  78.6 us (28%)
  Pallas kernels  62 us (22%)
  blocking collectives  13.5 us (5%)
  local copies, waits for them, and re-layouts  4.69 us (2%)
  other arithmetic  3.44 us (1%)
    ppermute x14, waiting for transfers between devices, send(): flying[m] = lax.ppermute(part, 'tm', pairs) if m else part  81.2 us
    ppermute x14, starting transfers between devices, send(): flying[m] = lax.ppermute(part, 'tm', pairs) if m else part  56.4 us
    all_to_all x2, waiting for transfers between devices, exchange(): return lax.all_to_all(value, axes, 0, 0, tiled=True)  22.9 us
    pallas_call x5, Pallas kernels, pack(): pl.pallas_call(functools.partial(pack_kernel, offsets), grid=(1,), in_spe...  19.2 us
    all_to_all x1, blocking collectives, exchange(): return lax.all_to_all(value, axes, 0, 0, tiled=True)  13.5 us
    all_to_all x1, starting transfers between devices, body(): rest = lax.all_to_all(rest, 'tm', 1, 1, tiled=True).sum(axis=1)  13.1 us
    pallas_call x1, Pallas kernels, early_gram(): pl.pallas_call(functools.partial(early_gram_kernel, tile, chunks, 1.0 / t...  11.3 us
    pallas_call x1, Pallas kernels, transform(): pl.pallas_call(transform_kernel, grid=(chunks,), in_specs=[pl.BlockSpec(t...  9.49 us
  transfers between devices with their start and end apart: 20, of which 8 were waited for; matrix products, arithmetic and copies ran while one was open for 2% of the time, Pallas kernels for 15%

profile of v6, /device:TPU:0, one launch (start us, length us, event | category | flops | bytes accessed | tf_op | source)
XLA Modules:
  0.0 277.8 jit_solution(5259764538799775870)
XLA Ops:
  0.6 2.9 %pack.5.refs_4_ = f32[3,128,512]{2,1,0:T(8,128)} custom-call(f32[128,32,512]{2,1,0:T(8,128)} %refs_3_.8, f32[1024,128]{1,0:T(8,128)} %constant.70.clone.refs_1_.refs_3_.refs_4_), custom_call_target="tpu_custom_call" | custom-call | tf_op jit(solution)/shard_map/pack/pallas_call | solution.py:111
  3.5 4.0 %collective-permute-start.3 = (f32[3,128,512]{2,1,0:T(8,128)}, f32[3,128,512]{2,1,0:T(8,128)S(1)}, u32[]{:S(2)}, u32[]{:S(2)}) collective-permute-start(f32[3,128,512]{2,1,0:T(8,128)} %pack.5.refs_4_), channel_id=1, source_target_pairs={{0,16},{4,20},{8,24},{12,28},{16,0},{20,4},{24,8},{28,12},{1,17},{... | collective-permute-start | bytes 2359304 | tf_op jit(solution)/shard_map/ppermute | solution.py:662
  7.5 4.7 %pack.6 = (f32[3,128,512]{2,1,0:T(8,128)}, f32[3,128,512]{2,1,0:T(8,128)}, f32[3,128,512]{2,1,0:T(8,128)}) custom-call(f32[128,32,512]{2,1,0:T(8,128)} %refs_3_.8, f32[128,32,512]{2,1,0:T(8,128)} %refs_3_.8, f32[128,32,512]{2,1,0:T(8,128)} %refs_3_.8, f32[1024,128]{1,0:T(8,128)} %constant.70.clone.refs_1_.refs_3_.refs_4_, f32[3,128,512]{2,1,0:T(8,128)} %pack.5.refs_4_), custom_call_target="tpu_custom_call" | custom-call | tf_op jit(solution)/shard_map/pack/pallas_call | solution.py:111
  12.2 5.7 %pack.7 = (f32[3,128,512]{2,1,0:T(8,128)}, f32[3,128,512]{2,1,0:T(8,128)}, f32[3,128,512]{2,1,0:T(8,128)}, f32[3,128,512]{2,1,0:T(8,128)}) custom-call(f32[128,32,512]{2,1,0:T(8,128)} %refs_3_.8, f32[128,32,512]{2,1,0:T(8,128)} %refs_3_.8, f32[128,32,512]{2,1,0:T(8,128)} %refs_3_.8, f32[128,32,512]{2,1,0:T(8,128)} %refs_3_.8, ...), custom_call_target="tpu_custom_call" | custom-call | tf_op jit(solution)/shard_map/pack/pallas_call | solution.py:111
  19.3 1.5 collective-permute-start
  21.1 1.7 collective-permute-start.2
  22.8 37.0 %collective-permute-done.3.refs_10_.refs_5_ = f32[3,128,512]{2,1,0:T(8,128)S(1)} collective-permute-done((f32[3,128,512]{2,1,0:T(8,128)}, f32[3,128,512]{2,1,0:T(8,128)S(1)}, u32[]{:S(2)}, u32[]{:S(2)}) %collective-permute-start.3) | collective-permute-done | bytes 786464 | tf_op jit(solution)/shard_map/ppermute | solution.py:662
  60.8 2.9 %collective-permute-start.6 = (f32[3,128,512]{2,1,0:T(8,128)}, f32[3,128,512]{2,1,0:T(8,128)}, u32[]{:S(2)}, u32[]{:S(2)}) collective-permute-start(f32[3,128,512]{2,1,0:T(8,128)} %get-tuple-element.27), channel_id=1, source_target_pairs={{0,28},{4,24},{8,20},{12,16},{16,12},{20,8},{24,4},{28,0},{1,29},{... | collective-permute-start | bytes 2359304 | tf_op jit(solution)/shard_map/ppermute | solution.py:662
  63.7 2.9 %pack.8 = (f32[1,128,512]{2,1,0:T(8,128)}, f32[1,128,512]{2,1,0:T(8,128)}, f32[1,128,512]{2,1,0:T(8,128)}, f32[1,128,512]{2,1,0:T(8,128)}) custom-call(f32[128,32,512]{2,1,0:T(8,128)} %refs_3_.8, f32[128,32,512]{2,1,0:T(8,128)} %refs_3_.8, f32[128,32,512]{2,1,0:T(8,128)} %refs_3_.8, f32[128,32,512]{2,1,0:T(8,128)} %refs_3_.8, ...), custom_call_target="tpu_custom_call" | custom-call | tf_op jit(solution)/shard_map/pack/pallas_call | solution.py:111
  66.7 3.0 %pack.9 = (f32[1,128,512]{2,1,0:T(8,128)}, f32[1,128,512]{2,1,0:T(8,128)}, f32[1,128,512]{2,1,0:T(8,128)}, f32[1,128,512]{2,1,0:T(8,128)}) custom-call(f32[128,32,512]{2,1,0:T(8,128)} %refs_3_.8, f32[128,32,512]{2,1,0:T(8,128)} %refs_3_.8, f32[128,32,512]{2,1,0:T(8,128)} %refs_3_.8, f32[128,32,512]{2,1,0:T(8,128)} %refs_3_.8, ...), custom_call_target="tpu_custom_call" | custom-call | tf_op jit(solution)/shard_map/pack/pallas_call | solution.py:111
  70.8 3.4 %collective-permute-done.1.refs_8_ = f32[3,128,512]{2,1,0:T(8,128)} collective-permute-done((f32[3,128,512]{2,1,0:T(8,128)}, f32[3,128,512]{2,1,0:T(8,128)}, u32[]{:S(2)}, u32[]{:S(2)}) %collective-permute-start.1) | collective-permute-done | bytes 786464 | tf_op jit(solution)/shard_map/ppermute | solution.py:662
  74.2 13.8 %collective-permute-start.8 = (f32[1,128,512]{2,1,0:T(8,128)}, f32[1,128,512]{2,1,0:T(8,128)S(1)}, u32[]{:S(2)}, u32[]{:S(2)}) collective-permute-start(f32[1,128,512]{2,1,0:T(8,128)} %get-tuple-element.30), channel_id=1, source_target_pairs={{0,8},{4,12},{8,0},{12,4},{16,24},{20,28},{24,16},{28,20},{1,9},{5... | collective-permute-start | bytes 786440 | tf_op jit(solution)/shard_map/ppermute | solution.py:662
  88.0 3.0 %collective-permute-done.2.refs_9_ = f32[3,128,512]{2,1,0:T(8,128)} collective-permute-done((f32[3,128,512]{2,1,0:T(8,128)}, f32[3,128,512]{2,1,0:T(8,128)}, u32[]{:S(2)}, u32[]{:S(2)}) %collective-permute-start.2) | collective-permute-done | bytes 786464 | tf_op jit(solution)/shard_map/ppermute | solution.py:662
  91.0 37.7 %collective-permute-done.4.refs_11_ = f32[3,128,512]{2,1,0:T(8,128)} collective-permute-done((f32[3,128,512]{2,1,0:T(8,128)S(1)}, f32[3,128,512]{2,1,0:T(8,128)}, u32[]{:S(2)}, u32[]{:S(2)}) %collective-permute-start.4) | collective-permute-done | bytes 786464 | tf_op jit(solution)/shard_map/ppermute | solution.py:662
  128.7 24.0 %collective-permute-start.11 = (f32[1,128,512]{2,1,0:T(8,128)}, f32[1,128,512]{2,1,0:T(8,128)S(1)}, u32[]{:S(2)}, u32[]{:S(2)}) collective-permute-start(f32[1,128,512]{2,1,0:T(8,128)} %get-tuple-element.33), channel_id=1, source_target_pairs={{0,20},{4,16},{8,28},{12,24},{16,4},{20,0},{24,12},{28,8},{1,21},{... | collective-permute-start | bytes 786440 | tf_op jit(solution)/shard_map/ppermute | solution.py:662
  153.7 3.8 %collective-permute-start.13 = (f32[1,128,512]{2,1,0:T(8,128)}, f32[1,128,512]{2,1,0:T(8,128)S(1)}, u32[]{:S(2)}, u32[]{:S(2)}) collective-permute-start(f32[1,128,512]{2,1,0:T(8,128)} %get-tuple-element.35), channel_id=1, source_target_pairs={{0,28},{4,24},{8,20},{12,16},{16,12},{20,8},{24,4},{28,0},{1,29},{... | collective-permute-start | bytes 786440 | tf_op jit(solution)/shard_map/ppermute | solution.py:662
  158.4 9.5 %transform.1.z_ref.refs_7_.refs_0_ = f32[3,4352,128]{2,1,0:T(8,128)} custom-call(bf16[512,512]{1,0:T(8,128)(2,1)S(1)} %copy-done, bf16[512,512]{1,0:T(8,128)(2,1)S(1)} %copy-done.1, bf16[256,256]{1,0:T(8,128)(2,1)S(1)} %copy-done.4, bf16[256,256]{1,0:T(8,128)(2,1)S(1)} %copy-done.5, bf16[320,256]{1,0:T(8,128)(2,1)S(1)} %copy-done.2, ...), custom_call_target="tpu_custom_call" | custom-call | tf_op jit(solution)/shard_map/transform/pallas_call | solution.py:188
  167.9 11.3 %early_gram.1.refs_8_.refs_2_ = f32[544,8,128]{2,1,0:T(8,128)} custom-call(f32[3,4352,128]{2,1,0:T(8,128)} %transform.1.z_ref.refs_7_.refs_0_, f32[1,128]{1,0:T(1,128)S(1)} %maximum_bitcast_fusion.w_ref.refs_6_.refs_3_), custom_call_target="tpu_custom_call" | custom-call | tf_op jit(solution)/shard_map/early_gram/pallas_call | solution.py:267
  180.8 8.3 %late_first.1 = (f32[1,4352,128]{2,1,0:T(8,128)}, f32[272,8,128]{2,1,0:T(8,128)}) custom-call(bf16[512,512]{1,0:T(8,128)(2,1)S(1)} %copy-done, bf16[512,512]{1,0:T(8,128)(2,1)S(1)} %copy-done.1, bf16[256,256]{1,0:T(8,128)(2,1)S(1)} %copy-done.4, bf16[256,256]{1,0:T(8,128)(2,1)S(1)} %copy-done.5, bf16[320,256]{1,0:T(8,128)(2,1)S(1)} %copy-done.2, ...), custom_call_target="tpu_custom_call" | custom-call | tf_op jit(solution)/shard_map/late_first/pallas_call | solution.py:358
  189.2 5.5 %late_second.1 = f32[272,8,128]{2,1,0:T(8,128)} custom-call(f32[3,4352,128]{2,1,0:T(8,128)} %transform.1.z_ref.refs_7_.refs_0_, f32[1,4352,128]{2,1,0:T(8,128)} %get-tuple-element.36.refs_1_, f32[544,8,128]{2,1,0:T(8,128)} %early_gram.1.refs_8_.refs_2_, f32[1,128]{1,0:T(1,128)S(1)} %maximum_bitcast_fusion.w_ref.refs_6_.refs_3_), custom_call_target="tpu_custom_call" | custom-call | tf_op jit(solution)/shard_map/late_second/pallas_call | solution.py:414
  197.0 1.5 collective-permute-start.15
  198.5 1.6 copy_add_fusion
  200.1 13.1 %all-to-all-start.1 = ((f32[2,8,3,8,128]{4,3,2,0,1:T(8,128)}), f32[2,8,3,8,128]{4,3,2,0,1:T(8,128)S(1)}, u32[]{:S(2)}, u32[]{:S(2)}) async-start(f32[2,8,3,8,128]{4,3,2,0,1:T(8,128)} %copy_add_fusion), calls=%async_computation.1 | async-start | bytes 393216 | tf_op jit(solution)/shard_map/all_to_all | solution.py:701
  214.0 7.4 %all-to-all-done.1 = f32[2,8,3,8,128]{4,3,2,0,1:T(8,128)S(1)} async-done(((f32[2,8,3,8,128]{4,3,2,0,1:T(8,128)}), f32[2,8,3,8,128]{4,3,2,0,1:T(8,128)S(1)}, u32[]{:S(2)}, u32[]{:S(2)}) %all-to-all-start.1) | async-done | bytes 196640 | tf_op jit(solution)/shard_map/all_to_all | solution.py:701
  221.4 3.5 %all-to-all-start = ((f32[8,14,8,128]{3,2,1,0:T(8,128)}), f32[8,14,8,128]{3,2,1,0:T(8,128)S(1)}, u32[]{:S(2)}, u32[]{:S(2)}) async-start(f32[8,14,8,128]{3,2,1,0:T(8,128)} %fusion), calls=%async_computation | async-start | bytes 917504 | tf_op jit(solution)/shard_map/all_to_all | solution.py:636
  225.6 3.2 %collective-permute-done.16 = f32[3,8,128]{2,1,0:T(8,128)S(1)} collective-permute-done((f32[3,8,128]{2,1,0:T(8,128)S(1)}, f32[3,8,128]{2,1,0:T(8,128)S(1)}, u32[]{:S(2)}, u32[]{:S(2)}) %collective-permute-start.16) | collective-permute-done | bytes 12320 | tf_op jit(solution)/shard_map/ppermute | solution.py:687
  228.7 8.7 %all-to-all-done = f32[8,14,8,128]{3,2,1,0:T(8,128)S(1)} async-done(((f32[8,14,8,128]{3,2,1,0:T(8,128)}), f32[8,14,8,128]{3,2,1,0:T(8,128)S(1)}, u32[]{:S(2)}, u32[]{:S(2)}) %all-to-all-start) | async-done | bytes 458784 | tf_op jit(solution)/shard_map/all_to_all | solution.py:636
  237.8 1.4 power.1
  239.2 13.5 %all_to_all.20.refs_2_ = f32[32,16,128]{2,1,0:T(8,128)S(1)} all-to-all(f32[32,16,128]{2,1,0:T(8,128)S(1)} %broadcast_in_dim.10), channel_id=1, replica_groups=mesh['tm'=8,'space'=4] {'tm','space'}, dimensions={0} | all-to-all | bytes 524288 | tf_op jit(solution)/shard_map/all_to_all | solution.py:636
  252.7 5.8 %modes.1 = (f32[1024,128]{1,0:T(8,128)}, f32[1024,128]{1,0:T(8,128)S(1)}) custom-call(f32[3,4352,128]{2,1,0:T(8,128)} %transform.1.z_ref.refs_7_.refs_0_, f32[1,4352,128]{2,1,0:T(8,128)} %get-tuple-element.36.refs_1_, f32[32,16,128]{2,1,0:T(8,128)S(1)} %all_to_all.20.refs_2_), custom_call_target="tpu_custom_call" | custom-call | tf_op jit(solution)/shard_map/modes/pallas_call | solution.py:596
  258.5 3.5 %all-to-all-start.3 = ((f32[8,128,128]{2,1,0:T(8,128)}), f32[8,128,128]{2,1,0:T(8,128)S(1)}, u32[]{:S(2)}, u32[]{:S(2)}) async-start(f32[8,128,128]{2,1,0:T(8,128)} %bitcast.10), calls=%async_computation.3 | async-start | bytes 1048576 | tf_op jit(solution)/shard_map/all_to_all | solution.py:636
  262.6 14.2 %all-to-all-done.3.x_ref = f32[8,128,128]{2,1,0:T(8,128)S(1)} async-done(((f32[8,128,128]{2,1,0:T(8,128)}), f32[8,128,128]{2,1,0:T(8,128)S(1)}, u32[]{:S(2)}, u32[]{:S(2)}) %all-to-all-start.3) | async-done | bytes 524320 | tf_op jit(solution)/shard_map/all_to_all | solution.py:636
  (73 shorter events, 12.9 us)
Async XLA Ops:
  3.5 56.4 %collective-permute-start.3 = (f32[3,128,512]{2,1,0:T(8,128)}, f32[3,128,512]{2,1,0:T(8,128)S(1)}, u32[]{:S(2)}, u32[]{:S(2)}) collective-permute-start(f32[3,128,512]{2,1,0:T(8,128)} %pack.5.refs_4_), channel_id=1, source_target_pairs={{0,16},{4,20},{8,24},{12,28},{16,0},{20,4},{24,8},{28,12},{1,17},{... | collective-permute-start | bytes 2359304 | tf_op jit(solution)/shard_map/ppermute | solution.py:662
  12.2 7.1 %copy-start.16 = (f32[3,128,512]{2,1,0:T(8,128)S(1)}, f32[3,128,512]{2,1,0:T(8,128)}, u32[]{:S(2)}) copy-start(f32[3,128,512]{2,1,0:T(8,128)} %get-tuple-element.22) | copy-start | bytes 2359300
  12.2 47.6 %copy-start.15 = (f32[3,128,512]{2,1,0:T(8,128)S(1)}, f32[3,128,512]{2,1,0:T(8,128)}, u32[]{:S(2)}) copy-start(f32[3,128,512]{2,1,0:T(8,128)} %get-tuple-element.25) | copy-start | bytes 2359300
  18.0 42.9 %collective-permute-start.5 = (f32[3,128,512]{2,1,0:T(8,128)}, f32[3,128,512]{2,1,0:T(8,128)S(1)}, u32[]{:S(2)}, u32[]{:S(2)}) collective-permute-start(f32[3,128,512]{2,1,0:T(8,128)} %get-tuple-element.26), channel_id=1, source_target_pairs={{0,24},{4,28},{8,16},{12,20},{16,8},{20,12},{24,0},{28,4},{1,25},{... | collective-permute-start | bytes 2359304 | tf_op jit(solution)/shard_map/ppermute | solution.py:662
  19.3 50.4 %collective-permute-start = (f32[3,128,512]{2,1,0:T(8,128)S(1)}, f32[3,128,512]{2,1,0:T(8,128)}, u32[]{:S(2)}, u32[]{:S(2)}) collective-permute-start(f32[3,128,512]{2,1,0:T(8,128)S(1)} %copy-done.16), channel_id=1, source_target_pairs={{0,4},{4,0},{8,12},{12,8},{16,20},{20,16},{24,28},{28,24},{1,5},{5... | collective-permute-start | bytes 2359304 | tf_op jit(solution)/shard_map/ppermute | solution.py:662
  20.8 53.3 %collective-permute-start.1 = (f32[3,128,512]{2,1,0:T(8,128)}, f32[3,128,512]{2,1,0:T(8,128)}, u32[]{:S(2)}, u32[]{:S(2)}) collective-permute-start(f32[3,128,512]{2,1,0:T(8,128)} %get-tuple-element.23), channel_id=1, source_target_pairs={{0,8},{4,12},{8,0},{12,4},{16,24},{20,28},{24,16},{28,20},{1,9},{5... | collective-permute-start | bytes 2359304 | tf_op jit(solution)/shard_map/ppermute | solution.py:662
  21.1 69.9 %collective-permute-start.2 = (f32[3,128,512]{2,1,0:T(8,128)}, f32[3,128,512]{2,1,0:T(8,128)}, u32[]{:S(2)}, u32[]{:S(2)}) collective-permute-start(f32[3,128,512]{2,1,0:T(8,128)} %get-tuple-element.24), channel_id=1, source_target_pairs={{0,12},{4,8},{8,4},{12,0},{16,28},{20,24},{24,20},{28,16},{1,13},{... | collective-permute-start | bytes 2359304 | tf_op jit(solution)/shard_map/ppermute | solution.py:662
  59.9 3.9 %copy-start.6 = (f32[3,128,512]{2,1,0:T(8,128)}, f32[3,128,512]{2,1,0:T(8,128)S(1)}, u32[]{:S(2)}) copy-start(f32[3,128,512]{2,1,0:T(8,128)S(1)} %collective-permute-done.3.refs_10_.refs_5_) | copy-start | bytes 2359300
  59.9 68.9 %collective-permute-start.4 = (f32[3,128,512]{2,1,0:T(8,128)S(1)}, f32[3,128,512]{2,1,0:T(8,128)}, u32[]{:S(2)}, u32[]{:S(2)}) collective-permute-start(f32[3,128,512]{2,1,0:T(8,128)S(1)} %copy-done.15), channel_id=1, source_target_pairs={{0,20},{4,16},{8,28},{12,24},{16,4},{20,0},{24,12},{28,8},{1,21},{... | collective-permute-start | bytes 2359304 | tf_op jit(solution)/shard_map/ppermute | solution.py:662
  60.8 5.8 %copy-start.7 = (f32[3,128,512]{2,1,0:T(8,128)}, f32[3,128,512]{2,1,0:T(8,128)S(1)}, u32[]{:S(2)}) copy-start(f32[3,128,512]{2,1,0:T(8,128)S(1)} %collective-permute-done.5.refs_12_.refs_6_) | copy-start | bytes 2359300
  60.8 67.9 %collective-permute-start.6 = (f32[3,128,512]{2,1,0:T(8,128)}, f32[3,128,512]{2,1,0:T(8,128)}, u32[]{:S(2)}, u32[]{:S(2)}) collective-permute-start(f32[3,128,512]{2,1,0:T(8,128)} %get-tuple-element.27), channel_id=1, source_target_pairs={{0,28},{4,24},{8,20},{12,16},{16,12},{20,8},{24,4},{28,0},{1,29},{... | collective-permute-start | bytes 2359304 | tf_op jit(solution)/shard_map/ppermute | solution.py:662
  66.6 91.7 %copy-start = (bf16[512,512]{1,0:T(8,128)(2,1)S(1)}, bf16[512,512]{1,0:T(8,128)(2,1)}, u32[]{:S(2)}) copy-start(bf16[512,512]{1,0:T(8,128)(2,1)} %constant.71.clone.refs_0_) | copy-start | bytes 1572868
  66.6 91.7 %copy-start.1 = (bf16[512,512]{1,0:T(8,128)(2,1)S(1)}, bf16[512,512]{1,0:T(8,128)(2,1)}, u32[]{:S(2)}) copy-start(bf16[512,512]{1,0:T(8,128)(2,1)} %constant.72.clone.refs_1_) | copy-start | bytes 1572868
  66.6 91.7 %copy-start.2 = (bf16[320,256]{1,0:T(8,128)(2,1)S(1)}, bf16[320,256]{1,0:T(8,128)(2,1)}, u32[]{:S(2)}) copy-start(bf16[320,256]{1,0:T(8,128)(2,1)} %constant.75.clone.refs_4_) | copy-start | bytes 491524
  66.7 91.7 %copy-start.3 = (bf16[320,256]{1,0:T(8,128)(2,1)S(1)}, bf16[320,256]{1,0:T(8,128)(2,1)}, u32[]{:S(2)}) copy-start(bf16[320,256]{1,0:T(8,128)(2,1)} %constant.76.clone.refs_5_) | copy-start | bytes 491524
  66.7 91.7 %copy-start.4 = (bf16[256,256]{1,0:T(8,128)(2,1)S(1)}, bf16[256,256]{1,0:T(8,128)(2,1)}, u32[]{:S(2)}) copy-start(bf16[256,256]{1,0:T(8,128)(2,1)} %constant.73.clone.refs_2_) | copy-start | bytes 393220
  66.7 91.7 %copy-start.5 = (bf16[256,256]{1,0:T(8,128)(2,1)S(1)}, bf16[256,256]{1,0:T(8,128)(2,1)}, u32[]{:S(2)}) copy-start(bf16[256,256]{1,0:T(8,128)(2,1)} %constant.74.clone.refs_3_) | copy-start | bytes 393220
  69.7 83.0 %collective-permute-start.7 = (f32[1,128,512]{2,1,0:T(8,128)S(1)}, f32[1,128,512]{2,1,0:T(8,128)S(1)}, u32[]{:S(2)}, u32[]{:S(2)}) collective-permute-start(f32[1,128,512]{2,1,0:T(8,128)S(1)} %copy-done.17), channel_id=1, source_target_pairs={{0,4},{4,0},{8,12},{12,8},{16,20},{20,16},{24,28},{28,24},{1,5},{5... | collective-permute-start | bytes 786440 | tf_op jit(solution)/shard_map/ppermute | solution.py:662
  74.2 79.5 %collective-permute-start.8 = (f32[1,128,512]{2,1,0:T(8,128)}, f32[1,128,512]{2,1,0:T(8,128)S(1)}, u32[]{:S(2)}, u32[]{:S(2)}) collective-permute-start(f32[1,128,512]{2,1,0:T(8,128)} %get-tuple-element.30), channel_id=1, source_target_pairs={{0,8},{4,12},{8,0},{12,4},{16,24},{20,28},{24,16},{28,20},{1,9},{5... | collective-permute-start | bytes 786440 | tf_op jit(solution)/shard_map/ppermute | solution.py:662
  91.0 88.1 %collective-permute-start.9 = (f32[1,128,512]{2,1,0:T(8,128)}, f32[1,128,512]{2,1,0:T(8,128)S(1)}, u32[]{:S(2)}, u32[]{:S(2)}) collective-permute-start(f32[1,128,512]{2,1,0:T(8,128)} %get-tuple-element.31), channel_id=1, source_target_pairs={{0,12},{4,8},{8,4},{12,0},{16,28},{20,24},{24,20},{28,16},{1,13},{... | collective-permute-start | bytes 786440 | tf_op jit(solution)/shard_map/ppermute | solution.py:662
  128.7 50.4 %collective-permute-start.10 = (f32[1,128,512]{2,1,0:T(8,128)}, f32[1,128,512]{2,1,0:T(8,128)S(1)}, u32[]{:S(2)}, u32[]{:S(2)}) collective-permute-start(f32[1,128,512]{2,1,0:T(8,128)} %get-tuple-element.32), channel_id=1, source_target_pairs={{0,16},{4,20},{8,24},{12,28},{16,0},{20,4},{24,8},{28,12},{1,17},{... | collective-permute-start | bytes 786440 | tf_op jit(solution)/shard_map/ppermute | solution.py:662
  128.7 50.5 %collective-permute-start.11 = (f32[1,128,512]{2,1,0:T(8,128)}, f32[1,128,512]{2,1,0:T(8,128)S(1)}, u32[]{:S(2)}, u32[]{:S(2)}) collective-permute-start(f32[1,128,512]{2,1,0:T(8,128)} %get-tuple-element.33), channel_id=1, source_target_pairs={{0,20},{4,16},{8,28},{12,24},{16,4},{20,0},{24,12},{28,8},{1,21},{... | collective-permute-start | bytes 786440 | tf_op jit(solution)/shard_map/ppermute | solution.py:662
  152.7 15.1 %copy-start.8 = (f32[1,128,512]{2,1,0:T(8,128)}, f32[1,128,512]{2,1,0:T(8,128)S(1)}, u32[]{:S(2)}) copy-start(f32[1,128,512]{2,1,0:T(8,128)S(1)} %collective-permute-done.7.refs_10_) | copy-start | bytes 786436
  152.7 26.5 %collective-permute-start.12 = (f32[1,128,512]{2,1,0:T(8,128)}, f32[1,128,512]{2,1,0:T(8,128)S(1)}, u32[]{:S(2)}, u32[]{:S(2)}) collective-permute-start(f32[1,128,512]{2,1,0:T(8,128)} %get-tuple-element.34), channel_id=1, source_target_pairs={{0,24},{4,28},{8,16},{12,20},{16,8},{20,12},{24,0},{28,4},{1,25},{... | collective-permute-start | bytes 786440 | tf_op jit(solution)/shard_map/ppermute | solution.py:662
  153.7 14.1 %copy-start.9 = (f32[1,128,512]{2,1,0:T(8,128)}, f32[1,128,512]{2,1,0:T(8,128)S(1)}, u32[]{:S(2)}) copy-start(f32[1,128,512]{2,1,0:T(8,128)S(1)} %collective-permute-done.8.refs_11_) | copy-start | bytes 786436
  153.7 25.5 %collective-permute-start.13 = (f32[1,128,512]{2,1,0:T(8,128)}, f32[1,128,512]{2,1,0:T(8,128)S(1)}, u32[]{:S(2)}, u32[]{:S(2)}) collective-permute-start(f32[1,128,512]{2,1,0:T(8,128)} %get-tuple-element.35), channel_id=1, source_target_pairs={{0,28},{4,24},{8,20},{12,16},{16,12},{20,8},{24,4},{28,0},{1,29},{... | collective-permute-start | bytes 786440 | tf_op jit(solution)/shard_map/ppermute | solution.py:662
  189.1 6.9 %collective-permute-start.14 = (f32[272,8,128]{2,1,0:T(8,128)}, f32[272,8,128]{2,1,0:T(8,128)S(1)}, u32[]{:S(2)}, u32[]{:S(2)}) collective-permute-start(f32[272,8,128]{2,1,0:T(8,128)} %get-tuple-element.37), channel_id=1, source_target_pairs={{0,1},{1,0},{2,3},{3,2},{4,5},{5,4},{6,7},{7,6},{8,9},{9,8},{10,11... | collective-permute-start | bytes 3342344 | tf_op jit(solution)/shard_map/ppermute | solution.py:687
  197.0 16.2 %collective-permute-start.15 = (f32[8,14,8,128]{3,2,1,0:T(8,128)}, f32[8,14,8,128]{3,2,1,0:T(8,128)S(1)}, u32[]{:S(2)}, u32[]{:S(2)}) collective-permute-start(f32[8,14,8,128]{3,2,1,0:T(8,128)} %slice_add_fusion), channel_id=1, source_target_pairs={{0,2},{1,3},{2,0},{3,1},{4,6},{5,7},{6,4},{7,5},{8,10},{9,11},{10,... | collective-permute-start | bytes 1376264 | tf_op jit(solution)/shard_map/ppermute | solution.py:687
  200.1 21.4 %all-to-all-start.1 = ((f32[2,8,3,8,128]{4,3,2,0,1:T(8,128)}), f32[2,8,3,8,128]{4,3,2,0,1:T(8,128)S(1)}, u32[]{:S(2)}, u32[]{:S(2)}) async-start(f32[2,8,3,8,128]{4,3,2,0,1:T(8,128)} %copy_add_fusion), calls=%async_computation.1 | async-start | bytes 393216 | tf_op jit(solution)/shard_map/all_to_all | solution.py:701
  221.4 16.0 %all-to-all-start = ((f32[8,14,8,128]{3,2,1,0:T(8,128)}), f32[8,14,8,128]{3,2,1,0:T(8,128)S(1)}, u32[]{:S(2)}, u32[]{:S(2)}) async-start(f32[8,14,8,128]{3,2,1,0:T(8,128)} %fusion), calls=%async_computation | async-start | bytes 917504 | tf_op jit(solution)/shard_map/all_to_all | solution.py:636
  225.0 3.8 %collective-permute-start.16 = (f32[3,8,128]{2,1,0:T(8,128)S(1)}, f32[3,8,128]{2,1,0:T(8,128)S(1)}, u32[]{:S(2)}, u32[]{:S(2)}) collective-permute-start(f32[3,8,128]{2,1,0:T(8,128)S(1)} %dynamic-slice_bitcast_fusion.4), channel_id=1, source_target_pairs={{0,2},{1,3},{2,0},{3,1},{4,6},{5,7},{6,4},{7,5},{8,10},{9,11},{10,... | collective-permute-start | bytes 36872 | tf_op jit(solution)/shard_map/ppermute | solution.py:687
  258.5 18.3 %all-to-all-start.3 = ((f32[8,128,128]{2,1,0:T(8,128)}), f32[8,128,128]{2,1,0:T(8,128)S(1)}, u32[]{:S(2)}, u32[]{:S(2)}) async-start(f32[8,128,128]{2,1,0:T(8,128)} %bitcast.10), calls=%async_computation.3 | async-start | bytes 1048576 | tf_op jit(solution)/shard_map/all_to_all | solution.py:636
  (6 other events, 7.1 us)
